TPU v7x, 512 devices: a whole 4x4x16 slice. The times are simulated.
512 devices in a mesh: grp: 4 (over y), seq: 32 (over z_lo, x), dp: 4 (over z_hi, core).
Axes of the slice: x: 4, y: 4, z: 16 (z_hi: 2, z_lo: 8; z = z_hi * 8 + z_lo), core: 2. Of those that a mesh axis runs over, the one named last changes fastest.
Arguments:
- img_qkv: bfloat16 [32, 16, 3, 1536, 128], P(('grp', 'dp'), None, None, 'seq'), may hold values from -6 to 6
- txt_qkv: bfloat16 [32, 16, 3, 512, 128], P(('grp', 'dp'), None, None, 'seq'), may hold values from -6 to 6
- img_cot: bfloat16 [32, 16, 1536, 128], P(('grp', 'dp'), None, 'seq'), may hold values from -6 to 6
- txt_cot: bfloat16 [32, 16, 512, 128], P(('grp', 'dp'), None, 'seq'), may hold values from -6 to 6
- lengths: int32 [32], P(('grp', 'dp')), may hold values from 1 to 512
- norm_gains: float32 [4, 128], replicated, may hold values from 0.25 to 1.75
Outputs:
- img_out: bfloat16 [32, 16, 1536, 128], P(('grp', 'dp'), None, 'seq')
- txt_out: bfloat16 [32, 16, 512, 128], P(('grp', 'dp'), None, 'seq')
- img_grad: bfloat16 [32, 16, 3, 1536, 128], P(('grp', 'dp'), None, None, 'seq')
- txt_grad: bfloat16 [32, 16, 3, 512, 128], P(('grp', 'dp'), None, None, 'seq')
- gain_grad: float32 [4, 128], replicated
All inputs are finite; a program needn't handle non-finite values.
Results may differ from a plain program's by a relative error of at most 0.011.
Values may be sent and summed in bfloat16 or wider, within the bound.
No kernel may reach another device: no remote copies, remote signals or barrier semaphores. Data moves between devices by JAX's collectives and lax.ppermute only.
A program may use at most 64 MiB of HBM per device.

v0:
```python
import math

import jax
import jax.numpy as jnp
from jax import lax
from jax.sharding import PartitionSpec as P


def rms_forward(raw_rows, gain_rows):
    values = raw_rows.astype(jnp.float32)
    inverse = lax.rsqrt(jnp.mean(values * values, axis=-1, keepdims=True) + 1e-06)
    return (values * inverse * gain_rows).astype(jnp.bfloat16)


def rms_backward(raw_rows, gain_rows, upstream):
    values = raw_rows.astype(jnp.float32)
    inverse = lax.rsqrt(jnp.mean(values * values, axis=-1, keepdims=True) + 1e-06)
    scaled = gain_rows * upstream
    inner = jnp.mean(scaled * values, axis=-1, keepdims=True)
    grad_rows = inverse * scaled - values * inverse * inverse * inverse * inner
    return (grad_rows, upstream * values * inverse)


def role_gain(is_text, norm_gains, which):
    return jnp.where(is_text[:, None], norm_gains[which + 2], norm_gains[which])


def gain_terms(terms_query, terms_key, is_text):
    text_float = is_text.astype(jnp.float32)[:, None]
    image_float = 1.0 - text_float
    return jnp.stack(
        [
            jnp.sum(terms_query * image_float, axis=(0, 1)),
            jnp.sum(terms_key * image_float, axis=(0, 1)),
            jnp.sum(terms_query * text_float, axis=(0, 1)),
            jnp.sum(terms_key * text_float, axis=(0, 1)),
        ],
        axis=0,
    )


def attend_blocks(query_normed, key_normed, values, cotangent, key_live):
    seq_len, head_size = query_normed.shape
    block = math.gcd(512, seq_len)
    scale = 1.0 / math.sqrt(head_size)

    def step(carry, start):
        grad_kn, grad_value = carry
        query_block = lax.dynamic_slice_in_dim(query_normed, start, block, 0)
        cot_block = lax.dynamic_slice_in_dim(cotangent, start, block, 0)
        scores = (
            jnp.einsum("qd,kd->qk", query_block, key_normed, preferred_element_type=jnp.float32)
            * scale
        )
        scores = jnp.where(key_live[None, :], scores, -jnp.inf)
        top_score = jnp.max(scores, axis=-1, keepdims=True)
        expo = jnp.exp(scores - top_score)
        probs = expo / jnp.sum(expo, axis=-1, keepdims=True)
        probs_b = probs.astype(jnp.bfloat16)
        attended = jnp.dot(probs_b, values, preferred_element_type=jnp.float32)
        dprobs = jnp.einsum("qd,kd->qk", cot_block, values, preferred_element_type=jnp.float32)
        delta = jnp.sum(probs * dprobs, axis=-1, keepdims=True)
        dscores = (probs * (dprobs - delta) * scale).astype(jnp.bfloat16)
        grad_qn = jnp.dot(dscores, key_normed, preferred_element_type=jnp.float32)
        grad_kn = grad_kn + jnp.einsum(
            "qk,qd->kd", dscores, query_block, preferred_element_type=jnp.float32
        )
        grad_value = grad_value + jnp.einsum(
            "qk,qd->kd", probs_b, cot_block, preferred_element_type=jnp.float32
        )
        return ((grad_kn, grad_value), (attended.astype(jnp.bfloat16), grad_qn))

    zeros_init = jnp.zeros((seq_len, head_size), jnp.float32)
    starts = jnp.arange(seq_len // block, dtype=jnp.int32) * block
    (grad_kn, grad_value), (attended, grad_qn) = lax.scan(step, (zeros_init, zeros_init), starts)
    return (
        attended.reshape(seq_len, head_size),
        grad_qn.reshape(seq_len, head_size),
        grad_kn,
        grad_value.astype(jnp.bfloat16),
    )


def per_device(img_qkv, txt_qkv, img_cot, txt_cot, lengths, norm_gains):
    samples_here, head_count, _, img_rows, head_size = img_qkv.shape
    txt_rows = txt_qkv.shape[3]
    row_count = img_rows + txt_rows
    pair_count = samples_here * head_count
    seq_devices = lax.axis_size("seq")
    pair_dev = pair_count // seq_devices
    full_len = row_count * seq_devices
    joint_qkv = jnp.concatenate(
        [
            img_qkv.reshape(pair_count, 3, img_rows, head_size),
            txt_qkv.reshape(pair_count, 3, txt_rows, head_size),
        ],
        axis=2,
    )
    joint_cot = jnp.concatenate(
        [
            img_cot.reshape(pair_count, 1, img_rows, head_size),
            txt_cot.reshape(pair_count, 1, txt_rows, head_size),
        ],
        axis=2,
    )
    local_text = jnp.arange(row_count) >= img_rows
    local_gq = role_gain(local_text, norm_gains, 0)
    local_gk = role_gain(local_text, norm_gains, 1)
    outgoing = jnp.stack(
        [
            rms_forward(joint_qkv[:, 0], local_gq),
            rms_forward(joint_qkv[:, 1], local_gk),
            joint_qkv[:, 2],
        ],
        axis=1,
    )
    arrived, arrived_cot = (
        lax.all_to_all(outgoing, "seq", split_axis=0, concat_axis=2, tiled=True),
        lax.all_to_all(joint_cot, "seq", split_axis=0, concat_axis=2, tiled=True),
    )
    position = jnp.arange(full_len)
    within = position % row_count
    far_text = within >= img_rows
    text_index = position // row_count * txt_rows + within - img_rows
    first_pair = lax.axis_index("seq") * pair_dev
    sample_of = (first_pair + jnp.arange(pair_dev)) // head_count
    pair_length = jnp.sum(
        jnp.where(sample_of[:, None] == jnp.arange(samples_here)[None, :], lengths[None, :], 0),
        axis=1,
    )
    key_live = jnp.logical_or(
        jnp.logical_not(far_text)[None, :], text_index[None, :] < pair_length[:, None]
    )
    query_normed = arrived[:, 0]
    key_normed = arrived[:, 1]

    def one_pair(inputs):
        return attend_blocks(inputs[0], inputs[1], inputs[2], inputs[3], inputs[4])

    attended, grad_qn, grad_kn, grad_value = lax.map(
        one_pair, (query_normed, key_normed, arrived[:, 2], arrived_cot[:, 0], key_live)
    )
    back_out, back_value = (
        lax.all_to_all(attended[:, None], "seq", split_axis=2, concat_axis=0, tiled=True),
        lax.all_to_all(grad_value[:, None], "seq", split_axis=2, concat_axis=0, tiled=True),
    )
    back_norm = lax.all_to_all(
        jnp.stack([grad_qn, grad_kn], axis=1), "seq", split_axis=2, concat_axis=0, tiled=True
    )
    grad_query, terms_query = rms_backward(joint_qkv[:, 0], local_gq, back_norm[:, 0])
    grad_key, terms_key = rms_backward(joint_qkv[:, 1], local_gk, back_norm[:, 1])
    back_grads = jnp.stack(
        [grad_query.astype(jnp.bfloat16), grad_key.astype(jnp.bfloat16), back_value[:, 0]], axis=1
    )
    partial_terms = gain_terms(terms_query, terms_key, local_text)
    gain_grad = lax.psum(partial_terms, ("grp", "seq", "dp"))
    img_out = back_out[:, 0, :img_rows].reshape(samples_here, head_count, img_rows, head_size)
    txt_out = back_out[:, 0, img_rows:].reshape(samples_here, head_count, txt_rows, head_size)
    img_grad = back_grads[:, :, :img_rows].reshape(samples_here, head_count, 3, img_rows, head_size)
    txt_grad = back_grads[:, :, img_rows:].reshape(samples_here, head_count, 3, txt_rows, head_size)
    return (img_out, txt_out, img_grad, txt_grad, gain_grad)


def solution(mesh):
    placed = (
        P(("grp", "dp"), None, None, "seq", None),
        P(("grp", "dp"), None, None, "seq", None),
        P(("grp", "dp"), None, "seq", None),
        P(("grp", "dp"), None, "seq", None),
        P(("grp", "dp")),
        P(),
    )
    return jax.shard_map(
        per_device,
        mesh=mesh,
        in_specs=placed,
        out_specs=(
            P(("grp", "dp"), None, "seq", None),
            P(("grp", "dp"), None, "seq", None),
            P(("grp", "dp"), None, None, "seq", None),
            P(("grp", "dp"), None, None, "seq", None),
            P(),
        ),
        check_vma=False,
    )
```

profile of v0, /device:TPU:24, one launch (start us, length us, event | category | flops | bytes accessed | tf_op | source)
XLA Modules:
  0.0 504.5 jit_solution(9161706309382950314)
XLA Ops:
  0.7 0.8 slice_bitcast_fusion.6
  1.5 1.3 copy.40
  5.2 1.3 copy.42
  6.5 15.5 %all-to-all-start = ((bf16[32,3,64,128]{3,2,1,0:T(8,128)(2,1)}), bf16[32,3,64,128]{3,2,1,0:T(8,128)(2,1)S(1)}, u32[]{:S(2)}, u32[]{:S(2)}) async-start(bf16[32,3,64,128]{3,2,1,0:T(8,128)(2,1)} %copy.42), calls=%async_computation | async-start | bytes 3145728 | tf_op jit(solution)/shard_map/all_to_all | solution.py:118
  22.0 0.9 pad_maximum_fusion.2
  22.9 72.5 %all-to-all-done = bf16[32,3,64,128]{3,2,1,0:T(8,128)(2,1)S(1)} async-done(((bf16[32,3,64,128]{3,2,1,0:T(8,128)(2,1)}), bf16[32,3,64,128]{3,2,1,0:T(8,128)(2,1)S(1)}, u32[]{:S(2)}, u32[]{:S(2)}) %all-to-all-start) | async-done | bytes 1572896 | tf_op jit(solution)/shard_map/all_to_all | solution.py:118
  95.4 7.6 %all-to-all-start.1 = ((bf16[32,1,64,128]{3,2,1,0:T(8,128)(2,1)}), bf16[32,1,64,128]{3,2,1,0:T(8,128)(2,1)S(1)}, u32[]{:S(2)}, u32[]{:S(2)}) async-start(bf16[32,1,64,128]{3,2,1,0:T(8,128)(2,1)} %pad_maximum_fusion.2), calls=%async_computation.1 | async-start | bytes 1048576 | tf_op jit(solution)/shard_map/all_to_all | solution.py:119
  103.9 27.9 %all-to-all-done.1 = bf16[32,1,64,128]{3,2,1,0:T(8,128)(2,1)S(1)} async-done(((bf16[32,1,64,128]{3,2,1,0:T(8,128)(2,1)}), bf16[32,1,64,128]{3,2,1,0:T(8,128)(2,1)S(1)}, u32[]{:S(2)}, u32[]{:S(2)}) %all-to-all-start.1) | async-done | bytes 524320 | tf_op jit(solution)/shard_map/all_to_all | solution.py:119
  131.8 71.4 %while.30 = (s32[]{:T(128)}, f32[2048,128]{1,0:T(8,128)}, f32[2048,128]{1,0:T(8,128)}, bf16[4,512,128]{2,1,0:T(8,128)(2,1)}, f32[4,512,128]{2,1,0:T(8,128)}, /*i...) while((s32[]{:T(128)}, f32[2048,128]{1,0:T(8,128)}, ...), condition=%wide.region_7.8_spmd.clone, body=%wide.region_3.7_spmd.clone.sunk | while | flops 1631687168 | bytes 93216128 | solution.py:75
  135.1 0.8 fusion.101
  135.9 0.9 fusion.102
  136.9 1.5 multiply_reduce_fusion.6
  138.3 1.9 copy-done
  140.8 2.8 convolution_add_fusion.4
  143.6 1.4 fusion.104
  145.0 2.7 convolution_add_fusion.5
  147.7 1.4 fusion.103
  152.3 0.8 fusion.101
  153.2 0.9 fusion.102
  154.1 1.5 multiply_reduce_fusion.6
  155.6 1.9 copy-done
  158.1 3.2 convolution_add_fusion.4
  161.2 1.4 fusion.104
  162.7 3.1 convolution_add_fusion.5
  165.7 1.4 fusion.103
  170.4 0.8 fusion.101
  171.2 0.9 fusion.102
  172.2 1.5 multiply_reduce_fusion.6
  173.6 1.9 copy-done
  176.1 3.2 convolution_add_fusion.4
  179.3 1.4 fusion.104
  180.7 3.1 convolution_add_fusion.5
  183.8 1.4 fusion.103
  188.4 0.8 fusion.101
  189.3 0.9 fusion.102
  190.2 1.5 multiply_reduce_fusion.6
  191.7 1.9 copy-done
  194.2 3.2 convolution_add_fusion.4
  197.3 1.4 fusion.104
  198.8 3.1 convolution_add_fusion.5
  201.8 1.4 fusion.103
  203.2 1.3 convert_bitcast_fusion.2
  204.5 8.1 %copy.53 = bf16[1,1,2048,128]{3,1,0,2:T(2,128)(2,1)S(1)} copy(bf16[1,1,2048,128]{3,2,1,0:T(8,128)(2,1)S(1)} %convert_bitcast_fusion.2) | data formatting | bytes 1048576 | tf_op jit(solution)/shard_map/broadcast_in_dim | solution.py:145
  213.1 11.7 %reduce.3 = bf16[2048,128]{1,0:T(8,128)(2,1)S(1)} reduce(bf16[2048,1,1,128]{3,2,1,0:T(2,128)(2,1)S(1)} %bitcast.152, bf16[]{:T(256)} %broadcast.268), dimensions={1,2}, to_apply=%bitcast.121.reduce_sub_computation | reduce | bytes 1048578
  224.9 0.9 reshape.216
  225.8 6.1 %all-to-all-start.4 = ((bf16[32,2,4096]{2,1,0:T(2,128)(2,1)}), bf16[32,2,4096]{2,1,0:T(2,128)(2,1)S(1)}, u32[]{:S(2)}, u32[]{:S(2)}) async-start(bf16[32,2,4096]{2,1,0:T(2,128)(2,1)} %reshape.216), calls=%async_computation.4 | async-start | bytes 1048576 | tf_op jit(solution)/shard_map/all_to_all | solution.py:145
  231.9 8.1 %copy.54 = bf16[1,1,2048,128]{3,1,0,2:T(2,128)(2,1)S(1)} copy(bf16[1,1,2048,128]{3,2,1,0:T(8,128)(2,1)S(1)} %bitcast.161) | data formatting | bytes 1048576 | tf_op jit(solution)/shard_map/broadcast_in_dim | solution.py:144
  240.1 11.6 %reduce.2 = bf16[2048,128]{1,0:T(8,128)(2,1)S(1)} reduce(bf16[2048,1,1,128]{3,2,1,0:T(2,128)(2,1)S(1)} %bitcast.153, bf16[]{:T(256)} %broadcast.268), dimensions={1,2}, to_apply=%bitcast.122.reduce_sub_computation | reduce | bytes 1048578
  251.7 0.9 reshape.214
  252.6 8.7 %all-to-all-done.4 = bf16[32,2,4096]{2,1,0:T(2,128)(2,1)S(1)} async-done(((bf16[32,2,4096]{2,1,0:T(2,128)(2,1)}), bf16[32,2,4096]{2,1,0:T(2,128)(2,1)S(1)}, u32[]{:S(2)}, u32[]{:S(2)}) %all-to-all-start.4) | async-done | bytes 524320 | tf_op jit(solution)/shard_map/all_to_all | solution.py:145
  261.3 6.1 %all-to-all-start.2 = ((bf16[32,2,4096]{2,1,0:T(2,128)(2,1)}), bf16[32,2,4096]{2,1,0:T(2,128)(2,1)S(1)}, u32[]{:S(2)}, u32[]{:S(2)}) async-start(bf16[32,2,4096]{2,1,0:T(2,128)(2,1)} %reshape.214), calls=%async_computation.2 | async-start | bytes 1048576 | tf_op jit(solution)/shard_map/all_to_all | solution.py:144
  267.4 4.0 pad_maximum_fusion
  271.4 25.4 %all-to-all-done.2 = bf16[32,2,4096]{2,1,0:T(2,128)(2,1)S(1)} async-done(((bf16[32,2,4096]{2,1,0:T(2,128)(2,1)}), bf16[32,2,4096]{2,1,0:T(2,128)(2,1)S(1)}, u32[]{:S(2)}, u32[]{:S(2)}) %all-to-all-start.2) | async-done | bytes 524320 | tf_op jit(solution)/shard_map/all_to_all | solution.py:144
  296.8 0.8 copy-done.13
  297.6 6.3 %all-to-all-start.3 = ((f32[1,2,2048,128]{3,1,0,2:T(2,128)}), f32[1,2,2048,128]{3,1,0,2:T(2,128)S(1)}, u32[]{:S(2)}, u32[]{:S(2)}) async-start(f32[1,2,2048,128]{3,1,0,2:T(2,128)} %pad_maximum_fusion), calls=%async_computation.3 | async-start | bytes 4194304 | tf_op jit(solution)/shard_map/all_to_all | solution.py:147
  304.0 3.6 reshape.215
  307.7 0.8 slice.85
  309.2 3.6 reshape.217
  312.8 0.9 copy.50
  313.7 85.7 %all-to-all-done.3 = f32[1,2,2048,128]{3,1,0,2:T(2,128)S(1)} async-done(((f32[1,2,2048,128]{3,1,0,2:T(2,128)}), f32[1,2,2048,128]{3,1,0,2:T(2,128)S(1)}, u32[]{:S(2)}, u32[]{:S(2)}) %all-to-all-start.3) | async-done | bytes 2097184 | tf_op jit(solution)/shard_map/all_to_all | solution.py:147
  399.5 1.4 multiply_reduce_fusion.3
  400.9 1.5 fusion.55
  402.7 99.8 %psum.7 = f32[4,128]{1,0:T(4,128)} all-reduce(f32[4,128]{1,0:T(4,128)S(1)} %pad_maximum_fusion.4), channel_id=1, replica_groups=mesh['grp'=4,'seq'=32,'dp'=4] {'grp','seq','dp'}, use_global_device_ids=true, to_apply=%region_14.15 | all-reduce | flops 512 | bytes 4096 | tf_op jit(solution)/shard_map/psum | solution.py:156
  503.4 1.1 copy.47
  (110 shorter events, 13.3 us)
Async XLA Ops:
  0.6 2.2 copy-start.15
  3.5 0.8 copy-start.3
  3.5 1.5 copy-start.5
  6.5 15.5 %copy-start.16 = (bf16[2,16,48,128]{3,2,1,0:T(8,128)(2,1)S(1)}, bf16[2,16,48,128]{3,2,1,0:T(8,128)(2,1)}, u32[]{:S(2)}) copy-start(bf16[2,16,48,128]{3,2,1,0:T(8,128)(2,1)} %param.10) | copy-start | bytes 1179652
  6.5 15.5 %copy-start.17 = (bf16[2,16,16,128]{3,2,1,0:T(8,128)(2,1)S(1)}, bf16[2,16,16,128]{3,2,1,0:T(8,128)(2,1)}, u32[]{:S(2)}) copy-start(bf16[2,16,16,128]{3,2,1,0:T(8,128)(2,1)} %param.11) | copy-start | bytes 393220
  6.5 96.5 %copy-start.18 = (s32[2]{0:T(128)S(1)}, s32[2]{0:T(128)}, u32[]{:S(2)}) copy-start(s32[2]{0:T(128)} %param.12) | copy-start | bytes 28
  6.5 88.9 %all-to-all-start = ((bf16[32,3,64,128]{3,2,1,0:T(8,128)(2,1)}), bf16[32,3,64,128]{3,2,1,0:T(8,128)(2,1)S(1)}, u32[]{:S(2)}, u32[]{:S(2)}) async-start(bf16[32,3,64,128]{3,2,1,0:T(8,128)(2,1)} %copy.42), calls=%async_computation | async-start | bytes 3145728 | tf_op jit(solution)/shard_map/all_to_all | solution.py:118
  95.4 36.4 %all-to-all-start.1 = ((bf16[32,1,64,128]{3,2,1,0:T(8,128)(2,1)}), bf16[32,1,64,128]{3,2,1,0:T(8,128)(2,1)S(1)}, u32[]{:S(2)}, u32[]{:S(2)}) async-start(bf16[32,1,64,128]{3,2,1,0:T(8,128)(2,1)} %pad_maximum_fusion.2), calls=%async_computation.1 | async-start | bytes 1048576 | tf_op jit(solution)/shard_map/all_to_all | solution.py:119
  131.8 4.1 copy-start.7
  131.8 5.0 %copy-start.10 = (bf16[2048,128]{1,0:T(8,128)(2,1)}, bf16[2048,128]{1,0:T(8,128)(2,1)S(1)}, u32[]{:S(2)}) copy-start(bf16[2048,128]{1,0:T(8,128)(2,1)S(1)} %get-tuple-element.321) | copy-start | bytes 1572868 | tf_op jit(solution)/shard_map/while/body/eval_jaxpr/while
  138.3 1.9 copy-start
  140.8 4.2 copy-start.1
  147.7 1.4 copy-start.8
  147.7 1.4 copy-start.11
  149.1 4.1 copy-start.7
  149.1 5.1 %copy-start.10 = (bf16[2048,128]{1,0:T(8,128)(2,1)}, bf16[2048,128]{1,0:T(8,128)(2,1)S(1)}, u32[]{:S(2)}) copy-start(bf16[2048,128]{1,0:T(8,128)(2,1)S(1)} %get-tuple-element.321) | copy-start | bytes 1572868 | tf_op jit(solution)/shard_map/while/body/eval_jaxpr/while
  155.6 1.9 copy-start
  158.1 4.6 copy-start.1
  165.7 1.4 copy-start.8
  165.7 1.4 copy-start.11
  167.1 4.1 copy-start.7
  167.1 5.1 %copy-start.10 = (bf16[2048,128]{1,0:T(8,128)(2,1)}, bf16[2048,128]{1,0:T(8,128)(2,1)S(1)}, u32[]{:S(2)}) copy-start(bf16[2048,128]{1,0:T(8,128)(2,1)S(1)} %get-tuple-element.321) | copy-start | bytes 1572868 | tf_op jit(solution)/shard_map/while/body/eval_jaxpr/while
  173.6 1.9 copy-start
  176.1 4.6 copy-start.1
  183.8 1.4 copy-start.8
  183.8 1.4 copy-start.11
  185.2 4.1 copy-start.7
  185.2 5.1 %copy-start.10 = (bf16[2048,128]{1,0:T(8,128)(2,1)}, bf16[2048,128]{1,0:T(8,128)(2,1)S(1)}, u32[]{:S(2)}) copy-start(bf16[2048,128]{1,0:T(8,128)(2,1)S(1)} %get-tuple-element.321) | copy-start | bytes 1572868 | tf_op jit(solution)/shard_map/while/body/eval_jaxpr/while
  191.7 1.9 copy-start
  194.2 4.6 copy-start.1
  201.8 1.4 copy-start.8
  201.8 1.4 copy-start.11
  212.6 19.3 %copy-start.14 = (bf16[4,512,128]{2,1,0:T(8,128)(2,1)S(1)}, bf16[4,512,128]{2,1,0:T(8,128)(2,1)}, u32[]{:S(2)}) copy-start(bf16[4,512,128]{2,1,0:T(8,128)(2,1)} %get-tuple-element.95) | copy-start | bytes 1572868
  225.8 35.5 %all-to-all-start.4 = ((bf16[32,2,4096]{2,1,0:T(2,128)(2,1)}), bf16[32,2,4096]{2,1,0:T(2,128)(2,1)S(1)}, u32[]{:S(2)}, u32[]{:S(2)}) async-start(bf16[32,2,4096]{2,1,0:T(2,128)(2,1)} %reshape.216), calls=%async_computation.4 | async-start | bytes 1048576 | tf_op jit(solution)/shard_map/all_to_all | solution.py:145
  240.0 27.3 %copy-start.2 = (f32[2048,128]{1,0:T(8,128)S(1)}, f32[2048,128]{1,0:T(8,128)}, u32[]{:S(2)}) copy-start(f32[2048,128]{1,0:T(8,128)} %get-tuple-element.97) | copy-start | bytes 3145732
  261.3 42.7 %copy-start.12 = (bf16[32,2,4096]{2,1,0:T(2,128)(2,1)}, bf16[32,2,4096]{2,1,0:T(2,128)(2,1)S(1)}, u32[]{:S(2)}) copy-start(bf16[32,2,4096]{2,1,0:T(2,128)(2,1)S(1)} %all-to-all-done.4) | copy-start | bytes 1572868
  261.3 35.5 %all-to-all-start.2 = ((bf16[32,2,4096]{2,1,0:T(2,128)(2,1)}), bf16[32,2,4096]{2,1,0:T(2,128)(2,1)S(1)}, u32[]{:S(2)}, u32[]{:S(2)}) async-start(bf16[32,2,4096]{2,1,0:T(2,128)(2,1)} %reshape.214), calls=%async_computation.2 | async-start | bytes 1048576 | tf_op jit(solution)/shard_map/all_to_all | solution.py:144
  296.8 0.8 copy-start.13
  297.6 101.7 %all-to-all-start.3 = ((f32[1,2,2048,128]{3,1,0,2:T(2,128)}), f32[1,2,2048,128]{3,1,0,2:T(2,128)S(1)}, u32[]{:S(2)}, u32[]{:S(2)}) async-start(f32[1,2,2048,128]{3,1,0,2:T(2,128)} %pad_maximum_fusion), calls=%async_computation.3 | async-start | bytes 4194304 | tf_op jit(solution)/shard_map/all_to_all | solution.py:147
  313.6 85.8 %copy-start.4 = (bf16[32,1,64,128]{3,2,0,1:T(8,128)(2,1)S(1)}, bf16[32,1,64,128]{3,2,0,1:T(8,128)(2,1)}, u32[]{:S(2)}) copy-start(bf16[32,1,64,128]{3,2,0,1:T(8,128)(2,1)} %copy-done.3) | copy-start | bytes 1572868
  313.7 85.8 %copy-start.6 = (bf16[32,1,64,128]{3,2,0,1:T(8,128)(2,1)S(1)}, bf16[32,1,64,128]{3,2,0,1:T(8,128)(2,1)}, u32[]{:S(2)}) copy-start(bf16[32,1,64,128]{3,2,0,1:T(8,128)(2,1)} %copy-done.5) | copy-start | bytes 1572868
  400.9 1.5 copy-start.9
where the time goes:
time: 508 us; the launch traced here: 504 us
  waiting for transfers between devices  220 us (43%)
  blocking collectives  99.8 us (20%)
  local copies, waits for them, and re-layouts  46.1 us (9%)
  matrix products  44.4 us (9%)
  other arithmetic  43.4 us (9%)
  starting transfers between devices  41.6 us (8%)
  loops' own time  7.97 us (2%)
    psum x1, blocking collectives, per_device(): gain_grad = lax.psum(partial_terms, ('grp', 'seq', 'dp'))  99.8 us
    all_to_all x1, waiting for transfers between devices, per_device(): lax.all_to_all(jnp.stack([grad_qn, grad_kn], axis=1), 'seq', split_axis=2...  85.7 us
    all_to_all x1, waiting for transfers between devices, per_device(): lax.all_to_all(outgoing, 'seq', split_axis=0, concat_axis=2, tiled=True)  72.5 us
    all_to_all x1, waiting for transfers between devices, per_device(): lax.all_to_all(joint_cot, 'seq', split_axis=0, concat_axis=2, tiled=True)  27.9 us
    all_to_all x1, waiting for transfers between devices, per_device(): lax.all_to_all(attended[:, None], 'seq', split_axis=2, concat_axis=0, til...  25.4 us
    unnamed x4, other arithmetic  23.4 us
    all_to_all x1, starting transfers between devices, per_device(): lax.all_to_all(outgoing, 'seq', split_axis=0, concat_axis=2, tiled=True)  15.5 us
    unnamed x37, local copies, waits for them, and re-layouts  15.3 us
  transfers between devices with their start and end apart: 5, of which 5 were waited for; matrix products, arithmetic and copies ran while one was open for 7% of the time, Pallas kernels for 0%

commit v1 on v0

v1 whole, which is shorter than its diff:
```python
import functools
import math

import jax
import jax.numpy as jnp
from jax import lax
from jax.experimental import pallas as pl
from jax.experimental.pallas import tpu as pltpu
from jax.sharding import PartitionSpec as P

F32 = jnp.float32
BF16 = jnp.bfloat16
EPS = 1e-06
GROUP = 4
KEY_TILE = 512


def inverse_rms(values):
    return lax.rsqrt(jnp.mean(values * values, axis=-1, keepdims=True) + EPS)


def norm_backward(values, gain, upstream):
    inverse = inverse_rms(values)
    scaled = gain * upstream
    inner = jnp.mean(scaled * values, axis=-1, keepdims=True)
    grad = inverse * scaled - values * (inverse * inverse * inverse * inner)
    return grad, upstream * values * inverse


def pair_kernel(img, txt, length_ref, gains_ref, in_ref, out_ref, terms_ref,
                kn_ref, vaug_ref, eb_ref, dkt_ref, dvt_ref):
    devices = in_ref.shape[0]
    head = in_ref.shape[2]
    blocks = devices // GROUP
    img_block, txt_block = GROUP * img, GROUP * txt
    block = img_block + txt_block
    full = blocks * block
    tile = math.gcd(KEY_TILE, full)
    scale = 1.0 / math.sqrt(head)
    to_exp2 = scale * math.log2(math.e)
    in_txt = 3 * img
    in_cot = 3 * (img + txt)
    out_img = img + txt
    out_txt = out_img + 3 * img
    length = length_ref[0]

    def load(b, img_at, txt_at):
        rows = pl.ds(b * GROUP, GROUP)
        return jnp.concatenate(
            [
                in_ref[rows, img_at : img_at + img].reshape(img_block, head),
                in_ref[rows, txt_at : txt_at + txt].reshape(txt_block, head),
            ],
            axis=0,
        )

    def store(b, img_at, txt_at, values):
        rows = pl.ds(b * GROUP, GROUP)
        out_ref[rows, img_at : img_at + img] = values[:img_block].reshape(GROUP, img, head)
        out_ref[rows, txt_at : txt_at + txt] = values[img_block:].reshape(GROUP, txt, head)

    def gain_rows(which):
        is_img = lax.broadcasted_iota(jnp.int32, (block, head), 0) < img_block
        return jnp.where(is_img, gains_ref[which : which + 1], gains_ref[which + 2 : which + 3])

    def live_rows(b):
        row = lax.broadcasted_iota(jnp.int32, (block, head), 0)
        return jnp.logical_or(row < img_block, row - img_block + b * txt_block < length)

    def add_terms(which, terms):
        terms_ref[which : which + 1] += jnp.sum(terms[:img_block], axis=0, keepdims=True)
        terms_ref[which + 2 : which + 3] += jnp.sum(terms[img_block:], axis=0, keepdims=True)

    terms_ref[...] = jnp.zeros_like(terms_ref)
    dkt_ref[...] = jnp.zeros_like(dkt_ref)
    dvt_ref[...] = jnp.zeros_like(dvt_ref)

    @pl.loop(0, blocks)
    def _keys(b):
        at = pl.ds(pl.multiple_of(b * block, block), block)
        live = live_rows(b)
        raw = load(b, img, in_txt + txt).astype(F32)
        normed = raw * inverse_rms(raw) * gain_rows(1)
        kn_ref[at, :] = jnp.where(live, normed, 0.0).astype(BF16)
        values = load(b, 2 * img, in_txt + 2 * txt).astype(F32)
        vaug_ref[at, :head] = jnp.where(live, values, 0.0).astype(BF16)
        vaug_ref[at, head:] = jnp.where(live, 1.0, 0.0).astype(BF16)

    by_rows = (((1,), (1,)), ((), ()))

    @pl.loop(0, blocks)
    def _queries(b):
        raw = load(b, 0, in_txt).astype(F32)
        gain = gain_rows(0)
        qn = (raw * inverse_rms(raw) * gain).astype(BF16)
        cot = load(b, in_cot, in_cot + img)
        summed = jnp.zeros((block, 2 * head), F32)
        for start in range(0, full, tile):
            keys = slice(start, start + tile)
            scores = lax.dot_general(qn, kn_ref[keys, :], by_rows, preferred_element_type=F32)
            expo = jnp.exp2(scores * to_exp2).astype(BF16)
            eb_ref[:, keys] = expo
            summed += jnp.dot(expo, vaug_ref[keys, :], preferred_element_type=F32)
        per_total = 1.0 / summed[:, head:]
        out = summed[:, :head] * per_total
        store(b, 0, img, out.astype(BF16))
        cot32 = cot.astype(F32)
        delta = jnp.sum(out * cot32, axis=-1, keepdims=True)
        cot_t = jnp.transpose((cot32 * per_total).astype(BF16))
        qn_t = jnp.transpose((qn.astype(F32) * (per_total * scale)).astype(BF16))
        dq = jnp.zeros((block, head), F32)
        for start in range(0, full, tile):
            keys = slice(start, start + tile)
            expo = eb_ref[:, keys]
            dprobs = lax.dot_general(
                cot, vaug_ref[keys, :head], by_rows, preferred_element_type=F32
            )
            dscores = (expo.astype(F32) * (dprobs - delta)).astype(BF16)
            dq += jnp.dot(dscores, kn_ref[keys, :], preferred_element_type=F32)
            dkt_ref[:, keys] += jnp.dot(qn_t, dscores, preferred_element_type=F32)
            dvt_ref[:, keys] += jnp.dot(cot_t, expo, preferred_element_type=F32)
        grad, terms = norm_backward(raw, gain, dq * (per_total * scale))
        store(b, out_img, out_txt, grad.astype(BF16))
        add_terms(0, terms)

    @pl.loop(0, blocks)
    def _key_grads(b):
        at = pl.ds(pl.multiple_of(b * block, block), block)
        live = live_rows(b)
        raw = load(b, img, in_txt + txt).astype(F32)
        dk = jnp.where(live, jnp.transpose(dkt_ref[:, at]), 0.0)
        grad, terms = norm_backward(raw, gain_rows(1), dk)
        store(b, out_img + img, out_txt + txt, grad.astype(BF16))
        add_terms(1, terms)
        dv = jnp.where(live, jnp.transpose(dvt_ref[:, at]), 0.0)
        store(b, out_img + 2 * img, out_txt + 2 * txt, dv.astype(BF16))


def attend_pair(arrived, length, gains, img, txt):
    devices, rows, head = arrived.shape
    full = devices * (img + txt)
    block = GROUP * (img + txt)
    return pl.pallas_call(
        functools.partial(pair_kernel, img, txt),
        out_shape=(
            jax.ShapeDtypeStruct((devices, rows, head), BF16),
            jax.ShapeDtypeStruct((4, head), F32),
        ),
        in_specs=[
            pl.BlockSpec(memory_space=pltpu.SMEM),
            pl.BlockSpec(memory_space=pltpu.VMEM),
            pl.BlockSpec(memory_space=pltpu.VMEM),
        ],
        out_specs=(
            pl.BlockSpec(memory_space=pltpu.VMEM),
            pl.BlockSpec(memory_space=pltpu.VMEM),
        ),
        scratch_shapes=[
            pltpu.VMEM((full, head), BF16),
            pltpu.VMEM((full, 2 * head), BF16),
            pltpu.VMEM((block, full), BF16),
            pltpu.VMEM((head, full), F32),
            pltpu.VMEM((head, full), F32),
        ],
        compiler_params=pltpu.CompilerParams(vmem_limit_bytes=40 * 1024 * 1024),
        cost_estimate=pl.CostEstimate(
            flops=12 * full * full * head,
            bytes_accessed=4 * devices * rows * head,
            transcendentals=full * full,
        ),
        name="attend_pair",
    )(length, gains, arrived)


def sum_everywhere(term, axes):
    count = math.prod(lax.axis_size(axis) for axis in axes)
    step = 1
    while step < count:
        radix = min(8, count // step)
        parts = [term]
        for other in range(1, radix):
            perm = [(i, i ^ (other * step)) for i in range(count)]
            parts.append(lax.ppermute(term, axes, perm))
        while len(parts) > 1:
            parts = [parts[i] + parts[i + 1] for i in range(0, len(parts), 2)]
        term = parts[0]
        step *= radix
    return term


def per_device(img_qkv, txt_qkv, img_cot, txt_cot, lengths, norm_gains):
    samples, heads, _, img, head = img_qkv.shape
    txt = txt_qkv.shape[3]
    pairs = samples * heads
    devices = lax.axis_size("seq")
    assert pairs == devices
    outgoing = jnp.concatenate(
        [
            img_qkv.reshape(pairs, 3 * img, head),
            txt_qkv.reshape(pairs, 3 * txt, head),
            img_cot.reshape(pairs, img, head),
            txt_cot.reshape(pairs, txt, head),
        ],
        axis=1,
    )
    arrived = lax.all_to_all(outgoing, "seq", split_axis=0, concat_axis=0, tiled=True)
    sample = lax.axis_index("seq") // heads
    length = lax.dynamic_slice_in_dim(lengths, sample, 1, 0)
    results, terms = attend_pair(arrived, length, norm_gains, img, txt)
    back = lax.all_to_all(results, "seq", split_axis=0, concat_axis=0, tiled=True)
    gain_grad = sum_everywhere(terms, ("grp", "seq", "dp"))
    own = img + txt
    img_out = back[:, :img].reshape(samples, heads, img, head)
    txt_out = back[:, img:own].reshape(samples, heads, txt, head)
    img_grad = back[:, own : own + 3 * img].reshape(samples, heads, 3, img, head)
    txt_grad = back[:, own + 3 * img :].reshape(samples, heads, 3, txt, head)
    return (img_out, txt_out, img_grad, txt_grad, gain_grad)


def solution(mesh):
    rows = P(("grp", "dp"), None, "seq", None)
    grads = P(("grp", "dp"), None, None, "seq", None)
    return jax.shard_map(
        per_device,
        mesh=mesh,
        in_specs=(grads, grads, rows, rows, P(("grp", "dp")), P()),
        out_specs=(rows, rows, grads, grads, P()),
        check_vma=False,
    )
```

time: 508 us -> 324 us (0.64)
  starting transfers between devices: 41.6 us -> 166 us
  blocking collectives: 99.8 us -> 0 us
  waiting for transfers between devices: 220 us -> 126 us
  matrix products: 44.4 us -> 0 us
  local copies, waits for them, and re-layouts: 46.1 us -> 3.31 us
  other arithmetic: 43.4 us -> 3.78 us
  Pallas kernels: 0 us -> 23 us
  loops' own time: 7.97 us -> 0 us
    ppermute x0 -> x21, starting transfers between devices: none -> 143 us  [sum_everywhere(): parts.append(lax.ppermute(term, axes, perm))]
    all_to_all x5 -> x2, waiting for transfers between devices: 220 us -> 95.2 us  [the longest x1 95.2 us: per_device(): lax.all_to_all(outgoing, 'seq', split_axis=0, concat_axis=0, tiled=True)]
    psum x1 -> x0, blocking collectives: 99.8 us -> none  [per_device(): gain_grad = lax.psum(partial_terms, ('grp', 'seq', 'dp'))]
    dot_general x24 -> x0, matrix products: 44.4 us -> none  [the longest x4 12.3 us: step(): jnp.einsum('qk,qd->kd', dscores, query_block, preferred_element_type=jnp....]
    ppermute x0 -> x21, waiting for transfers between devices: none -> 31.2 us  [sum_everywhere(): parts.append(lax.ppermute(term, axes, perm))]
    unnamed x4 -> x0, other arithmetic: 23.4 us -> none
    pallas_call x0 -> x1, Pallas kernels: none -> 23 us  [attend_pair(): pl.pallas_call(functools.partial(pair_kernel, img, txt), out_shape=(jax.S...]
    all_to_all x5 -> x2, starting transfers between devices: 41.6 us -> 22.9 us  [the longest x1 15.5 us: per_device(): lax.all_to_all(outgoing, 'seq', split_axis=0, concat_axis=0, tiled=True)]
  transfers between devices with their start and end apart: 5 -> 23, of which waited for: 5 -> 5; matrix products, arithmetic and copies ran while one was open for 7% -> 0% of each run, Pallas kernels for 0% -> 0%
where the time goes in v1:
time: 324 us; the launch traced here: 323 us
  starting transfers between devices  166 us (51%)
  waiting for transfers between devices  126 us (39%)
  Pallas kernels  23 us (7%)
  other arithmetic  3.78 us (1%)
  local copies, waits for them, and re-layouts  3.31 us (1%)
    ppermute x21, starting transfers between devices, sum_everywhere(): parts.append(lax.ppermute(term, axes, perm))  143 us
    all_to_all x1, waiting for transfers between devices, per_device(): lax.all_to_all(outgoing, 'seq', split_axis=0, concat_axis=0, tiled=True)  95.2 us
    ppermute x21, waiting for transfers between devices, sum_everywhere(): parts.append(lax.ppermute(term, axes, perm))  31.2 us
    pallas_call x1, Pallas kernels, attend_pair(): pl.pallas_call(functools.partial(pair_kernel, img, txt), out_shape=(jax.S...  23 us
    all_to_all x1, starting transfers between devices, per_device(): lax.all_to_all(outgoing, 'seq', split_axis=0, concat_axis=0, tiled=True)  15.5 us
    all_to_all x1, starting transfers between devices, per_device(): lax.all_to_all(results, 'seq', split_axis=0, concat_axis=0, tiled=True)  7.43 us
  transfers between devices with their start and end apart: 23, of which 5 were waited for; matrix products, arithmetic and copies ran while one was open for 0% of the time, Pallas kernels for 0%

profile of v1, /device:TPU:24, one launch (start us, length us, event | category | flops | bytes accessed | tf_op | source)
XLA Modules:
  0.0 323.1 jit_solution(11756960146604750691)
XLA Ops:
  0.6 3.2 pad_maximum_fusion
  3.8 0.0 copy-start.1
  3.8 0.0 copy-start
  3.8 15.5 %all-to-all-start = ((bf16[32,256,128]{2,1,0:T(8,128)(2,1)}), bf16[32,256,128]{2,1,0:T(8,128)(2,1)S(1)}, u32[]{:S(2)}, u32[]{:S(2)}) async-start(bf16[32,256,128]{2,1,0:T(8,128)(2,1)} %pad_maximum_fusion), calls=%async_computation | async-start | bytes 4194304 | tf_op jit(solution)/shard_map/all_to_all | solution.py:206
  19.3 0.0 copy-done.1
  19.4 0.6 dynamic_slice.3.length_ref
  19.9 95.2 %all-to-all-done.in_ref = bf16[32,256,128]{2,1,0:T(8,128)(2,1)S(1)} async-done(((bf16[32,256,128]{2,1,0:T(8,128)(2,1)}), bf16[32,256,128]{2,1,0:T(8,128)(2,1)S(1)}, u32[]{:S(2)}, u32[]{:S(2)}) %all-to-all-start) | async-done | bytes 2097184 | tf_op jit(solution)/shard_map/all_to_all | solution.py:206
  115.1 0.0 copy-done
  115.1 23.0 %attend_pair.1 = (bf16[32,256,128]{2,1,0:T(8,128)(2,1)}, f32[4,128]{1,0:T(4,128)S(1)}) custom-call(s32[1]{0:T(128)} %dynamic_slice.3.length_ref, f32[4,128]{1,0:T(4,128)S(1)} %copy-done, bf16[32,256,128]{2,1,0:T(8,128)(2,1)S(1)} %all-to-all-done.in_ref), custom_call_target="tpu_custom_call" | custom-call | flops 6442450944 | bytes 4194304 | tf_op jit(solution)/shard_map/attend_pair/pallas_call | solution.py:143
  138.1 7.4 %all-to-all-start.1 = ((bf16[32,256,128]{2,1,0:T(8,128)(2,1)}), bf16[32,256,128]{2,1,0:T(8,128)(2,1)S(1)}, u32[]{:S(2)}, u32[]{:S(2)}) async-start(bf16[32,256,128]{2,1,0:T(8,128)(2,1)} %get-tuple-element.7), calls=%async_computation.1 | async-start | bytes 4194304 | tf_op jit(solution)/shard_map/all_to_all | solution.py:210
  145.6 8.0 %collective-permute-start.6 = (f32[4,128]{1,0:T(4,128)S(1)}, f32[4,128]{1,0:T(4,128)S(1)}, u32[]{:S(2)}, u32[]{:S(2)}) collective-permute-start(f32[4,128]{1,0:T(4,128)S(1)} %get-tuple-element.8), channel_id=1, source_target_pairs={{0,7},{1,6},{2,5},{3,4},{4,3},{5,2},{6,1},{7,0},{8,15},{9,14},{10,... | collective-permute-start | bytes 6152 | tf_op jit(solution)/shard_map/ppermute | solution.py:183
  153.6 6.3 %collective-permute-start.5 = (f32[4,128]{1,0:T(4,128)S(1)}, f32[4,128]{1,0:T(4,128)S(1)}, u32[]{:S(2)}, u32[]{:S(2)}) collective-permute-start(f32[4,128]{1,0:T(4,128)S(1)} %get-tuple-element.8), channel_id=1, source_target_pairs={{0,6},{1,7},{2,4},{3,5},{4,2},{5,3},{6,0},{7,1},{8,14},{9,15},{10,... | collective-permute-start | bytes 6152 | tf_op jit(solution)/shard_map/ppermute | solution.py:183
  159.9 4.3 %collective-permute-start.4 = (f32[4,128]{1,0:T(4,128)S(1)}, f32[4,128]{1,0:T(4,128)S(1)}, u32[]{:S(2)}, u32[]{:S(2)}) collective-permute-start(f32[4,128]{1,0:T(4,128)S(1)} %get-tuple-element.8), channel_id=1, source_target_pairs={{0,5},{1,4},{2,7},{3,6},{4,1},{5,0},{6,3},{7,2},{8,13},{9,12},{10,... | collective-permute-start | bytes 6152 | tf_op jit(solution)/shard_map/ppermute | solution.py:183
  164.2 2.1 collective-permute-start.3
  166.3 7.7 %collective-permute-start.2 = (f32[4,128]{1,0:T(4,128)S(1)}, f32[4,128]{1,0:T(4,128)S(1)}, u32[]{:S(2)}, u32[]{:S(2)}) collective-permute-start(f32[4,128]{1,0:T(4,128)S(1)} %get-tuple-element.8), channel_id=1, source_target_pairs={{0,3},{1,2},{2,1},{3,0},{4,7},{5,6},{6,5},{7,4},{8,11},{9,10},{10,... | collective-permute-start | bytes 6152 | tf_op jit(solution)/shard_map/ppermute | solution.py:183
  174.0 16.8 %collective-permute-done.6 = f32[4,128]{1,0:T(4,128)S(1)} collective-permute-done((f32[4,128]{1,0:T(4,128)S(1)}, f32[4,128]{1,0:T(4,128)S(1)}, u32[]{:S(2)}, u32[]{:S(2)}) %collective-permute-start.6) | collective-permute-done | bytes 2080 | tf_op jit(solution)/shard_map/ppermute | solution.py:183
  190.8 6.4 %collective-permute-start.1 = (f32[4,128]{1,0:T(4,128)S(1)}, f32[4,128]{1,0:T(4,128)S(1)}, u32[]{:S(2)}, u32[]{:S(2)}) collective-permute-start(f32[4,128]{1,0:T(4,128)S(1)} %get-tuple-element.8), channel_id=1, source_target_pairs={{0,2},{1,3},{2,0},{3,1},{4,6},{5,7},{6,4},{7,5},{8,10},{9,11},{10,... | collective-permute-start | bytes 6152 | tf_op jit(solution)/shard_map/ppermute | solution.py:183
  197.2 0.0 collective-permute-done.5
  197.2 3.4 %collective-permute-start = (f32[4,128]{1,0:T(4,128)S(1)}, f32[4,128]{1,0:T(4,128)S(1)}, u32[]{:S(2)}, u32[]{:S(2)}) collective-permute-start(f32[4,128]{1,0:T(4,128)S(1)} %get-tuple-element.8), channel_id=1, source_target_pairs={{0,1},{1,0},{2,3},{3,2},{4,5},{5,4},{6,7},{7,6},{8,9},{9,8},{10,11... | collective-permute-start | bytes 6152 | tf_op jit(solution)/shard_map/ppermute | solution.py:183
  200.6 0.0 collective-permute-done.4
  200.6 0.0 collective-permute-done.3
  200.6 0.0 collective-permute-done.2
  200.6 4.6 %collective-permute-done.1 = f32[4,128]{1,0:T(4,128)S(1)} collective-permute-done((f32[4,128]{1,0:T(4,128)S(1)}, f32[4,128]{1,0:T(4,128)S(1)}, u32[]{:S(2)}, u32[]{:S(2)}) %collective-permute-start.1) | collective-permute-done | bytes 2080 | tf_op jit(solution)/shard_map/ppermute | solution.py:183
  205.3 0.0 collective-permute-done
  205.3 24.6 %collective-permute-start.13 = (f32[4,128]{1,0:T(4,128)S(1)}, f32[4,128]{1,0:T(4,128)S(1)}, u32[]{:S(2)}, u32[]{:S(2)}) collective-permute-start(f32[4,128]{1,0:T(4,128)S(1)} %add_add_fusion.2), channel_id=1, source_target_pairs={{0,56},{1,57},{2,58},{3,59},{4,60},{5,61},{6,62},{7,63},{8,48},{9,... | collective-permute-start | bytes 6152 | tf_op jit(solution)/shard_map/ppermute | solution.py:183
  229.9 1.9 collective-permute-start.12
  231.9 33.0 %collective-permute-start.11 = (f32[4,128]{1,0:T(4,128)S(1)}, f32[4,128]{1,0:T(4,128)S(1)}, u32[]{:S(2)}, u32[]{:S(2)}) collective-permute-start(f32[4,128]{1,0:T(4,128)S(1)} %add_add_fusion.2), channel_id=1, source_target_pairs={{0,40},{1,41},{2,42},{3,43},{4,44},{5,45},{6,46},{7,47},{8,32},{9,... | collective-permute-start | bytes 6152 | tf_op jit(solution)/shard_map/ppermute | solution.py:183
  264.9 1.9 collective-permute-start.10
  266.8 5.1 %collective-permute-start.9 = (f32[4,128]{1,0:T(4,128)S(1)}, f32[4,128]{1,0:T(4,128)S(1)}, u32[]{:S(2)}, u32[]{:S(2)}) collective-permute-start(f32[4,128]{1,0:T(4,128)S(1)} %add_add_fusion.2), channel_id=1, source_target_pairs={{0,24},{1,25},{2,26},{3,27},{4,28},{5,29},{6,30},{7,31},{8,16},{9,... | collective-permute-start | bytes 6152 | tf_op jit(solution)/shard_map/ppermute | solution.py:183
  271.9 0.0 collective-permute-done.13
  272.0 2.5 collective-permute-start.8
  274.4 0.0 collective-permute-done.12
  274.4 3.1 collective-permute-start.7
  277.6 0.0 collective-permute-done.11
  277.6 0.0 collective-permute-done.10
  277.6 0.0 collective-permute-done.9
  277.6 0.0 collective-permute-done.8
  277.6 3.8 %collective-permute-done.7 = f32[4,128]{1,0:T(4,128)S(1)} collective-permute-done((f32[4,128]{1,0:T(4,128)S(1)}, f32[4,128]{1,0:T(4,128)S(1)}, u32[]{:S(2)}, u32[]{:S(2)}) %collective-permute-start.7) | collective-permute-done | bytes 2080 | tf_op jit(solution)/shard_map/ppermute | solution.py:183
  281.4 6.0 %collective-permute-start.20 = (f32[4,128]{1,0:T(4,128)S(1)}, f32[4,128]{1,0:T(4,128)S(1)}, u32[]{:S(2)}, u32[]{:S(2)}) collective-permute-start(f32[4,128]{1,0:T(4,128)S(1)} %add_add_fusion.1), channel_id=1, source_target_pairs={{0,448},{1,449},{2,450},{3,451},{4,452},{5,453},{6,454},{7,455},{8... | collective-permute-start | bytes 6152 | tf_op jit(solution)/shard_map/ppermute | solution.py:183
  287.4 4.9 %collective-permute-start.19 = (f32[4,128]{1,0:T(4,128)S(1)}, f32[4,128]{1,0:T(4,128)S(1)}, u32[]{:S(2)}, u32[]{:S(2)}) collective-permute-start(f32[4,128]{1,0:T(4,128)S(1)} %add_add_fusion.1), channel_id=1, source_target_pairs={{0,384},{1,385},{2,386},{3,387},{4,388},{5,389},{6,390},{7,391},{8... | collective-permute-start | bytes 6152 | tf_op jit(solution)/shard_map/ppermute | solution.py:183
  292.4 2.8 collective-permute-start.18
  295.2 5.4 %collective-permute-start.17 = (f32[4,128]{1,0:T(4,128)S(1)}, f32[4,128]{1,0:T(4,128)S(1)}, u32[]{:S(2)}, u32[]{:S(2)}) collective-permute-start(f32[4,128]{1,0:T(4,128)S(1)} %add_add_fusion.1), channel_id=1, source_target_pairs={{0,256},{1,257},{2,258},{3,259},{4,260},{5,261},{6,262},{7,263},{8... | collective-permute-start | bytes 6152 | tf_op jit(solution)/shard_map/ppermute | solution.py:183
  300.7 5.3 %collective-permute-start.16 = (f32[4,128]{1,0:T(4,128)S(1)}, f32[4,128]{1,0:T(4,128)S(1)}, u32[]{:S(2)}, u32[]{:S(2)}) collective-permute-start(f32[4,128]{1,0:T(4,128)S(1)} %add_add_fusion.1), channel_id=1, source_target_pairs={{0,192},{1,193},{2,194},{3,195},{4,196},{5,197},{6,198},{7,199},{8... | collective-permute-start | bytes 6152 | tf_op jit(solution)/shard_map/ppermute | solution.py:183
  306.0 0.0 collective-permute-done.20
  306.0 4.4 %collective-permute-start.15 = (f32[4,128]{1,0:T(4,128)S(1)}, f32[4,128]{1,0:T(4,128)S(1)}, u32[]{:S(2)}, u32[]{:S(2)}) collective-permute-start(f32[4,128]{1,0:T(4,128)S(1)} %add_add_fusion.1), channel_id=1, source_target_pairs={{0,128},{1,129},{2,130},{3,131},{4,132},{5,133},{6,134},{7,135},{8... | collective-permute-start | bytes 6152 | tf_op jit(solution)/shard_map/ppermute | solution.py:183
  310.4 0.0 collective-permute-done.19
  310.4 3.4 %collective-permute-start.14 = (f32[4,128]{1,0:T(4,128)S(1)}, f32[4,128]{1,0:T(4,128)S(1)}, u32[]{:S(2)}, u32[]{:S(2)}) collective-permute-start(f32[4,128]{1,0:T(4,128)S(1)} %add_add_fusion.1), channel_id=1, source_target_pairs={{0,64},{1,65},{2,66},{3,67},{4,68},{5,69},{6,70},{7,71},{8,72},{9,... | collective-permute-start | bytes 6152 | tf_op jit(solution)/shard_map/ppermute | solution.py:183
  313.8 0.0 collective-permute-done.18
  313.8 0.0 collective-permute-done.17
  313.9 0.0 collective-permute-done.16
  313.9 0.0 collective-permute-done.15
  313.9 5.9 %collective-permute-done.14 = f32[4,128]{1,0:T(4,128)S(1)} collective-permute-done((f32[4,128]{1,0:T(4,128)S(1)}, f32[4,128]{1,0:T(4,128)S(1)}, u32[]{:S(2)}, u32[]{:S(2)}) %collective-permute-start.14) | collective-permute-done | bytes 2080 | tf_op jit(solution)/shard_map/ppermute | solution.py:183
  319.8 0.6 add_add_fusion
  320.4 0.0 all-to-all-done.1
  320.4 0.7 slice.17
  321.1 0.9 fusion
  322.0 1.1 slice.18
  (2 shorter events, 0.0 us)
Async XLA Ops:
  3.8 15.5 %copy-start.1 = (s32[2]{0:T(128)S(1)}, s32[2]{0:T(128)}, u32[]{:S(2)}) copy-start(s32[2]{0:T(128)} %param.10) | copy-start | bytes 28
  3.8 111.3 %copy-start = (f32[4,128]{1,0:T(4,128)S(1)}, f32[4,128]{1,0:T(4,128)}, u32[]{:S(2)}) copy-start(f32[4,128]{1,0:T(4,128)} %gains_ref.1) | copy-start | bytes 6148
  3.8 111.3 %all-to-all-start = ((bf16[32,256,128]{2,1,0:T(8,128)(2,1)}), bf16[32,256,128]{2,1,0:T(8,128)(2,1)S(1)}, u32[]{:S(2)}, u32[]{:S(2)}) async-start(bf16[32,256,128]{2,1,0:T(8,128)(2,1)} %pad_maximum_fusion), calls=%async_computation | async-start | bytes 4194304 | tf_op jit(solution)/shard_map/all_to_all | solution.py:206
  138.1 182.3 %all-to-all-start.1 = ((bf16[32,256,128]{2,1,0:T(8,128)(2,1)}), bf16[32,256,128]{2,1,0:T(8,128)(2,1)S(1)}, u32[]{:S(2)}, u32[]{:S(2)}) async-start(bf16[32,256,128]{2,1,0:T(8,128)(2,1)} %get-tuple-element.7), calls=%async_computation.1 | async-start | bytes 4194304 | tf_op jit(solution)/shard_map/all_to_all | solution.py:210
  145.6 45.3 %collective-permute-start.6 = (f32[4,128]{1,0:T(4,128)S(1)}, f32[4,128]{1,0:T(4,128)S(1)}, u32[]{:S(2)}, u32[]{:S(2)}) collective-permute-start(f32[4,128]{1,0:T(4,128)S(1)} %get-tuple-element.8), channel_id=1, source_target_pairs={{0,7},{1,6},{2,5},{3,4},{4,3},{5,2},{6,1},{7,0},{8,15},{9,14},{10,... | collective-permute-start | bytes 6152 | tf_op jit(solution)/shard_map/ppermute | solution.py:183
  153.6 43.6 %collective-permute-start.5 = (f32[4,128]{1,0:T(4,128)S(1)}, f32[4,128]{1,0:T(4,128)S(1)}, u32[]{:S(2)}, u32[]{:S(2)}) collective-permute-start(f32[4,128]{1,0:T(4,128)S(1)} %get-tuple-element.8), channel_id=1, source_target_pairs={{0,6},{1,7},{2,4},{3,5},{4,2},{5,3},{6,0},{7,1},{8,14},{9,15},{10,... | collective-permute-start | bytes 6152 | tf_op jit(solution)/shard_map/ppermute | solution.py:183
  159.9 40.7 %collective-permute-start.4 = (f32[4,128]{1,0:T(4,128)S(1)}, f32[4,128]{1,0:T(4,128)S(1)}, u32[]{:S(2)}, u32[]{:S(2)}) collective-permute-start(f32[4,128]{1,0:T(4,128)S(1)} %get-tuple-element.8), channel_id=1, source_target_pairs={{0,5},{1,4},{2,7},{3,6},{4,1},{5,0},{6,3},{7,2},{8,13},{9,12},{10,... | collective-permute-start | bytes 6152 | tf_op jit(solution)/shard_map/ppermute | solution.py:183
  164.2 36.4 %collective-permute-start.3 = (f32[4,128]{1,0:T(4,128)S(1)}, f32[4,128]{1,0:T(4,128)S(1)}, u32[]{:S(2)}, u32[]{:S(2)}) collective-permute-start(f32[4,128]{1,0:T(4,128)S(1)} %get-tuple-element.8), channel_id=1, source_target_pairs={{0,4},{1,5},{2,6},{3,7},{4,0},{5,1},{6,2},{7,3},{8,12},{9,13},{10,... | collective-permute-start | bytes 6152 | tf_op jit(solution)/shard_map/ppermute | solution.py:183
  166.3 34.3 %collective-permute-start.2 = (f32[4,128]{1,0:T(4,128)S(1)}, f32[4,128]{1,0:T(4,128)S(1)}, u32[]{:S(2)}, u32[]{:S(2)}) collective-permute-start(f32[4,128]{1,0:T(4,128)S(1)} %get-tuple-element.8), channel_id=1, source_target_pairs={{0,3},{1,2},{2,1},{3,0},{4,7},{5,6},{6,5},{7,4},{8,11},{9,10},{10,... | collective-permute-start | bytes 6152 | tf_op jit(solution)/shard_map/ppermute | solution.py:183
  190.8 14.4 %collective-permute-start.1 = (f32[4,128]{1,0:T(4,128)S(1)}, f32[4,128]{1,0:T(4,128)S(1)}, u32[]{:S(2)}, u32[]{:S(2)}) collective-permute-start(f32[4,128]{1,0:T(4,128)S(1)} %get-tuple-element.8), channel_id=1, source_target_pairs={{0,2},{1,3},{2,0},{3,1},{4,6},{5,7},{6,4},{7,5},{8,10},{9,11},{10,... | collective-permute-start | bytes 6152 | tf_op jit(solution)/shard_map/ppermute | solution.py:183
  197.2 8.1 %collective-permute-start = (f32[4,128]{1,0:T(4,128)S(1)}, f32[4,128]{1,0:T(4,128)S(1)}, u32[]{:S(2)}, u32[]{:S(2)}) collective-permute-start(f32[4,128]{1,0:T(4,128)S(1)} %get-tuple-element.8), channel_id=1, source_target_pairs={{0,1},{1,0},{2,3},{3,2},{4,5},{5,4},{6,7},{7,6},{8,9},{9,8},{10,11... | collective-permute-start | bytes 6152 | tf_op jit(solution)/shard_map/ppermute | solution.py:183
  205.3 66.7 %collective-permute-start.13 = (f32[4,128]{1,0:T(4,128)S(1)}, f32[4,128]{1,0:T(4,128)S(1)}, u32[]{:S(2)}, u32[]{:S(2)}) collective-permute-start(f32[4,128]{1,0:T(4,128)S(1)} %add_add_fusion.2), channel_id=1, source_target_pairs={{0,56},{1,57},{2,58},{3,59},{4,60},{5,61},{6,62},{7,63},{8,48},{9,... | collective-permute-start | bytes 6152 | tf_op jit(solution)/shard_map/ppermute | solution.py:183
  229.9 44.5 %collective-permute-start.12 = (f32[4,128]{1,0:T(4,128)S(1)}, f32[4,128]{1,0:T(4,128)S(1)}, u32[]{:S(2)}, u32[]{:S(2)}) collective-permute-start(f32[4,128]{1,0:T(4,128)S(1)} %add_add_fusion.2), channel_id=1, source_target_pairs={{0,48},{1,49},{2,50},{3,51},{4,52},{5,53},{6,54},{7,55},{8,56},{9,... | collective-permute-start | bytes 6152 | tf_op jit(solution)/shard_map/ppermute | solution.py:183
  231.9 45.7 %collective-permute-start.11 = (f32[4,128]{1,0:T(4,128)S(1)}, f32[4,128]{1,0:T(4,128)S(1)}, u32[]{:S(2)}, u32[]{:S(2)}) collective-permute-start(f32[4,128]{1,0:T(4,128)S(1)} %add_add_fusion.2), channel_id=1, source_target_pairs={{0,40},{1,41},{2,42},{3,43},{4,44},{5,45},{6,46},{7,47},{8,32},{9,... | collective-permute-start | bytes 6152 | tf_op jit(solution)/shard_map/ppermute | solution.py:183
  264.9 12.7 %collective-permute-start.10 = (f32[4,128]{1,0:T(4,128)S(1)}, f32[4,128]{1,0:T(4,128)S(1)}, u32[]{:S(2)}, u32[]{:S(2)}) collective-permute-start(f32[4,128]{1,0:T(4,128)S(1)} %add_add_fusion.2), channel_id=1, source_target_pairs={{0,32},{1,33},{2,34},{3,35},{4,36},{5,37},{6,38},{7,39},{8,40},{9,... | collective-permute-start | bytes 6152 | tf_op jit(solution)/shard_map/ppermute | solution.py:183
  266.8 10.8 %collective-permute-start.9 = (f32[4,128]{1,0:T(4,128)S(1)}, f32[4,128]{1,0:T(4,128)S(1)}, u32[]{:S(2)}, u32[]{:S(2)}) collective-permute-start(f32[4,128]{1,0:T(4,128)S(1)} %add_add_fusion.2), channel_id=1, source_target_pairs={{0,24},{1,25},{2,26},{3,27},{4,28},{5,29},{6,30},{7,31},{8,16},{9,... | collective-permute-start | bytes 6152 | tf_op jit(solution)/shard_map/ppermute | solution.py:183
  272.0 5.7 %collective-permute-start.8 = (f32[4,128]{1,0:T(4,128)S(1)}, f32[4,128]{1,0:T(4,128)S(1)}, u32[]{:S(2)}, u32[]{:S(2)}) collective-permute-start(f32[4,128]{1,0:T(4,128)S(1)} %add_add_fusion.2), channel_id=1, source_target_pairs={{0,16},{1,17},{2,18},{3,19},{4,20},{5,21},{6,22},{7,23},{8,24},{9,... | collective-permute-start | bytes 6152 | tf_op jit(solution)/shard_map/ppermute | solution.py:183
  274.4 7.0 %collective-permute-start.7 = (f32[4,128]{1,0:T(4,128)S(1)}, f32[4,128]{1,0:T(4,128)S(1)}, u32[]{:S(2)}, u32[]{:S(2)}) collective-permute-start(f32[4,128]{1,0:T(4,128)S(1)} %add_add_fusion.2), channel_id=1, source_target_pairs={{0,8},{1,9},{2,10},{3,11},{4,12},{5,13},{6,14},{7,15},{8,0},{9,1},... | collective-permute-start | bytes 6152 | tf_op jit(solution)/shard_map/ppermute | solution.py:183
  281.4 24.5 %collective-permute-start.20 = (f32[4,128]{1,0:T(4,128)S(1)}, f32[4,128]{1,0:T(4,128)S(1)}, u32[]{:S(2)}, u32[]{:S(2)}) collective-permute-start(f32[4,128]{1,0:T(4,128)S(1)} %add_add_fusion.1), channel_id=1, source_target_pairs={{0,448},{1,449},{2,450},{3,451},{4,452},{5,453},{6,454},{7,455},{8... | collective-permute-start | bytes 6152 | tf_op jit(solution)/shard_map/ppermute | solution.py:183
  287.4 23.0 %collective-permute-start.19 = (f32[4,128]{1,0:T(4,128)S(1)}, f32[4,128]{1,0:T(4,128)S(1)}, u32[]{:S(2)}, u32[]{:S(2)}) collective-permute-start(f32[4,128]{1,0:T(4,128)S(1)} %add_add_fusion.1), channel_id=1, source_target_pairs={{0,384},{1,385},{2,386},{3,387},{4,388},{5,389},{6,390},{7,391},{8... | collective-permute-start | bytes 6152 | tf_op jit(solution)/shard_map/ppermute | solution.py:183
  292.4 21.5 %collective-permute-start.18 = (f32[4,128]{1,0:T(4,128)S(1)}, f32[4,128]{1,0:T(4,128)S(1)}, u32[]{:S(2)}, u32[]{:S(2)}) collective-permute-start(f32[4,128]{1,0:T(4,128)S(1)} %add_add_fusion.1), channel_id=1, source_target_pairs={{0,320},{1,321},{2,322},{3,323},{4,324},{5,325},{6,326},{7,327},{8... | collective-permute-start | bytes 6152 | tf_op jit(solution)/shard_map/ppermute | solution.py:183
  295.2 18.6 %collective-permute-start.17 = (f32[4,128]{1,0:T(4,128)S(1)}, f32[4,128]{1,0:T(4,128)S(1)}, u32[]{:S(2)}, u32[]{:S(2)}) collective-permute-start(f32[4,128]{1,0:T(4,128)S(1)} %add_add_fusion.1), channel_id=1, source_target_pairs={{0,256},{1,257},{2,258},{3,259},{4,260},{5,261},{6,262},{7,263},{8... | collective-permute-start | bytes 6152 | tf_op jit(solution)/shard_map/ppermute | solution.py:183
  300.7 13.2 %collective-permute-start.16 = (f32[4,128]{1,0:T(4,128)S(1)}, f32[4,128]{1,0:T(4,128)S(1)}, u32[]{:S(2)}, u32[]{:S(2)}) collective-permute-start(f32[4,128]{1,0:T(4,128)S(1)} %add_add_fusion.1), channel_id=1, source_target_pairs={{0,192},{1,193},{2,194},{3,195},{4,196},{5,197},{6,198},{7,199},{8... | collective-permute-start | bytes 6152 | tf_op jit(solution)/shard_map/ppermute | solution.py:183
  306.0 7.9 %collective-permute-start.15 = (f32[4,128]{1,0:T(4,128)S(1)}, f32[4,128]{1,0:T(4,128)S(1)}, u32[]{:S(2)}, u32[]{:S(2)}) collective-permute-start(f32[4,128]{1,0:T(4,128)S(1)} %add_add_fusion.1), channel_id=1, source_target_pairs={{0,128},{1,129},{2,130},{3,131},{4,132},{5,133},{6,134},{7,135},{8... | collective-permute-start | bytes 6152 | tf_op jit(solution)/shard_map/ppermute | solution.py:183
  310.4 9.4 %collective-permute-start.14 = (f32[4,128]{1,0:T(4,128)S(1)}, f32[4,128]{1,0:T(4,128)S(1)}, u32[]{:S(2)}, u32[]{:S(2)}) collective-permute-start(f32[4,128]{1,0:T(4,128)S(1)} %add_add_fusion.1), channel_id=1, source_target_pairs={{0,64},{1,65},{2,66},{3,67},{4,68},{5,69},{6,70},{7,71},{8,72},{9,... | collective-permute-start | bytes 6152 | tf_op jit(solution)/shard_map/ppermute | solution.py:183

commit v2 on v1

--- a/solution.py
+++ b/solution.py
@@ -88,19 +88,21 @@
 
     by_rows = (((1,), (1,)), ((), ()))
 
-    @pl.loop(0, blocks)
-    def _queries(b):
+    def forward(b, held):
         raw = load(b, 0, in_txt).astype(F32)
         gain = gain_rows(0)
         qn = (raw * inverse_rms(raw) * gain).astype(BF16)
-        cot = load(b, in_cot, in_cot + img)
         summed = jnp.zeros((block, 2 * head), F32)
         for start in range(0, full, tile):
             keys = slice(start, start + tile)
             scores = lax.dot_general(qn, kn_ref[keys, :], by_rows, preferred_element_type=F32)
             expo = jnp.exp2(scores * to_exp2).astype(BF16)
-            eb_ref[:, keys] = expo
+            held[:, keys] = expo
             summed += jnp.dot(expo, vaug_ref[keys, :], preferred_element_type=F32)
+        return raw, gain, qn, summed
+
+    def backward(b, held, raw, gain, qn, summed):
+        cot = load(b, in_cot, in_cot + img)
         per_total = 1.0 / summed[:, head:]
         out = summed[:, :head] * per_total
         store(b, 0, img, out.astype(BF16))
@@ -111,7 +113,7 @@
         dq = jnp.zeros((block, head), F32)
         for start in range(0, full, tile):
             keys = slice(start, start + tile)
-            expo = eb_ref[:, keys]
+            expo = held[:, keys]
             dprobs = lax.dot_general(
                 cot, vaug_ref[keys, :head], by_rows, preferred_element_type=F32
             )
@@ -122,6 +124,13 @@
         grad, terms = norm_backward(raw, gain, dq * (per_total * scale))
         store(b, out_img, out_txt, grad.astype(BF16))
         add_terms(0, terms)
+
+    @pl.loop(0, blocks, step=2)
+    def _queries(b):
+        first = forward(b, eb_ref.at[0])
+        second = forward(b + 1, eb_ref.at[1])
+        backward(b, eb_ref.at[0], *first)
+        backward(b + 1, eb_ref.at[1], *second)
 
     @pl.loop(0, blocks)
     def _key_grads(b):
@@ -158,7 +167,7 @@
         scratch_shapes=[
             pltpu.VMEM((full, head), BF16),
             pltpu.VMEM((full, 2 * head), BF16),
-            pltpu.VMEM((block, full), BF16),
+            pltpu.VMEM((2, block, full), BF16),
             pltpu.VMEM((head, full), F32),
             pltpu.VMEM((head, full), F32),
         ],
@@ -176,15 +185,8 @@
     count = math.prod(lax.axis_size(axis) for axis in axes)
     step = 1
     while step < count:
-        radix = min(8, count // step)
-        parts = [term]
-        for other in range(1, radix):
-            perm = [(i, i ^ (other * step)) for i in range(count)]
-            parts.append(lax.ppermute(term, axes, perm))
-        while len(parts) > 1:
-            parts = [parts[i] + parts[i + 1] for i in range(0, len(parts), 2)]
-        term = parts[0]
-        step *= radix
+        term = term + lax.ppermute(term, axes, [(i, i ^ step) for i in range(count)])
+        step *= 2
     return term
 
 

time: 324 us -> 283 us (0.87)
  starting transfers between devices: 166 us -> 106 us
  waiting for transfers between devices: 126 us -> 148 us
  Pallas kernels: 23 us -> 19.1 us
    ppermute x21 -> x9, starting transfers between devices: 143 us -> 83.3 us  [sum_everywhere(): lax.ppermute(term, axes, [(i, i ^ step) for i in range(count)])]
    ppermute x21 -> x9, waiting for transfers between devices: 31.2 us -> 53.2 us  [sum_everywhere(): lax.ppermute(term, axes, [(i, i ^ step) for i in range(count)])]
    pallas_call x1, Pallas kernels: 23 us -> 19.1 us  [attend_pair(): pl.pallas_call(functools.partial(pair_kernel, img, txt), out_shape=(jax.S...]
  transfers between devices with their start and end apart: 23 -> 11, of which waited for: 5 -> 10; matrix products, arithmetic and copies ran while one was open for 0% -> 0% of each run, Pallas kernels for 0% -> 0%
where the time goes in v2:
time: 283 us; the launch traced here: 281 us
  waiting for transfers between devices  148 us (52%)
  starting transfers between devices  106 us (37%)
  Pallas kernels  19.1 us (7%)
  other arithmetic  3.77 us (1%)
  local copies, waits for them, and re-layouts  3.31 us (1%)
    all_to_all x1, waiting for transfers between devices, per_device(): lax.all_to_all(outgoing, 'seq', split_axis=0, concat_axis=0, tiled=True)  95.2 us
    ppermute x9, starting transfers between devices, sum_everywhere(): lax.ppermute(term, axes, [(i, i ^ step) for i in range(count)])  83.3 us
    ppermute x9, waiting for transfers between devices, sum_everywhere(): lax.ppermute(term, axes, [(i, i ^ step) for i in range(count)])  53.2 us
    pallas_call x1, Pallas kernels, attend_pair(): pl.pallas_call(functools.partial(pair_kernel, img, txt), out_shape=(jax.S...  19.1 us
    all_to_all x1, starting transfers between devices, per_device(): lax.all_to_all(outgoing, 'seq', split_axis=0, concat_axis=0, tiled=True)  15.5 us
    all_to_all x1, starting transfers between devices, per_device(): lax.all_to_all(results, 'seq', split_axis=0, concat_axis=0, tiled=True)  7.4 us
  transfers between devices with their start and end apart: 11, of which 10 were waited for; matrix products, arithmetic and copies ran while one was open for 0% of the time, Pallas kernels for 0%

profile of v2, /device:TPU:24, one launch (start us, length us, event | category | flops | bytes accessed | tf_op | source)
XLA Modules:
  0.0 281.5 jit_solution(3028833642184390735)
XLA Ops:
  0.6 3.2 %pad_maximum_fusion = bf16[32,256,128]{2,1,0:T(8,128)(2,1)} fusion(bf16[32,16,128]{2,1,0:T(8,128)(2,1)} %bitcast.14, bf16[32,48,128]{2,1,0:T(8,128)(2,1)} %bitcast.10, bf16[32,48,128]{2,1,0:T(8,128)(2,1)} %bitcast.11, bf16[32,144,128]{2,1,0:T(8,128)(2,1)} %bitcast.9), kind=kLoop, calls=%fused_computation | loop fusion | flops 8388608 | bytes 4194304 | tf_op jit(solution)/shard_map/concatenate | solution.py:199
  3.8 0.0 copy-start.1
  3.8 0.0 copy-start
  3.8 15.5 %all-to-all-start = ((bf16[32,256,128]{2,1,0:T(8,128)(2,1)}), bf16[32,256,128]{2,1,0:T(8,128)(2,1)S(1)}, u32[]{:S(2)}, u32[]{:S(2)}) async-start(bf16[32,256,128]{2,1,0:T(8,128)(2,1)} %pad_maximum_fusion), calls=%async_computation | async-start | bytes 4194304 | tf_op jit(solution)/shard_map/all_to_all | solution.py:208
  19.3 0.0 copy-done.1
  19.3 0.6 dynamic_slice.3.length_ref
  19.9 95.2 %all-to-all-done.in_ref = bf16[32,256,128]{2,1,0:T(8,128)(2,1)S(1)} async-done(((bf16[32,256,128]{2,1,0:T(8,128)(2,1)}), bf16[32,256,128]{2,1,0:T(8,128)(2,1)S(1)}, u32[]{:S(2)}, u32[]{:S(2)}) %all-to-all-start) | async-done | bytes 2097184 | tf_op jit(solution)/shard_map/all_to_all | solution.py:208
  115.1 0.0 copy-done
  115.1 19.1 %attend_pair.1 = (bf16[32,256,128]{2,1,0:T(8,128)(2,1)}, f32[4,128]{1,0:T(4,128)S(1)}) custom-call(s32[1]{0:T(128)} %dynamic_slice.3.length_ref, f32[4,128]{1,0:T(4,128)S(1)} %copy-done, bf16[32,256,128]{2,1,0:T(8,128)(2,1)S(1)} %all-to-all-done.in_ref), custom_call_target="tpu_custom_call" | custom-call | flops 6442450944 | bytes 4194304 | tf_op jit(solution)/shard_map/attend_pair/pallas_call | solution.py:152
  134.2 7.4 %all-to-all-start.1 = ((bf16[32,256,128]{2,1,0:T(8,128)(2,1)}), bf16[32,256,128]{2,1,0:T(8,128)(2,1)S(1)}, u32[]{:S(2)}, u32[]{:S(2)}) async-start(bf16[32,256,128]{2,1,0:T(8,128)(2,1)} %get-tuple-element.7), calls=%async_computation.1 | async-start | bytes 4194304 | tf_op jit(solution)/shard_map/all_to_all | solution.py:212
  141.6 1.9 collective-permute-start
  143.5 1.1 collective-permute-done
  144.7 8.2 %collective-permute-start.1 = (f32[4,128]{1,0:T(4,128)S(1)}, f32[4,128]{1,0:T(4,128)S(1)}, u32[]{:S(2)}, u32[]{:S(2)}) collective-permute-start(f32[4,128]{1,0:T(4,128)S(1)} %add.32), channel_id=1, source_target_pairs={{0,2},{1,3},{2,0},{3,1},{4,6},{5,7},{6,4},{7,5},{8,10},{9,11},{10,... | collective-permute-start | bytes 6152 | tf_op jit(solution)/shard_map/ppermute | solution.py:188
  152.9 34.7 %collective-permute-done.1 = f32[4,128]{1,0:T(4,128)S(1)} collective-permute-done((f32[4,128]{1,0:T(4,128)S(1)}, f32[4,128]{1,0:T(4,128)S(1)}, u32[]{:S(2)}, u32[]{:S(2)}) %collective-permute-start.1) | collective-permute-done | bytes 2080 | tf_op jit(solution)/shard_map/ppermute | solution.py:188
  187.5 3.6 %collective-permute-start.2 = (f32[4,128]{1,0:T(4,128)S(1)}, f32[4,128]{1,0:T(4,128)S(1)}, u32[]{:S(2)}, u32[]{:S(2)}) collective-permute-start(f32[4,128]{1,0:T(4,128)S(1)} %add.33), channel_id=1, source_target_pairs={{0,4},{1,5},{2,6},{3,7},{4,0},{5,1},{6,2},{7,3},{8,12},{9,13},{10,... | collective-permute-start | bytes 6152 | tf_op jit(solution)/shard_map/ppermute | solution.py:188
  191.2 1.8 collective-permute-done.2
  193.0 5.2 %collective-permute-start.3 = (f32[4,128]{1,0:T(4,128)S(1)}, f32[4,128]{1,0:T(4,128)S(1)}, u32[]{:S(2)}, u32[]{:S(2)}) collective-permute-start(f32[4,128]{1,0:T(4,128)S(1)} %add.34), channel_id=1, source_target_pairs={{0,8},{1,9},{2,10},{3,11},{4,12},{5,13},{6,14},{7,15},{8,0},{9,1},... | collective-permute-start | bytes 6152 | tf_op jit(solution)/shard_map/ppermute | solution.py:188
  198.2 1.8 collective-permute-done.3
  200.0 1.9 collective-permute-start.4
  201.9 3.6 %collective-permute-done.4 = f32[4,128]{1,0:T(4,128)S(1)} collective-permute-done((f32[4,128]{1,0:T(4,128)S(1)}, f32[4,128]{1,0:T(4,128)S(1)}, u32[]{:S(2)}, u32[]{:S(2)}) %collective-permute-start.4) | collective-permute-done | bytes 2080 | tf_op jit(solution)/shard_map/ppermute | solution.py:188
  205.5 49.3 %collective-permute-start.5 = (f32[4,128]{1,0:T(4,128)S(1)}, f32[4,128]{1,0:T(4,128)S(1)}, u32[]{:S(2)}, u32[]{:S(2)}) collective-permute-start(f32[4,128]{1,0:T(4,128)S(1)} %add.36), channel_id=1, source_target_pairs={{0,32},{1,33},{2,34},{3,35},{4,36},{5,37},{6,38},{7,39},{8,40},{9,... | collective-permute-start | bytes 6152 | tf_op jit(solution)/shard_map/ppermute | solution.py:188
  254.8 1.5 collective-permute-done.5
  256.3 7.3 %collective-permute-start.6 = (f32[4,128]{1,0:T(4,128)S(1)}, f32[4,128]{1,0:T(4,128)S(1)}, u32[]{:S(2)}, u32[]{:S(2)}) collective-permute-start(f32[4,128]{1,0:T(4,128)S(1)} %add.37), channel_id=1, source_target_pairs={{0,64},{1,65},{2,66},{3,67},{4,68},{5,69},{6,70},{7,71},{8,72},{9,... | collective-permute-start | bytes 6152 | tf_op jit(solution)/shard_map/ppermute | solution.py:188
  263.7 2.0 collective-permute-done.6
  265.7 2.6 collective-permute-start.7
  268.4 2.8 %collective-permute-done.7 = f32[4,128]{1,0:T(4,128)S(1)} collective-permute-done((f32[4,128]{1,0:T(4,128)S(1)}, f32[4,128]{1,0:T(4,128)S(1)}, u32[]{:S(2)}, u32[]{:S(2)}) %collective-permute-start.7) | collective-permute-done | bytes 2080 | tf_op jit(solution)/shard_map/ppermute | solution.py:188
  271.2 3.1 %collective-permute-start.8 = (f32[4,128]{1,0:T(4,128)S(1)}, f32[4,128]{1,0:T(4,128)S(1)}, u32[]{:S(2)}, u32[]{:S(2)}) collective-permute-start(f32[4,128]{1,0:T(4,128)S(1)} %add.39), channel_id=1, source_target_pairs={{0,256},{1,257},{2,258},{3,259},{4,260},{5,261},{6,262},{7,263},{8... | collective-permute-start | bytes 6152 | tf_op jit(solution)/shard_map/ppermute | solution.py:188
  274.3 3.8 %collective-permute-done.8 = f32[4,128]{1,0:T(4,128)S(1)} collective-permute-done((f32[4,128]{1,0:T(4,128)S(1)}, f32[4,128]{1,0:T(4,128)S(1)}, u32[]{:S(2)}, u32[]{:S(2)}) %collective-permute-start.8) | collective-permute-done | bytes 2080 | tf_op jit(solution)/shard_map/ppermute | solution.py:188
  278.2 0.6 add.40
  278.7 0.0 all-to-all-done.1
  278.7 0.7 slice.17
  279.4 0.9 fusion
  280.4 1.1 slice.18
  (8 shorter events, 0.0 us)
Async XLA Ops:
  3.8 15.5 %copy-start.1 = (s32[2]{0:T(128)S(1)}, s32[2]{0:T(128)}, u32[]{:S(2)}) copy-start(s32[2]{0:T(128)} %param.10) | copy-start | bytes 28
  3.8 111.3 %copy-start = (f32[4,128]{1,0:T(4,128)S(1)}, f32[4,128]{1,0:T(4,128)}, u32[]{:S(2)}) copy-start(f32[4,128]{1,0:T(4,128)} %gains_ref.1) | copy-start | bytes 6148
  3.8 111.3 %all-to-all-start = ((bf16[32,256,128]{2,1,0:T(8,128)(2,1)}), bf16[32,256,128]{2,1,0:T(8,128)(2,1)S(1)}, u32[]{:S(2)}, u32[]{:S(2)}) async-start(bf16[32,256,128]{2,1,0:T(8,128)(2,1)} %pad_maximum_fusion), calls=%async_computation | async-start | bytes 4194304 | tf_op jit(solution)/shard_map/all_to_all | solution.py:208
  134.2 144.6 %all-to-all-start.1 = ((bf16[32,256,128]{2,1,0:T(8,128)(2,1)}), bf16[32,256,128]{2,1,0:T(8,128)(2,1)S(1)}, u32[]{:S(2)}, u32[]{:S(2)}) async-start(bf16[32,256,128]{2,1,0:T(8,128)(2,1)} %get-tuple-element.7), calls=%async_computation.1 | async-start | bytes 4194304 | tf_op jit(solution)/shard_map/all_to_all | solution.py:212
  141.6 3.1 %collective-permute-start = (f32[4,128]{1,0:T(4,128)S(1)}, f32[4,128]{1,0:T(4,128)S(1)}, u32[]{:S(2)}, u32[]{:S(2)}) collective-permute-start(f32[4,128]{1,0:T(4,128)S(1)} %get-tuple-element.8), channel_id=1, source_target_pairs={{0,1},{1,0},{2,3},{3,2},{4,5},{5,4},{6,7},{7,6},{8,9},{9,8},{10,11... | collective-permute-start | bytes 6152 | tf_op jit(solution)/shard_map/ppermute | solution.py:188
  144.7 42.9 %collective-permute-start.1 = (f32[4,128]{1,0:T(4,128)S(1)}, f32[4,128]{1,0:T(4,128)S(1)}, u32[]{:S(2)}, u32[]{:S(2)}) collective-permute-start(f32[4,128]{1,0:T(4,128)S(1)} %add.32), channel_id=1, source_target_pairs={{0,2},{1,3},{2,0},{3,1},{4,6},{5,7},{6,4},{7,5},{8,10},{9,11},{10,... | collective-permute-start | bytes 6152 | tf_op jit(solution)/shard_map/ppermute | solution.py:188
  187.5 5.5 %collective-permute-start.2 = (f32[4,128]{1,0:T(4,128)S(1)}, f32[4,128]{1,0:T(4,128)S(1)}, u32[]{:S(2)}, u32[]{:S(2)}) collective-permute-start(f32[4,128]{1,0:T(4,128)S(1)} %add.33), channel_id=1, source_target_pairs={{0,4},{1,5},{2,6},{3,7},{4,0},{5,1},{6,2},{7,3},{8,12},{9,13},{10,... | collective-permute-start | bytes 6152 | tf_op jit(solution)/shard_map/ppermute | solution.py:188
  193.0 7.0 %collective-permute-start.3 = (f32[4,128]{1,0:T(4,128)S(1)}, f32[4,128]{1,0:T(4,128)S(1)}, u32[]{:S(2)}, u32[]{:S(2)}) collective-permute-start(f32[4,128]{1,0:T(4,128)S(1)} %add.34), channel_id=1, source_target_pairs={{0,8},{1,9},{2,10},{3,11},{4,12},{5,13},{6,14},{7,15},{8,0},{9,1},... | collective-permute-start | bytes 6152 | tf_op jit(solution)/shard_map/ppermute | solution.py:188
  200.0 5.5 %collective-permute-start.4 = (f32[4,128]{1,0:T(4,128)S(1)}, f32[4,128]{1,0:T(4,128)S(1)}, u32[]{:S(2)}, u32[]{:S(2)}) collective-permute-start(f32[4,128]{1,0:T(4,128)S(1)} %add.35), channel_id=1, source_target_pairs={{0,16},{1,17},{2,18},{3,19},{4,20},{5,21},{6,22},{7,23},{8,24},{9,... | collective-permute-start | bytes 6152 | tf_op jit(solution)/shard_map/ppermute | solution.py:188
  205.5 50.9 %collective-permute-start.5 = (f32[4,128]{1,0:T(4,128)S(1)}, f32[4,128]{1,0:T(4,128)S(1)}, u32[]{:S(2)}, u32[]{:S(2)}) collective-permute-start(f32[4,128]{1,0:T(4,128)S(1)} %add.36), channel_id=1, source_target_pairs={{0,32},{1,33},{2,34},{3,35},{4,36},{5,37},{6,38},{7,39},{8,40},{9,... | collective-permute-start | bytes 6152 | tf_op jit(solution)/shard_map/ppermute | solution.py:188
  256.3 9.4 %collective-permute-start.6 = (f32[4,128]{1,0:T(4,128)S(1)}, f32[4,128]{1,0:T(4,128)S(1)}, u32[]{:S(2)}, u32[]{:S(2)}) collective-permute-start(f32[4,128]{1,0:T(4,128)S(1)} %add.37), channel_id=1, source_target_pairs={{0,64},{1,65},{2,66},{3,67},{4,68},{5,69},{6,70},{7,71},{8,72},{9,... | collective-permute-start | bytes 6152 | tf_op jit(solution)/shard_map/ppermute | solution.py:188
  265.7 5.5 %collective-permute-start.7 = (f32[4,128]{1,0:T(4,128)S(1)}, f32[4,128]{1,0:T(4,128)S(1)}, u32[]{:S(2)}, u32[]{:S(2)}) collective-permute-start(f32[4,128]{1,0:T(4,128)S(1)} %add.38), channel_id=1, source_target_pairs={{0,128},{1,129},{2,130},{3,131},{4,132},{5,133},{6,134},{7,135},{8... | collective-permute-start | bytes 6152 | tf_op jit(solution)/shard_map/ppermute | solution.py:188
  271.2 7.0 %collective-permute-start.8 = (f32[4,128]{1,0:T(4,128)S(1)}, f32[4,128]{1,0:T(4,128)S(1)}, u32[]{:S(2)}, u32[]{:S(2)}) collective-permute-start(f32[4,128]{1,0:T(4,128)S(1)} %add.39), channel_id=1, source_target_pairs={{0,256},{1,257},{2,258},{3,259},{4,260},{5,261},{6,262},{7,263},{8... | collective-permute-start | bytes 6152 | tf_op jit(solution)/shard_map/ppermute | solution.py:188

commit v3 on v2

--- a/solution.py
+++ b/solution.py
@@ -181,15 +181,6 @@
     )(length, gains, arrived)
 
 
-def sum_everywhere(term, axes):
-    count = math.prod(lax.axis_size(axis) for axis in axes)
-    step = 1
-    while step < count:
-        term = term + lax.ppermute(term, axes, [(i, i ^ step) for i in range(count)])
-        step *= 2
-    return term
-
-
 def per_device(img_qkv, txt_qkv, img_cot, txt_cot, lengths, norm_gains):
     samples, heads, _, img, head = img_qkv.shape
     txt = txt_qkv.shape[3]
@@ -210,7 +201,7 @@
     length = lax.dynamic_slice_in_dim(lengths, sample, 1, 0)
     results, terms = attend_pair(arrived, length, norm_gains, img, txt)
     back = lax.all_to_all(results, "seq", split_axis=0, concat_axis=0, tiled=True)
-    gain_grad = sum_everywhere(terms, ("grp", "seq", "dp"))
+    gain_grad = jnp.sum(lax.all_gather(terms, ("grp", "seq", "dp")), axis=0)
     own = img + txt
     img_out = back[:, :img].reshape(samples, heads, img, head)
     txt_out = back[:, img:own].reshape(samples, heads, txt, head)

time: 283 us -> 939 us (3.32)
  waiting for transfers between devices: 148 us -> 869 us
  starting transfers between devices: 106 us -> 23 us
  between operations: 0.76 us -> 14.1 us
    all_gather x0 -> x1, waiting for transfers between devices: none -> 773 us  [per_device(): gain_grad = jnp.sum(lax.all_gather(terms, ('grp', 'seq', 'dp')), axis=0)]
    ppermute x9 -> x0, starting transfers between devices: 83.3 us -> none  [sum_everywhere(): lax.ppermute(term, axes, [(i, i ^ step) for i in range(count)])]
    ppermute x9 -> x0, waiting for transfers between devices: 53.2 us -> none  [sum_everywhere(): lax.ppermute(term, axes, [(i, i ^ step) for i in range(count)])]
  transfers between devices with their start and end apart: 11 -> 3, of which waited for: 10 -> 2; matrix products, arithmetic and copies ran while one was open for 0% -> 0% of each run, Pallas kernels for 0% -> 0%
where the time goes in v3:
time: 939 us; the launch traced here: 934 us
  waiting for transfers between devices  869 us (93%)
  starting transfers between devices  23 us (2%)
  Pallas kernels  18.3 us (2%)
  between operations  14.1 us (2%)
    all_gather x1, waiting for transfers between devices, per_device(): gain_grad = jnp.sum(lax.all_gather(terms, ('grp', 'seq', 'dp')), axis=0)  773 us
    all_to_all x1, waiting for transfers between devices, per_device(): lax.all_to_all(outgoing, 'seq', split_axis=0, concat_axis=0, tiled=True)  95.2 us
  transfers between devices with their start and end apart: 3, of which 2 were waited for; matrix products, arithmetic and copies ran while one was open for 0% of the time, Pallas kernels for 0%

profile of v3, /device:TPU:24, one launch (start us, length us, event | category | flops | bytes accessed | tf_op | source)
XLA Modules:
  0.0 934.4 jit_solution(618436075423030833)
XLA Ops:
  7.2 3.2 pad_maximum_fusion
  10.3 0.0 copy-start.2
  10.3 0.0 copy-start.1
  10.3 15.5 %all-to-all-start = ((bf16[32,256,128]{2,1,0:T(8,128)(2,1)}), bf16[32,256,128]{2,1,0:T(8,128)(2,1)S(1)}, u32[]{:S(2)}, u32[]{:S(2)}) async-start(bf16[32,256,128]{2,1,0:T(8,128)(2,1)} %pad_maximum_fusion), calls=%async_computation | async-start | bytes 4194304 | tf_op jit(solution)/shard_map/all_to_all | solution.py:199
  25.9 0.0 copy-done.2
  25.9 0.6 dynamic_slice.3.length_ref
  26.5 95.2 %all-to-all-done.in_ref = bf16[32,256,128]{2,1,0:T(8,128)(2,1)S(1)} async-done(((bf16[32,256,128]{2,1,0:T(8,128)(2,1)}), bf16[32,256,128]{2,1,0:T(8,128)(2,1)S(1)}, u32[]{:S(2)}, u32[]{:S(2)}) %all-to-all-start) | async-done | bytes 2097184 | tf_op jit(solution)/shard_map/all_to_all | solution.py:199
  121.7 0.0 copy-done.1
  121.7 18.3 %attend_pair.1 = (bf16[32,256,128]{2,1,0:T(8,128)(2,1)S(1)}, f32[4,128]{1,0:T(4,128)}) custom-call(s32[1]{0:T(128)} %dynamic_slice.3.length_ref, f32[4,128]{1,0:T(4,128)S(1)} %copy-done.1, bf16[32,256,128]{2,1,0:T(8,128)(2,1)S(1)} %all-to-all-done.in_ref), custom_call_target="tpu_custom_call" | custom-call | flops 6442450944 | bytes 4194304 | tf_op jit(solution)/shard_map/attend_pair/pallas_call | solution.py:152
  139.9 0.0 copy-start
  139.9 1.3 copy-done
  141.3 7.4 all-to-all-start.1
  148.7 0.0 all-gather.4.cloned.1.call-start
  148.7 0.7 all-gather.4.cloned.1.call-update
  149.4 773.0 %all-gather.4.cloned.1.call-done = f32[512,4,128]{2,1,0:T(4,128)} async-done(((f32[1,4,128]{2,1,0:T(4,128)}), f32[512,4,128]{2,1,0:T(4,128)}) %all-gather.4.cloned.1.call-update) | async-done | bytes 1048592 | tf_op jit(solution)/shard_map/all_gather | solution.py:204
  922.5 2.3 reduce_sum.9
  924.8 0.0 all-to-all-done.1
  924.8 0.7 slice.17
  925.5 0.9 fusion
  926.4 1.1 slice.18
Async XLA Ops:
  10.3 15.5 %copy-start.2 = (s32[2]{0:T(128)S(1)}, s32[2]{0:T(128)}, u32[]{:S(2)}) copy-start(s32[2]{0:T(128)} %param.10) | copy-start | bytes 28
  10.3 111.3 %copy-start.1 = (f32[4,128]{1,0:T(4,128)S(1)}, f32[4,128]{1,0:T(4,128)}, u32[]{:S(2)}) copy-start(f32[4,128]{1,0:T(4,128)} %gains_ref.1) | copy-start | bytes 6148
  10.3 111.3 %all-to-all-start = ((bf16[32,256,128]{2,1,0:T(8,128)(2,1)}), bf16[32,256,128]{2,1,0:T(8,128)(2,1)S(1)}, u32[]{:S(2)}, u32[]{:S(2)}) async-start(bf16[32,256,128]{2,1,0:T(8,128)(2,1)} %pad_maximum_fusion), calls=%async_computation | async-start | bytes 4194304 | tf_op jit(solution)/shard_map/all_to_all | solution.py:199
  139.9 1.3 copy-start
  141.3 783.5 %all-to-all-start.1 = ((bf16[32,256,128]{2,1,0:T(8,128)(2,1)}), bf16[32,256,128]{2,1,0:T(8,128)(2,1)S(1)}, u32[]{:S(2)}, u32[]{:S(2)}) async-start(bf16[32,256,128]{2,1,0:T(8,128)(2,1)} %copy-done), calls=%async_computation.1 | async-start | bytes 4194304 | tf_op jit(solution)/shard_map/all_to_all | solution.py:203
  148.7 773.8 %all-gather.4.cloned.1.call-start = ((), (), s32[]{:S(2)}) async-start(), calls=%async_computation.2 | async-start | bytes 1050624 | tf_op jit(solution)/shard_map/all_gather | solution.py:204
Sparse Core Ops, SparseCore 0:
  152.2 770.2 all-gather.3

commit v4 on v3

--- a/solution.py
+++ b/solution.py
@@ -11,7 +11,7 @@
 F32 = jnp.float32
 BF16 = jnp.bfloat16
 EPS = 1e-06
-GROUP = 4
+GROUP = 8
 KEY_TILE = 512
 
 
@@ -75,9 +75,8 @@
     dkt_ref[...] = jnp.zeros_like(dkt_ref)
     dvt_ref[...] = jnp.zeros_like(dvt_ref)
 
-    @pl.loop(0, blocks)
-    def _keys(b):
-        at = pl.ds(pl.multiple_of(b * block, block), block)
+    for b in range(blocks):
+        at = slice(b * block, (b + 1) * block)
         live = live_rows(b)
         raw = load(b, img, in_txt + txt).astype(F32)
         normed = raw * inverse_rms(raw) * gain_rows(1)
@@ -117,7 +116,7 @@
             dprobs = lax.dot_general(
                 cot, vaug_ref[keys, :head], by_rows, preferred_element_type=F32
             )
-            dscores = (expo.astype(F32) * (dprobs - delta)).astype(BF16)
+            dscores = expo * (dprobs - delta).astype(BF16)
             dq += jnp.dot(dscores, kn_ref[keys, :], preferred_element_type=F32)
             dkt_ref[:, keys] += jnp.dot(qn_t, dscores, preferred_element_type=F32)
             dvt_ref[:, keys] += jnp.dot(cot_t, expo, preferred_element_type=F32)
@@ -179,6 +178,17 @@
         ),
         name="attend_pair",
     )(length, gains, arrived)
+
+
+def sum_pairwise(term, axis, steps):
+    count = lax.axis_size(axis)
+    for step in steps:
+        term = term + lax.ppermute(term, axis, [(i, i ^ step) for i in range(count)])
+    return term
+
+
+def powers_of_two(count):
+    return [1 << bit for bit in range(count.bit_length() - 1)]
 
 
 def per_device(img_qkv, txt_qkv, img_cot, txt_cot, lengths, norm_gains):
@@ -201,7 +211,12 @@
     length = lax.dynamic_slice_in_dim(lengths, sample, 1, 0)
     results, terms = attend_pair(arrived, length, norm_gains, img, txt)
     back = lax.all_to_all(results, "seq", split_axis=0, concat_axis=0, tiled=True)
-    gain_grad = jnp.sum(lax.all_gather(terms, ("grp", "seq", "dp")), axis=0)
+    for axis in ("grp", "dp"):
+        terms = sum_pairwise(terms, axis, powers_of_two(lax.axis_size(axis)))
+    back, terms = lax.optimization_barrier((back, terms))
+    copies = jnp.broadcast_to(terms[None], (devices,) + terms.shape)
+    group_terms = lax.all_to_all(copies, "seq", split_axis=0, concat_axis=0, tiled=True)
+    gain_grad = jnp.sum(group_terms, axis=0)
     own = img + txt
     img_out = back[:, :img].reshape(samples, heads, img, head)
     txt_out = back[:, img:own].reshape(samples, heads, txt, head)

time: 939 us -> 258 us (0.27)
  waiting for transfers between devices: 869 us -> 187 us
  starting transfers between devices: 23 us -> 46.2 us
  between operations: 14.1 us -> 0.74 us
    all_gather x1 -> x0, waiting for transfers between devices: 773 us -> none  [per_device(): gain_grad = jnp.sum(lax.all_gather(terms, ('grp', 'seq', 'dp')), axis=0)]
    all_to_all x1, waiting for transfers between devices: 0.01 us -> 49.7 us  [per_device(): lax.all_to_all(results, 'seq', split_axis=0, concat_axis=0, tiled=True)]
    ppermute x0 -> x4, waiting for transfers between devices: none -> 30 us  [sum_pairwise(): lax.ppermute(term, axis, [(i, i ^ step) for i in range(count)])]
    ppermute x0 -> x4, starting transfers between devices: none -> 15.9 us  [sum_pairwise(): lax.ppermute(term, axis, [(i, i ^ step) for i in range(count)])]
    all_to_all x0 -> x1, waiting for transfers between devices: none -> 11.9 us  [per_device(): lax.all_to_all(copies, 'seq', split_axis=0, concat_axis=0, tiled=True)]
  transfers between devices with their start and end apart: 3 -> 7, of which waited for: 2 -> 7; matrix products, arithmetic and copies ran while one was open for 0% -> 1% of each run, Pallas kernels for 0% -> 0%
where the time goes in v4:
time: 258 us; the launch traced here: 257 us
  waiting for transfers between devices  187 us (72%)
  starting transfers between devices  46.2 us (18%)
  Pallas kernels  14.5 us (6%)
  local copies, waits for them, and re-layouts  5.28 us (2%)
  other arithmetic  3.8 us (1%)
    all_to_all x1, waiting for transfers between devices, per_device(): lax.all_to_all(outgoing, 'seq', split_axis=0, concat_axis=0, tiled=True)  95.2 us
    all_to_all x1, waiting for transfers between devices, per_device(): lax.all_to_all(results, 'seq', split_axis=0, concat_axis=0, tiled=True)  49.7 us
    ppermute x4, waiting for transfers between devices, sum_pairwise(): lax.ppermute(term, axis, [(i, i ^ step) for i in range(count)])  30 us
    ppermute x4, starting transfers between devices, sum_pairwise(): lax.ppermute(term, axis, [(i, i ^ step) for i in range(count)])  15.9 us
    all_to_all x1, starting transfers between devices, per_device(): lax.all_to_all(outgoing, 'seq', split_axis=0, concat_axis=0, tiled=True)  15.5 us
    pallas_call x1, Pallas kernels, attend_pair(): pl.pallas_call(functools.partial(pair_kernel, img, txt), out_shape=(jax.S...  14.5 us
    all_to_all x1, waiting for transfers between devices, per_device(): lax.all_to_all(copies, 'seq', split_axis=0, concat_axis=0, tiled=True)  11.9 us
    all_to_all x1, starting transfers between devices, per_device(): lax.all_to_all(copies, 'seq', split_axis=0, concat_axis=0, tiled=True)  7.41 us
  transfers between devices with their start and end apart: 7, of which 7 were waited for; matrix products, arithmetic and copies ran while one was open for 1% of the time, Pallas kernels for 0%

profile of v4, /device:TPU:24, one launch (start us, length us, event | category | flops | bytes accessed | tf_op | source)
XLA Modules:
  0.0 257.4 jit_solution(11029624822499173592)
XLA Ops:
  0.6 3.2 %pad_maximum_fusion = bf16[32,256,128]{2,1,0:T(8,128)(2,1)} fusion(bf16[32,16,128]{2,1,0:T(8,128)(2,1)} %bitcast.14, bf16[32,48,128]{2,1,0:T(8,128)(2,1)} %bitcast.10, bf16[32,48,128]{2,1,0:T(8,128)(2,1)} %bitcast.11, bf16[32,144,128]{2,1,0:T(8,128)(2,1)} %bitcast.9), kind=kLoop, calls=%fused_computation | loop fusion | flops 8388608 | bytes 4194304 | tf_op jit(solution)/shard_map/concatenate | solution.py:200
  3.8 0.0 copy-start.2
  3.8 0.0 copy-start.1
  3.8 15.5 %all-to-all-start = ((bf16[32,256,128]{2,1,0:T(8,128)(2,1)}), bf16[32,256,128]{2,1,0:T(8,128)(2,1)S(1)}, u32[]{:S(2)}, u32[]{:S(2)}) async-start(bf16[32,256,128]{2,1,0:T(8,128)(2,1)} %pad_maximum_fusion), calls=%async_computation | async-start | bytes 4194304 | tf_op jit(solution)/shard_map/all_to_all | solution.py:209
  19.3 0.0 copy-done.2
  19.3 0.6 dynamic_slice.3.length_ref
  19.9 95.2 %all-to-all-done.in_ref = bf16[32,256,128]{2,1,0:T(8,128)(2,1)S(1)} async-done(((bf16[32,256,128]{2,1,0:T(8,128)(2,1)}), bf16[32,256,128]{2,1,0:T(8,128)(2,1)S(1)}, u32[]{:S(2)}, u32[]{:S(2)}) %all-to-all-start) | async-done | bytes 2097184 | tf_op jit(solution)/shard_map/all_to_all | solution.py:209
  115.1 0.0 copy-done.1
  115.1 14.5 %attend_pair.1 = (bf16[32,256,128]{2,1,0:T(8,128)(2,1)S(1)}, f32[4,128]{1,0:T(4,128)S(1)}) custom-call(s32[1]{0:T(128)} %dynamic_slice.3.length_ref, f32[4,128]{1,0:T(4,128)S(1)} %copy-done.1, bf16[32,256,128]{2,1,0:T(8,128)(2,1)S(1)} %all-to-all-done.in_ref), custom_call_target="tpu_custom_call" | custom-call | flops 6442450944 | bytes 4194304 | tf_op jit(solution)/shard_map/attend_pair/pallas_call | solution.py:151
  129.7 0.0 copy-start
  129.7 1.3 copy-done
  131.0 7.4 %all-to-all-start.1 = ((bf16[32,256,128]{2,1,0:T(8,128)(2,1)}), bf16[32,256,128]{2,1,0:T(8,128)(2,1)S(1)}, u32[]{:S(2)}, u32[]{:S(2)}) async-start(bf16[32,256,128]{2,1,0:T(8,128)(2,1)} %copy-done), calls=%async_computation.1 | async-start | bytes 4194304 | tf_op jit(solution)/shard_map/all_to_all | solution.py:213
  138.4 2.7 %collective-permute-start = (f32[4,128]{1,0:T(4,128)S(1)}, f32[4,128]{1,0:T(4,128)S(1)}, u32[]{:S(2)}, u32[]{:S(2)}) collective-permute-start(f32[4,128]{1,0:T(4,128)S(1)} %get-tuple-element.10), channel_id=1, source_target_pairs={{0,128},{128,0},{256,384},{384,256},{1,129},{129,1},{257,385},{385... | collective-permute-start | bytes 6152 | tf_op jit(solution)/shard_map/ppermute | solution.py:186
  141.1 2.8 %collective-permute-done = f32[4,128]{1,0:T(4,128)S(1)} collective-permute-done((f32[4,128]{1,0:T(4,128)S(1)}, f32[4,128]{1,0:T(4,128)S(1)}, u32[]{:S(2)}, u32[]{:S(2)}) %collective-permute-start) | collective-permute-done | bytes 2080 | tf_op jit(solution)/shard_map/ppermute | solution.py:186
  143.9 3.1 %collective-permute-start.1 = (f32[4,128]{1,0:T(4,128)S(1)}, f32[4,128]{1,0:T(4,128)S(1)}, u32[]{:S(2)}, u32[]{:S(2)}) collective-permute-start(f32[4,128]{1,0:T(4,128)S(1)} %add.17), channel_id=1, source_target_pairs={{0,256},{128,384},{256,0},{384,128},{1,257},{129,385},{257,1},{385... | collective-permute-start | bytes 6152 | tf_op jit(solution)/shard_map/ppermute | solution.py:186
  147.1 3.8 %collective-permute-done.1 = f32[4,128]{1,0:T(4,128)S(1)} collective-permute-done((f32[4,128]{1,0:T(4,128)S(1)}, f32[4,128]{1,0:T(4,128)S(1)}, u32[]{:S(2)}, u32[]{:S(2)}) %collective-permute-start.1) | collective-permute-done | bytes 2080 | tf_op jit(solution)/shard_map/ppermute | solution.py:186
  150.9 1.9 collective-permute-start.2
  152.8 1.1 collective-permute-done.2
  153.9 8.2 %collective-permute-start.3 = (f32[4,128]{1,0:T(4,128)S(1)}, f32[4,128]{1,0:T(4,128)S(1)}, u32[]{:S(2)}, u32[]{:S(2)}) collective-permute-start(f32[4,128]{1,0:T(4,128)S(1)} %add.19), channel_id=1, source_target_pairs={{0,2},{1,3},{2,0},{3,1},{4,6},{5,7},{6,4},{7,5},{8,10},{9,11},{10,... | collective-permute-start | bytes 6152 | tf_op jit(solution)/shard_map/ppermute | solution.py:186
  162.1 22.2 %collective-permute-done.3 = f32[4,128]{1,0:T(4,128)S(1)} collective-permute-done((f32[4,128]{1,0:T(4,128)S(1)}, f32[4,128]{1,0:T(4,128)S(1)}, u32[]{:S(2)}, u32[]{:S(2)}) %collective-permute-start.3) | collective-permute-done | bytes 2080 | tf_op jit(solution)/shard_map/ppermute | solution.py:186
  184.4 49.7 %all-to-all-done.1 = bf16[32,256,128]{2,1,0:T(8,128)(2,1)S(1)} async-done(((bf16[32,256,128]{2,1,0:T(8,128)(2,1)}), bf16[32,256,128]{2,1,0:T(8,128)(2,1)S(1)}, u32[]{:S(2)}, u32[]{:S(2)}) %all-to-all-start.1) | async-done | bytes 2097184 | tf_op jit(solution)/shard_map/all_to_all | solution.py:213
  234.1 0.7 slice.13
  234.8 1.1 slice.14
  235.9 0.6 broadcast_in_dim.2
  236.5 7.4 %all-to-all-start.2 = ((f32[32,4,128]{2,1,0:T(4,128)}), f32[32,4,128]{2,1,0:T(4,128)S(1)}, u32[]{:S(2)}, u32[]{:S(2)}) async-start(f32[32,4,128]{2,1,0:T(4,128)} %broadcast_in_dim.2), calls=%async_computation.2 | async-start | bytes 131072 | tf_op jit(solution)/shard_map/all_to_all | solution.py:218
  243.9 0.9 fusion
  244.9 11.9 %all-to-all-done.2 = f32[32,4,128]{2,1,0:T(4,128)S(1)} async-done(((f32[32,4,128]{2,1,0:T(4,128)}), f32[32,4,128]{2,1,0:T(4,128)S(1)}, u32[]{:S(2)}, u32[]{:S(2)}) %all-to-all-start.2) | async-done | bytes 65568 | tf_op jit(solution)/shard_map/all_to_all | solution.py:218
  256.8 0.6 reduce_sum.9
  (4 shorter events, 0.0 us)
Async XLA Ops:
  3.8 15.5 %copy-start.2 = (s32[2]{0:T(128)S(1)}, s32[2]{0:T(128)}, u32[]{:S(2)}) copy-start(s32[2]{0:T(128)} %param.10) | copy-start | bytes 28
  3.8 111.3 %copy-start.1 = (f32[4,128]{1,0:T(4,128)S(1)}, f32[4,128]{1,0:T(4,128)}, u32[]{:S(2)}) copy-start(f32[4,128]{1,0:T(4,128)} %gains_ref.1) | copy-start | bytes 6148
  3.8 111.3 %all-to-all-start = ((bf16[32,256,128]{2,1,0:T(8,128)(2,1)}), bf16[32,256,128]{2,1,0:T(8,128)(2,1)S(1)}, u32[]{:S(2)}, u32[]{:S(2)}) async-start(bf16[32,256,128]{2,1,0:T(8,128)(2,1)} %pad_maximum_fusion), calls=%async_computation | async-start | bytes 4194304 | tf_op jit(solution)/shard_map/all_to_all | solution.py:209
  129.7 1.3 copy-start
  131.0 103.1 %all-to-all-start.1 = ((bf16[32,256,128]{2,1,0:T(8,128)(2,1)}), bf16[32,256,128]{2,1,0:T(8,128)(2,1)S(1)}, u32[]{:S(2)}, u32[]{:S(2)}) async-start(bf16[32,256,128]{2,1,0:T(8,128)(2,1)} %copy-done), calls=%async_computation.1 | async-start | bytes 4194304 | tf_op jit(solution)/shard_map/all_to_all | solution.py:213
  138.4 5.5 %collective-permute-start = (f32[4,128]{1,0:T(4,128)S(1)}, f32[4,128]{1,0:T(4,128)S(1)}, u32[]{:S(2)}, u32[]{:S(2)}) collective-permute-start(f32[4,128]{1,0:T(4,128)S(1)} %get-tuple-element.10), channel_id=1, source_target_pairs={{0,128},{128,0},{256,384},{384,256},{1,129},{129,1},{257,385},{385... | collective-permute-start | bytes 6152 | tf_op jit(solution)/shard_map/ppermute | solution.py:186
  143.9 7.0 %collective-permute-start.1 = (f32[4,128]{1,0:T(4,128)S(1)}, f32[4,128]{1,0:T(4,128)S(1)}, u32[]{:S(2)}, u32[]{:S(2)}) collective-permute-start(f32[4,128]{1,0:T(4,128)S(1)} %add.17), channel_id=1, source_target_pairs={{0,256},{128,384},{256,0},{384,128},{1,257},{129,385},{257,1},{385... | collective-permute-start | bytes 6152 | tf_op jit(solution)/shard_map/ppermute | solution.py:186
  150.9 3.0 %collective-permute-start.2 = (f32[4,128]{1,0:T(4,128)S(1)}, f32[4,128]{1,0:T(4,128)S(1)}, u32[]{:S(2)}, u32[]{:S(2)}) collective-permute-start(f32[4,128]{1,0:T(4,128)S(1)} %add.18), channel_id=1, source_target_pairs={{0,1},{1,0},{2,3},{3,2},{4,5},{5,4},{6,7},{7,6},{8,9},{9,8},{10,11... | collective-permute-start | bytes 6152 | tf_op jit(solution)/shard_map/ppermute | solution.py:186
  153.9 30.4 %collective-permute-start.3 = (f32[4,128]{1,0:T(4,128)S(1)}, f32[4,128]{1,0:T(4,128)S(1)}, u32[]{:S(2)}, u32[]{:S(2)}) collective-permute-start(f32[4,128]{1,0:T(4,128)S(1)} %add.19), channel_id=1, source_target_pairs={{0,2},{1,3},{2,0},{3,1},{4,6},{5,7},{6,4},{7,5},{8,10},{9,11},{10,... | collective-permute-start | bytes 6152 | tf_op jit(solution)/shard_map/ppermute | solution.py:186
  236.5 20.3 %all-to-all-start.2 = ((f32[32,4,128]{2,1,0:T(4,128)}), f32[32,4,128]{2,1,0:T(4,128)S(1)}, u32[]{:S(2)}, u32[]{:S(2)}) async-start(f32[32,4,128]{2,1,0:T(4,128)} %broadcast_in_dim.2), calls=%async_computation.2 | async-start | bytes 131072 | tf_op jit(solution)/shard_map/all_to_all | solution.py:218

commit v5 on v4

--- a/solution.py
+++ b/solution.py
@@ -13,6 +13,7 @@
 EPS = 1e-06
 GROUP = 8
 KEY_TILE = 512
+ALONG_X = 4
 
 
 def inverse_rms(values):
@@ -180,6 +181,33 @@
     )(length, gains, arrived)
 
 
+def pack_kernel(*refs):
+    *parts, out_ref, sems = refs
+    copies = []
+    at = 0
+    for i, part in enumerate(parts):
+        rows = part.shape[1]
+        copies.append(pltpu.make_async_copy(part, out_ref.at[:, at : at + rows], sems.at[i]))
+        at += rows
+    for copy in copies:
+        copy.start()
+    for copy in copies:
+        copy.wait()
+
+
+def pack_rows(*parts):
+    pairs, _, head = parts[0].shape
+    rows = sum(part.shape[1] for part in parts)
+    return pl.pallas_call(
+        pack_kernel,
+        out_shape=jax.ShapeDtypeStruct((pairs, rows, head), BF16),
+        in_specs=[pl.BlockSpec(memory_space=pl.ANY)] * len(parts),
+        out_specs=pl.BlockSpec(memory_space=pl.ANY),
+        scratch_shapes=[pltpu.SemaphoreType.DMA((len(parts),))],
+        name="pack_rows",
+    )(*parts)
+
+
 def sum_pairwise(term, axis, steps):
     count = lax.axis_size(axis)
     for step in steps:
@@ -197,14 +225,11 @@
     pairs = samples * heads
     devices = lax.axis_size("seq")
     assert pairs == devices
-    outgoing = jnp.concatenate(
-        [
-            img_qkv.reshape(pairs, 3 * img, head),
-            txt_qkv.reshape(pairs, 3 * txt, head),
-            img_cot.reshape(pairs, img, head),
-            txt_cot.reshape(pairs, txt, head),
-        ],
-        axis=1,
+    outgoing = pack_rows(
+        img_qkv.reshape(pairs, 3 * img, head),
+        txt_qkv.reshape(pairs, 3 * txt, head),
+        img_cot.reshape(pairs, img, head),
+        txt_cot.reshape(pairs, txt, head),
     )
     arrived = lax.all_to_all(outgoing, "seq", split_axis=0, concat_axis=0, tiled=True)
     sample = lax.axis_index("seq") // heads
@@ -213,10 +238,15 @@
     back = lax.all_to_all(results, "seq", split_axis=0, concat_axis=0, tiled=True)
     for axis in ("grp", "dp"):
         terms = sum_pairwise(terms, axis, powers_of_two(lax.axis_size(axis)))
-    back, terms = lax.optimization_barrier((back, terms))
-    copies = jnp.broadcast_to(terms[None], (devices,) + terms.shape)
-    group_terms = lax.all_to_all(copies, "seq", split_axis=0, concat_axis=0, tiled=True)
-    gain_grad = jnp.sum(group_terms, axis=0)
+    terms = sum_pairwise(terms, "seq", powers_of_two(ALONG_X))
+    ends = devices // ALONG_X
+    copies = jnp.broadcast_to(terms[None], (ends,) + terms.shape)
+    back, copies = lax.optimization_barrier((back, copies))
+    lines = [[x + ALONG_X * z for z in range(ends)] for x in range(ALONG_X)]
+    line_terms = lax.all_to_all(
+        copies, "seq", split_axis=0, concat_axis=0, axis_index_groups=lines, tiled=True
+    )
+    gain_grad = jnp.sum(line_terms, axis=0)
     own = img + txt
     img_out = back[:, :img].reshape(samples, heads, img, head)
     txt_out = back[:, img:own].reshape(samples, heads, txt, head)

time: 258 us -> 323 us (1.25)
  Pallas kernels: 14.5 us -> 80.5 us
  starting transfers between devices: 46.2 us -> 62.9 us
  waiting for transfers between devices: 187 us -> 174 us
    pallas_call x0 -> x1, Pallas kernels: none -> 64.7 us  [pack_rows(): pl.pallas_call(pack_kernel, out_shape=jax.ShapeDtypeStruct((pairs, rows,...]
    all_to_all x1, waiting for transfers between devices: 49.7 us -> 37.3 us  [per_device(): lax.all_to_all(results, 'seq', split_axis=0, concat_axis=0, tiled=True)]
    ppermute x4 -> x6, starting transfers between devices: 15.9 us -> 24.7 us  [sum_pairwise(): lax.ppermute(term, axis, [(i, i ^ step) for i in range(count)])]
    all_to_all x1, starting transfers between devices: 7.41 us -> 15.4 us  [per_device(): lax.all_to_all(copies, 'seq', split_axis=0, concat_axis=0, axis_index_gro...]
    all_to_all x1, waiting for transfers between devices: 11.9 us -> 7.79 us  [per_device(): lax.all_to_all(copies, 'seq', split_axis=0, concat_axis=0, axis_index_gro...]
    ppermute x4 -> x6, waiting for transfers between devices: 30 us -> 33.6 us  [sum_pairwise(): lax.ppermute(term, axis, [(i, i ^ step) for i in range(count)])]
  transfers between devices with their start and end apart: 7 -> 9, of which waited for: 7 -> 9; matrix products, arithmetic and copies ran while one was open for 1% -> 1% of each run, Pallas kernels for 0% -> 0%
where the time goes in v5:
time: 323 us
  waiting for transfers between devices  174 us (54%)
  Pallas kernels  80.5 us (25%)
  starting transfers between devices  62.9 us (19%)
  local copies, waits for them, and re-layouts  3.92 us (1%)
    all_to_all x1, waiting for transfers between devices, per_device(): lax.all_to_all(outgoing, 'seq', split_axis=0, concat_axis=0, tiled=True)  95.2 us
    pallas_call x1, Pallas kernels, pack_rows(): pl.pallas_call(pack_kernel, out_shape=jax.ShapeDtypeStruct((pairs, rows,...  64.7 us
    all_to_all x1, waiting for transfers between devices, per_device(): lax.all_to_all(results, 'seq', split_axis=0, concat_axis=0, tiled=True)  37.3 us
    ppermute x6, waiting for transfers between devices, sum_pairwise(): lax.ppermute(term, axis, [(i, i ^ step) for i in range(count)])  33.6 us
    ppermute x6, starting transfers between devices, sum_pairwise(): lax.ppermute(term, axis, [(i, i ^ step) for i in range(count)])  24.7 us
    pallas_call x1, Pallas kernels, attend_pair(): pl.pallas_call(functools.partial(pair_kernel, img, txt), out_shape=(jax.S...  15.9 us
    all_to_all x1, starting transfers between devices, per_device(): lax.all_to_all(outgoing, 'seq', split_axis=0, concat_axis=0, tiled=True)  15.4 us
    all_to_all x1, starting transfers between devices, per_device(): lax.all_to_all(copies, 'seq', split_axis=0, concat_axis=0, axis_index_gro...  15.4 us
  transfers between devices with their start and end apart: 9, of which 9 were waited for; matrix products, arithmetic and copies ran while one was open for 1% of the time, Pallas kernels for 0%

profile of v5, /device:TPU:24, one launch (start us, length us, event | category | flops | bytes accessed | tf_op | source)
XLA Modules:
  0.0 322.6 jit_solution(4298378131314722709)
XLA Ops:
  0.6 64.7 %pack_rows.1 = bf16[32,256,128]{2,1,0:T(8,128)(2,1)} custom-call(bf16[32,144,128]{2,1,0:T(8,128)(2,1)} %bitcast.9, bf16[32,48,128]{2,1,0:T(8,128)(2,1)} %bitcast.10, bf16[32,48,128]{2,1,0:T(8,128)(2,1)} %bitcast.11, bf16[32,16,128]{2,1,0:T(8,128)(2,1)} %bitcast.14), custom_call_target="tpu_custom_call" | custom-call | tf_op jit(solution)/shard_map/pack_rows/pallas_call | solution.py:201
  65.3 0.0 copy-start.1
  65.3 0.0 copy-start
  65.3 15.4 %all-to-all-start = ((bf16[32,256,128]{2,1,0:T(8,128)(2,1)}), bf16[32,256,128]{2,1,0:T(8,128)(2,1)S(1)}, u32[]{:S(2)}, u32[]{:S(2)}) async-start(bf16[32,256,128]{2,1,0:T(8,128)(2,1)} %pack_rows.1), calls=%async_computation | async-start | bytes 4194304 | tf_op jit(solution)/shard_map/all_to_all | solution.py:234
  80.7 0.0 copy-done.1
  80.8 0.6 dynamic_slice.3.length_ref
  81.3 95.2 %all-to-all-done.in_ref = bf16[32,256,128]{2,1,0:T(8,128)(2,1)S(1)} async-done(((bf16[32,256,128]{2,1,0:T(8,128)(2,1)}), bf16[32,256,128]{2,1,0:T(8,128)(2,1)S(1)}, u32[]{:S(2)}, u32[]{:S(2)}) %all-to-all-start) | async-done | bytes 2097184 | tf_op jit(solution)/shard_map/all_to_all | solution.py:234
  176.5 0.0 copy-done
  176.5 15.9 %attend_pair.1 = (bf16[32,256,128]{2,1,0:T(8,128)(2,1)}, f32[4,128]{1,0:T(4,128)S(1)}) custom-call(s32[1]{0:T(128)} %dynamic_slice.3.length_ref, f32[4,128]{1,0:T(4,128)S(1)} %copy-done, bf16[32,256,128]{2,1,0:T(8,128)(2,1)S(1)} %all-to-all-done.in_ref), custom_call_target="tpu_custom_call" | custom-call | flops 6442450944 | bytes 4194304 | tf_op jit(solution)/shard_map/attend_pair/pallas_call | solution.py:152
  192.4 7.4 %all-to-all-start.1 = ((bf16[32,256,128]{2,1,0:T(8,128)(2,1)}), bf16[32,256,128]{2,1,0:T(8,128)(2,1)S(1)}, u32[]{:S(2)}, u32[]{:S(2)}) async-start(bf16[32,256,128]{2,1,0:T(8,128)(2,1)} %get-tuple-element.9), calls=%async_computation.1 | async-start | bytes 4194304 | tf_op jit(solution)/shard_map/all_to_all | solution.py:238
  199.8 2.7 collective-permute-start
  202.5 2.8 collective-permute-done
  205.3 3.1 collective-permute-start.1
  208.4 3.8 %collective-permute-done.1 = f32[4,128]{1,0:T(4,128)S(1)} collective-permute-done((f32[4,128]{1,0:T(4,128)S(1)}, f32[4,128]{1,0:T(4,128)S(1)}, u32[]{:S(2)}, u32[]{:S(2)}) %collective-permute-start.1) | collective-permute-done | bytes 2080 | tf_op jit(solution)/shard_map/ppermute | solution.py:214
  212.3 1.9 collective-permute-start.2
  214.2 1.1 collective-permute-done.2
  215.3 8.2 %collective-permute-start.3 = (f32[4,128]{1,0:T(4,128)S(1)}, f32[4,128]{1,0:T(4,128)S(1)}, u32[]{:S(2)}, u32[]{:S(2)}) collective-permute-start(f32[4,128]{1,0:T(4,128)S(1)} %add.25), channel_id=1, source_target_pairs={{0,2},{1,3},{2,0},{3,1},{4,6},{5,7},{6,4},{7,5},{8,10},{9,11},{10,... | collective-permute-start | bytes 6152 | tf_op jit(solution)/shard_map/ppermute | solution.py:214
  223.5 22.2 %collective-permute-done.3 = f32[4,128]{1,0:T(4,128)S(1)} collective-permute-done((f32[4,128]{1,0:T(4,128)S(1)}, f32[4,128]{1,0:T(4,128)S(1)}, u32[]{:S(2)}, u32[]{:S(2)}) %collective-permute-start.3) | collective-permute-done | bytes 2080 | tf_op jit(solution)/shard_map/ppermute | solution.py:214
  245.8 3.6 %collective-permute-start.4 = (f32[4,128]{1,0:T(4,128)S(1)}, f32[4,128]{1,0:T(4,128)S(1)}, u32[]{:S(2)}, u32[]{:S(2)}) collective-permute-start(f32[4,128]{1,0:T(4,128)S(1)} %add.26), channel_id=1, source_target_pairs={{0,4},{4,0},{8,12},{12,8},{16,20},{20,16},{24,28},{28,24},{32,36},... | collective-permute-start | bytes 6152 | tf_op jit(solution)/shard_map/ppermute | solution.py:214
  249.4 1.8 collective-permute-done.4
  251.2 5.2 %collective-permute-start.5 = (f32[4,128]{1,0:T(4,128)S(1)}, f32[4,128]{1,0:T(4,128)S(1)}, u32[]{:S(2)}, u32[]{:S(2)}) collective-permute-start(f32[4,128]{1,0:T(4,128)S(1)} %add.27), channel_id=1, source_target_pairs={{0,8},{4,12},{8,0},{12,4},{16,24},{20,28},{24,16},{28,20},{32,40},... | collective-permute-start | bytes 6152 | tf_op jit(solution)/shard_map/ppermute | solution.py:214
  256.4 1.8 collective-permute-done.5
  258.2 37.3 %all-to-all-done.1 = bf16[32,256,128]{2,1,0:T(8,128)(2,1)S(1)} async-done(((bf16[32,256,128]{2,1,0:T(8,128)(2,1)}), bf16[32,256,128]{2,1,0:T(8,128)(2,1)S(1)}, u32[]{:S(2)}, u32[]{:S(2)}) %all-to-all-start.1) | async-done | bytes 2097184 | tf_op jit(solution)/shard_map/all_to_all | solution.py:238
  295.5 0.6 broadcast_in_dim.2
  296.1 15.4 %all-to-all-start.2 = ((f32[8,4,128]{2,1,0:T(4,128)}), f32[8,4,128]{2,1,0:T(4,128)S(1)}, u32[]{:S(2)}, u32[]{:S(2)}) async-start(f32[8,4,128]{2,1,0:T(4,128)} %broadcast_in_dim.2), calls=%async_computation.2 | async-start | bytes 32768 | tf_op jit(solution)/shard_map/all_to_all | solution.py:246
  311.5 0.9 fusion
  312.4 0.7 slice.13
  313.1 1.1 slice.14
  314.2 7.8 %all-to-all-done.2 = f32[8,4,128]{2,1,0:T(4,128)S(1)} async-done(((f32[8,4,128]{2,1,0:T(4,128)}), f32[8,4,128]{2,1,0:T(4,128)S(1)}, u32[]{:S(2)}, u32[]{:S(2)}) %all-to-all-start.2) | async-done | bytes 16416 | tf_op jit(solution)/shard_map/all_to_all | solution.py:246
  322.0 0.6 reduce_sum.9
  (6 shorter events, 0.0 us)
Async XLA Ops:
  65.3 15.4 %copy-start.1 = (s32[2]{0:T(128)S(1)}, s32[2]{0:T(128)}, u32[]{:S(2)}) copy-start(s32[2]{0:T(128)} %param.10) | copy-start | bytes 28
  65.3 111.2 %copy-start = (f32[4,128]{1,0:T(4,128)S(1)}, f32[4,128]{1,0:T(4,128)}, u32[]{:S(2)}) copy-start(f32[4,128]{1,0:T(4,128)} %gains_ref.1) | copy-start | bytes 6148
  65.3 111.2 %all-to-all-start = ((bf16[32,256,128]{2,1,0:T(8,128)(2,1)}), bf16[32,256,128]{2,1,0:T(8,128)(2,1)S(1)}, u32[]{:S(2)}, u32[]{:S(2)}) async-start(bf16[32,256,128]{2,1,0:T(8,128)(2,1)} %pack_rows.1), calls=%async_computation | async-start | bytes 4194304 | tf_op jit(solution)/shard_map/all_to_all | solution.py:234
  192.4 103.1 %all-to-all-start.1 = ((bf16[32,256,128]{2,1,0:T(8,128)(2,1)}), bf16[32,256,128]{2,1,0:T(8,128)(2,1)S(1)}, u32[]{:S(2)}, u32[]{:S(2)}) async-start(bf16[32,256,128]{2,1,0:T(8,128)(2,1)} %get-tuple-element.9), calls=%async_computation.1 | async-start | bytes 4194304 | tf_op jit(solution)/shard_map/all_to_all | solution.py:238
  199.8 5.5 %collective-permute-start = (f32[4,128]{1,0:T(4,128)S(1)}, f32[4,128]{1,0:T(4,128)S(1)}, u32[]{:S(2)}, u32[]{:S(2)}) collective-permute-start(f32[4,128]{1,0:T(4,128)S(1)} %get-tuple-element.10), channel_id=1, source_target_pairs={{0,128},{128,0},{256,384},{384,256},{1,129},{129,1},{257,385},{385... | collective-permute-start | bytes 6152 | tf_op jit(solution)/shard_map/ppermute | solution.py:214
  205.3 7.0 %collective-permute-start.1 = (f32[4,128]{1,0:T(4,128)S(1)}, f32[4,128]{1,0:T(4,128)S(1)}, u32[]{:S(2)}, u32[]{:S(2)}) collective-permute-start(f32[4,128]{1,0:T(4,128)S(1)} %add.23), channel_id=1, source_target_pairs={{0,256},{128,384},{256,0},{384,128},{1,257},{129,385},{257,1},{385... | collective-permute-start | bytes 6152 | tf_op jit(solution)/shard_map/ppermute | solution.py:214
  212.3 3.0 collective-permute-start.2
  215.3 30.4 %collective-permute-start.3 = (f32[4,128]{1,0:T(4,128)S(1)}, f32[4,128]{1,0:T(4,128)S(1)}, u32[]{:S(2)}, u32[]{:S(2)}) collective-permute-start(f32[4,128]{1,0:T(4,128)S(1)} %add.25), channel_id=1, source_target_pairs={{0,2},{1,3},{2,0},{3,1},{4,6},{5,7},{6,4},{7,5},{8,10},{9,11},{10,... | collective-permute-start | bytes 6152 | tf_op jit(solution)/shard_map/ppermute | solution.py:214
  245.8 5.5 %collective-permute-start.4 = (f32[4,128]{1,0:T(4,128)S(1)}, f32[4,128]{1,0:T(4,128)S(1)}, u32[]{:S(2)}, u32[]{:S(2)}) collective-permute-start(f32[4,128]{1,0:T(4,128)S(1)} %add.26), channel_id=1, source_target_pairs={{0,4},{4,0},{8,12},{12,8},{16,20},{20,16},{24,28},{28,24},{32,36},... | collective-permute-start | bytes 6152 | tf_op jit(solution)/shard_map/ppermute | solution.py:214
  251.2 7.0 %collective-permute-start.5 = (f32[4,128]{1,0:T(4,128)S(1)}, f32[4,128]{1,0:T(4,128)S(1)}, u32[]{:S(2)}, u32[]{:S(2)}) collective-permute-start(f32[4,128]{1,0:T(4,128)S(1)} %add.27), channel_id=1, source_target_pairs={{0,8},{4,12},{8,0},{12,4},{16,24},{20,28},{24,16},{28,20},{32,40},... | collective-permute-start | bytes 6152 | tf_op jit(solution)/shard_map/ppermute | solution.py:214
  296.1 25.9 %all-to-all-start.2 = ((f32[8,4,128]{2,1,0:T(4,128)}), f32[8,4,128]{2,1,0:T(4,128)S(1)}, u32[]{:S(2)}, u32[]{:S(2)}) async-start(f32[8,4,128]{2,1,0:T(4,128)} %broadcast_in_dim.2), calls=%async_computation.2 | async-start | bytes 32768 | tf_op jit(solution)/shard_map/all_to_all | solution.py:246

commit v6 on v5

v6 whole, which is shorter than its diff:
```python
import functools
import math

import jax
import jax.numpy as jnp
from jax import lax
from jax.experimental import pallas as pl
from jax.experimental.pallas import tpu as pltpu
from jax.sharding import PartitionSpec as P

F32 = jnp.float32
BF16 = jnp.bfloat16
EPS = 1e-06
GROUP = 8
KEY_TILE = 512
SPARE_ROWS = 16


def inverse_rms(values):
    return lax.rsqrt(jnp.mean(values * values, axis=-1, keepdims=True) + EPS)


def norm_backward(values, gain, upstream):
    inverse = inverse_rms(values)
    scaled = gain * upstream
    inner = jnp.mean(scaled * values, axis=-1, keepdims=True)
    grad = inverse * scaled - values * (inverse * inverse * inverse * inner)
    return grad, upstream * values * inverse


def pair_kernel(img, txt, values_part, length_ref, gains_ref, in_ref, out_ref, *rest):
    if values_part:
        kn_ref, vaug_ref, eb_ref, acc_ref = rest
    else:
        terms_ref, kn_ref, vaug_ref, eb_ref, acc_ref = rest
    devices = in_ref.shape[0]
    head = in_ref.shape[2]
    blocks = devices // GROUP
    img_block, txt_block = GROUP * img, GROUP * txt
    block = img_block + txt_block
    full = blocks * block
    tile = math.gcd(KEY_TILE, full)
    scale = 1.0 / math.sqrt(head)
    to_exp2 = scale * math.log2(math.e)
    in_txt = 3 * img
    in_cot = 3 * (img + txt)
    out_dv = img + txt
    out_txt = 2 * img
    length = length_ref[0]

    def load(b, img_at, txt_at):
        rows = pl.ds(b * GROUP, GROUP)
        return jnp.concatenate(
            [
                in_ref[rows, img_at : img_at + img].reshape(img_block, head),
                in_ref[rows, txt_at : txt_at + txt].reshape(txt_block, head),
            ],
            axis=0,
        )

    def store(b, img_at, txt_at, values):
        rows = pl.ds(b * GROUP, GROUP)
        out_ref[rows, img_at : img_at + img] = values[:img_block].reshape(GROUP, img, head)
        out_ref[rows, txt_at : txt_at + txt] = values[img_block:].reshape(GROUP, txt, head)

    def gain_rows(which):
        is_img = lax.broadcasted_iota(jnp.int32, (block, head), 0) < img_block
        return jnp.where(is_img, gains_ref[which : which + 1], gains_ref[which + 2 : which + 3])

    def live_rows(b):
        row = lax.broadcasted_iota(jnp.int32, (block, head), 0)
        return jnp.logical_or(row < img_block, row - img_block + b * txt_block < length)

    def add_terms(which, terms):
        terms_ref[which : which + 1] += jnp.sum(terms[:img_block], axis=0, keepdims=True)
        terms_ref[which + 2 : which + 3] += jnp.sum(terms[img_block:], axis=0, keepdims=True)

    acc_ref[...] = jnp.zeros_like(acc_ref)
    if not values_part:
        terms_ref[...] = jnp.zeros_like(terms_ref)

    for b in range(blocks):
        at = slice(b * block, (b + 1) * block)
        live = live_rows(b)
        raw = load(b, img, in_txt + txt).astype(F32)
        normed = raw * inverse_rms(raw) * gain_rows(1)
        kn_ref[at, :] = jnp.where(live, normed, 0.0).astype(BF16)
        values = load(b, 2 * img, in_txt + 2 * txt).astype(F32)
        vaug_ref[at, :head] = jnp.where(live, values, 0.0).astype(BF16)
        vaug_ref[at, head:] = jnp.where(live, 1.0, 0.0).astype(BF16)

    by_rows = (((1,), (1,)), ((), ()))

    def forward(b, held):
        raw = load(b, 0, in_txt).astype(F32)
        gain = gain_rows(0)
        qn = (raw * inverse_rms(raw) * gain).astype(BF16)
        summed = jnp.zeros((block, 2 * head), F32)
        for start in range(0, full, tile):
            keys = slice(start, start + tile)
            scores = lax.dot_general(qn, kn_ref[keys, :], by_rows, preferred_element_type=F32)
            expo = jnp.exp2(scores * to_exp2).astype(BF16)
            held[:, keys] = expo
            summed += jnp.dot(expo, vaug_ref[keys, :], preferred_element_type=F32)
        per_total = 1.0 / summed[:, head:]
        return raw, gain, qn, summed[:, :head] * per_total, per_total

    def values_backward(b, held, raw, gain, qn, out, per_total):
        store(b, 0, img, out.astype(BF16))
        cot32 = load(b, in_cot, in_cot + img).astype(F32)
        cot_t = jnp.transpose((cot32 * per_total).astype(BF16))
        for start in range(0, full, tile):
            keys = slice(start, start + tile)
            acc_ref[:, keys] += jnp.dot(cot_t, held[:, keys], preferred_element_type=F32)

    def scores_backward(b, held, raw, gain, qn, out, per_total):
        cot = load(b, in_cot, in_cot + img)
        delta = jnp.sum(out * cot.astype(F32), axis=-1, keepdims=True)
        qn_t = jnp.transpose((qn.astype(F32) * (per_total * scale)).astype(BF16))
        dq = jnp.zeros((block, head), F32)
        for start in range(0, full, tile):
            keys = slice(start, start + tile)
            dprobs = lax.dot_general(
                cot, vaug_ref[keys, :head], by_rows, preferred_element_type=F32
            )
            dscores = held[:, keys] * (dprobs - delta).astype(BF16)
            dq += jnp.dot(dscores, kn_ref[keys, :], preferred_element_type=F32)
            acc_ref[:, keys] += jnp.dot(qn_t, dscores, preferred_element_type=F32)
        grad, terms = norm_backward(raw, gain, dq * (per_total * scale))
        store(b, 0, out_txt, grad.astype(BF16))
        add_terms(0, terms)

    backward = values_backward if values_part else scores_backward

    @pl.loop(0, blocks, step=2)
    def _queries(b):
        first = forward(b, eb_ref.at[0])
        second = forward(b + 1, eb_ref.at[1])
        backward(b, eb_ref.at[0], *first)
        backward(b + 1, eb_ref.at[1], *second)

    @pl.loop(0, blocks)
    def _key_grads(b):
        at = pl.ds(pl.multiple_of(b * block, block), block)
        upstream = jnp.where(live_rows(b), jnp.transpose(acc_ref[:, at]), 0.0)
        if values_part:
            store(b, out_dv, out_dv + img, upstream.astype(BF16))
        else:
            raw = load(b, img, in_txt + txt).astype(F32)
            grad, terms = norm_backward(raw, gain_rows(1), upstream)
            store(b, img, out_txt + txt, grad.astype(BF16))
            add_terms(1, terms)


def attend_pair(arrived, length, gains, img, txt, values_part, spare_rows):
    devices, _, head = arrived.shape
    rows = 2 * (img + txt) + spare_rows
    full = devices * (img + txt)
    block = GROUP * (img + txt)
    in_vmem = pl.BlockSpec(memory_space=pltpu.VMEM)
    out_shape = [jax.ShapeDtypeStruct((devices, rows, head), BF16)]
    if not values_part:
        out_shape.append(jax.ShapeDtypeStruct((4, head), F32))
    return pl.pallas_call(
        functools.partial(pair_kernel, img, txt, values_part),
        out_shape=out_shape,
        in_specs=[pl.BlockSpec(memory_space=pltpu.SMEM), in_vmem, in_vmem],
        out_specs=[in_vmem] * len(out_shape),
        scratch_shapes=[
            pltpu.VMEM((full, head), BF16),
            pltpu.VMEM((full, 2 * head), BF16),
            pltpu.VMEM((2, block, full), BF16),
            pltpu.VMEM((head, full), F32),
        ],
        compiler_params=pltpu.CompilerParams(vmem_limit_bytes=40 * 1024 * 1024),
        cost_estimate=pl.CostEstimate(
            flops=(6 if values_part else 10) * full * full * head,
            bytes_accessed=4 * devices * rows * head,
            transcendentals=full * full,
        ),
        name="attend_values" if values_part else "attend_scores",
    )(length, gains, arrived)


def pack_kernel(*refs):
    *parts, out_ref = refs
    at = 0
    for part in parts:
        rows = part.shape[1]
        out_ref[:, at : at + rows] = part[...]
        at += rows


def pack_rows(*parts):
    pairs, _, head = parts[0].shape
    rows = sum(part.shape[1] for part in parts)
    step = pairs // 4
    return pl.pallas_call(
        pack_kernel,
        out_shape=jax.ShapeDtypeStruct((pairs, rows, head), BF16),
        grid=(pairs // step,),
        in_specs=[pl.BlockSpec((step, part.shape[1], head), lambda i: (i, 0, 0)) for part in parts],
        out_specs=pl.BlockSpec((step, rows, head), lambda i: (i, 0, 0)),
        name="pack_rows",
    )(*parts)


def split_exact(term):
    high = lax.reduce_precision(term, 8, 7)
    middle = lax.reduce_precision(term - high, 8, 7)
    low = term - high - middle
    return jnp.concatenate([high, middle, low], axis=0).astype(BF16)


def sum_pairwise(term, axis, steps):
    count = lax.axis_size(axis)
    for step in steps:
        term = term + lax.ppermute(term, axis, [(i, i ^ step) for i in range(count)])
    return term


def powers_of_two(count):
    return [1 << bit for bit in range(count.bit_length() - 1)]


def per_device(img_qkv, txt_qkv, img_cot, txt_cot, lengths, norm_gains):
    samples, heads, _, img, head = img_qkv.shape
    txt = txt_qkv.shape[3]
    pairs = samples * heads
    devices = lax.axis_size("seq")
    assert pairs == devices
    outgoing = pack_rows(
        img_qkv.reshape(pairs, 3 * img, head),
        txt_qkv.reshape(pairs, 3 * txt, head),
        img_cot.reshape(pairs, img, head),
        txt_cot.reshape(pairs, txt, head),
    )
    arrived = lax.all_to_all(outgoing, "seq", split_axis=0, concat_axis=0, tiled=True)
    sample = lax.axis_index("seq") // heads
    length = lax.dynamic_slice_in_dim(lengths, sample, 1, 0)
    (values_out,) = attend_pair(arrived, length, norm_gains, img, txt, True, 0)
    values_out, arrived = lax.optimization_barrier((values_out, arrived))
    values_back = lax.all_to_all(values_out, "seq", split_axis=0, concat_axis=0, tiled=True)
    scores_out, terms = attend_pair(arrived, length, norm_gains, img, txt, False, SPARE_ROWS)
    for axis in ("grp", "dp"):
        terms = sum_pairwise(terms, axis, powers_of_two(lax.axis_size(axis)))
    own = img + txt
    split = split_exact(terms)
    split = jnp.pad(split, ((0, SPARE_ROWS - split.shape[0]), (0, 0)))
    scores_out = lax.dynamic_update_slice(
        scores_out, jnp.broadcast_to(split[None], (devices,) + split.shape), (0, 2 * own, 0)
    )
    scores_back = lax.all_to_all(scores_out, "seq", split_axis=0, concat_axis=0, tiled=True)
    group_terms = scores_back[:, 2 * own : 2 * own + 12].astype(F32)
    gain_grad = jnp.sum(group_terms.reshape(devices, 3, 4, head), axis=(0, 1))

    def in_samples(rows):
        return rows.reshape(samples, heads, -1, rows.shape[1], head)

    img_out = in_samples(values_back[:, :img])[:, :, 0]
    txt_out = in_samples(values_back[:, img:own])[:, :, 0]
    img_grad = jnp.concatenate(
        [scores_back[:, : 2 * img], values_back[:, own : own + img]], axis=1
    ).reshape(samples, heads, 3, img, head)
    txt_grad = jnp.concatenate(
        [scores_back[:, 2 * img : 2 * own], values_back[:, own + img :]], axis=1
    ).reshape(samples, heads, 3, txt, head)
    return (img_out, txt_out, img_grad, txt_grad, gain_grad)


def solution(mesh):
    rows = P(("grp", "dp"), None, "seq", None)
    grads = P(("grp", "dp"), None, None, "seq", None)
    return jax.shard_map(
        per_device,
        mesh=mesh,
        in_specs=(grads, grads, rows, rows, P(("grp", "dp")), P()),
        out_specs=(rows, rows, grads, grads, P()),
        check_vma=False,
    )
```

time: 323 us -> 252 us (0.78)
  Pallas kernels: 80.5 us -> 27.9 us
  starting transfers between devices: 62.9 us -> 47 us
    pallas_call x1, Pallas kernels: 64.7 us -> 3.76 us  [pack_rows(): pl.pallas_call(pack_kernel, out_shape=jax.ShapeDtypeStruct((pairs, rows,...]
    ppermute x6 -> x4, waiting for transfers between devices: 33.6 us -> 13.8 us  [sum_pairwise(): lax.ppermute(term, axis, [(i, i ^ step) for i in range(count)])]
    all_to_all x2, waiting for transfers between devices: 45.1 us -> 61.6 us  [the longest x1 54.5 us: per_device(): lax.all_to_all(scores_out, 'seq', split_axis=0, concat_axis=0, tiled=True)]
    ppermute x6 -> x4, starting transfers between devices: 24.7 us -> 15.9 us  [sum_pairwise(): lax.ppermute(term, axis, [(i, i ^ step) for i in range(count)])]
    pallas_call x1 -> x2, Pallas kernels: 15.9 us -> 24.2 us  [attend_pair(): pl.pallas_call(functools.partial(pair_kernel, img, txt, values_part), out...]
    all_to_all x2, starting transfers between devices: 22.8 us -> 15.6 us  [the longest x1 8.18 us: per_device(): lax.all_to_all(scores_out, 'seq', split_axis=0, concat_axis=0, tiled=True)]
  transfers between devices with their start and end apart: 9 -> 7, of which waited for: 9 -> 7; matrix products, arithmetic and copies ran while one was open for 1% -> 1% of each run, Pallas kernels for 0% -> 6%
where the time goes in v6:
time: 252 us
  waiting for transfers between devices  171 us (68%)
  starting transfers between devices  47 us (19%)
  Pallas kernels  27.9 us (11%)
  local copies, waits for them, and re-layouts  2.85 us (1%)
  other arithmetic  2.52 us (1%)
    all_to_all x1, waiting for transfers between devices, per_device(): lax.all_to_all(outgoing, 'seq', split_axis=0, concat_axis=0, tiled=True)  95.2 us
    all_to_all x1, waiting for transfers between devices, per_device(): lax.all_to_all(scores_out, 'seq', split_axis=0, concat_axis=0, tiled=True)  54.5 us
    pallas_call x2, Pallas kernels, attend_pair(): pl.pallas_call(functools.partial(pair_kernel, img, txt, values_part), out...  24.2 us
    ppermute x4, starting transfers between devices, sum_pairwise(): lax.ppermute(term, axis, [(i, i ^ step) for i in range(count)])  15.9 us
    all_to_all x1, starting transfers between devices, per_device(): lax.all_to_all(outgoing, 'seq', split_axis=0, concat_axis=0, tiled=True)  15.5 us
    ppermute x4, waiting for transfers between devices, sum_pairwise(): lax.ppermute(term, axis, [(i, i ^ step) for i in range(count)])  13.8 us
    all_to_all x1, starting transfers between devices, per_device(): lax.all_to_all(scores_out, 'seq', split_axis=0, concat_axis=0, tiled=True)  8.18 us
    all_to_all x1, starting transfers between devices, per_device(): lax.all_to_all(values_out, 'seq', split_axis=0, concat_axis=0, tiled=True)  7.41 us
  transfers between devices with their start and end apart: 7, of which 7 were waited for; matrix products, arithmetic and copies ran while one was open for 1% of the time, Pallas kernels for 6%

profile of v6, /device:TPU:24, one launch (start us, length us, event | category | flops | bytes accessed | tf_op | source)
XLA Modules:
  0.0 251.6 jit_solution(15892662252015602628)
XLA Ops:
  0.6 3.8 %pack_rows.1 = bf16[32,256,128]{2,1,0:T(8,128)(2,1)} custom-call(bf16[32,144,128]{2,1,0:T(8,128)(2,1)} %bitcast.9, bf16[32,48,128]{2,1,0:T(8,128)(2,1)} %bitcast.10, bf16[32,48,128]{2,1,0:T(8,128)(2,1)} %bitcast.11, bf16[32,16,128]{2,1,0:T(8,128)(2,1)} %bitcast.14), custom_call_target="tpu_custom_call" | custom-call | tf_op jit(solution)/shard_map/pack_rows/pallas_call | solution.py:198
  4.4 0.0 copy-start.1
  4.4 0.0 copy-start
  4.4 15.5 %all-to-all-start = ((bf16[32,256,128]{2,1,0:T(8,128)(2,1)}), bf16[32,256,128]{2,1,0:T(8,128)(2,1)S(1)}, u32[]{:S(2)}, u32[]{:S(2)}) async-start(bf16[32,256,128]{2,1,0:T(8,128)(2,1)} %pack_rows.1), calls=%async_computation | async-start | bytes 4194304 | tf_op jit(solution)/shard_map/all_to_all | solution.py:238
  19.9 0.0 copy-done.1
  19.9 0.6 dynamic_slice.3.length_ref
  20.5 95.2 %all-to-all-done.in_ref = bf16[32,256,128]{2,1,0:T(8,128)(2,1)S(1)} async-done(((bf16[32,256,128]{2,1,0:T(8,128)(2,1)}), bf16[32,256,128]{2,1,0:T(8,128)(2,1)S(1)}, u32[]{:S(2)}, u32[]{:S(2)}) %all-to-all-start) | async-done | bytes 2097184 | tf_op jit(solution)/shard_map/all_to_all | solution.py:238
  115.7 0.0 copy-done
  115.7 9.9 %attend_values.1 = bf16[32,128,128]{2,1,0:T(8,128)(2,1)} custom-call(s32[1]{0:T(128)} %dynamic_slice.3.length_ref, f32[4,128]{1,0:T(4,128)S(1)} %copy-done, bf16[32,256,128]{2,1,0:T(8,128)(2,1)S(1)} %all-to-all-done.in_ref), custom_call_target="tpu_custom_call" | custom-call | flops 3221225472 | bytes 2097152 | tf_op jit(solution)/shard_map/attend_values/pallas_call | solution.py:164
  125.6 7.4 %all-to-all-start.1 = ((bf16[32,128,128]{2,1,0:T(8,128)(2,1)}), bf16[32,128,128]{2,1,0:T(8,128)(2,1)S(1)}, u32[]{:S(2)}, u32[]{:S(2)}) async-start(bf16[32,128,128]{2,1,0:T(8,128)(2,1)} %attend_values.1), calls=%async_computation.1 | async-start | bytes 2097152 | tf_op jit(solution)/shard_map/all_to_all | solution.py:243
  133.0 14.3 %attend_scores.1 = (bf16[32,144,128]{2,1,0:T(8,128)(2,1)}, f32[4,128]{1,0:T(4,128)S(1)}) custom-call(s32[1]{0:T(128)} %dynamic_slice.3.length_ref, f32[4,128]{1,0:T(4,128)S(1)} %copy-done, bf16[32,256,128]{2,1,0:T(8,128)(2,1)S(1)} %all-to-all-done.in_ref), custom_call_target="tpu_custom_call" | custom-call | flops 5368709120 | bytes 2359296 | tf_op jit(solution)/shard_map/attend_scores/pallas_call | solution.py:164
  147.3 2.6 %collective-permute-start = (f32[4,128]{1,0:T(4,128)S(1)}, f32[4,128]{1,0:T(4,128)S(1)}, u32[]{:S(2)}, u32[]{:S(2)}) collective-permute-start(f32[4,128]{1,0:T(4,128)S(1)} %get-tuple-element.12), channel_id=1, source_target_pairs={{0,128},{128,0},{256,384},{384,256},{1,129},{129,1},{257,385},{385... | collective-permute-start | bytes 6152 | tf_op jit(solution)/shard_map/ppermute | solution.py:218
  149.9 2.8 %collective-permute-done = f32[4,128]{1,0:T(4,128)S(1)} collective-permute-done((f32[4,128]{1,0:T(4,128)S(1)}, f32[4,128]{1,0:T(4,128)S(1)}, u32[]{:S(2)}, u32[]{:S(2)}) %collective-permute-start) | collective-permute-done | bytes 2080 | tf_op jit(solution)/shard_map/ppermute | solution.py:218
  152.8 3.1 %collective-permute-start.1 = (f32[4,128]{1,0:T(4,128)S(1)}, f32[4,128]{1,0:T(4,128)S(1)}, u32[]{:S(2)}, u32[]{:S(2)}) collective-permute-start(f32[4,128]{1,0:T(4,128)S(1)} %add.19), channel_id=1, source_target_pairs={{0,256},{128,384},{256,0},{384,128},{1,257},{129,385},{257,1},{385... | collective-permute-start | bytes 6152 | tf_op jit(solution)/shard_map/ppermute | solution.py:218
  155.9 3.8 %collective-permute-done.1 = f32[4,128]{1,0:T(4,128)S(1)} collective-permute-done((f32[4,128]{1,0:T(4,128)S(1)}, f32[4,128]{1,0:T(4,128)S(1)}, u32[]{:S(2)}, u32[]{:S(2)}) %collective-permute-start.1) | collective-permute-done | bytes 2080 | tf_op jit(solution)/shard_map/ppermute | solution.py:218
  159.7 1.9 collective-permute-start.2
  161.7 1.1 collective-permute-done.2
  162.8 8.2 %collective-permute-start.3 = (f32[4,128]{1,0:T(4,128)S(1)}, f32[4,128]{1,0:T(4,128)S(1)}, u32[]{:S(2)}, u32[]{:S(2)}) collective-permute-start(f32[4,128]{1,0:T(4,128)S(1)} %add.21), channel_id=1, source_target_pairs={{0,2},{1,3},{2,0},{3,1},{4,6},{5,7},{6,4},{7,5},{8,10},{9,11},{10,... | collective-permute-start | bytes 6152 | tf_op jit(solution)/shard_map/ppermute | solution.py:218
  171.0 6.1 %collective-permute-done.3 = f32[4,128]{1,0:T(4,128)S(1)} collective-permute-done((f32[4,128]{1,0:T(4,128)S(1)}, f32[4,128]{1,0:T(4,128)S(1)}, u32[]{:S(2)}, u32[]{:S(2)}) %collective-permute-start.3) | collective-permute-done | bytes 2080 | tf_op jit(solution)/shard_map/ppermute | solution.py:218
  177.1 0.7 broadcast_dynamic-update-slice_fusion
  177.8 7.1 %all-to-all-done.1 = bf16[32,128,128]{2,1,0:T(8,128)(2,1)S(1)} async-done(((bf16[32,128,128]{2,1,0:T(8,128)(2,1)}), bf16[32,128,128]{2,1,0:T(8,128)(2,1)S(1)}, u32[]{:S(2)}, u32[]{:S(2)}) %all-to-all-start.1) | async-done | bytes 1048608 | tf_op jit(solution)/shard_map/all_to_all | solution.py:243
  184.8 8.2 %all-to-all-start.2 = ((bf16[32,144,128]{2,1,0:T(8,128)(2,1)}), bf16[32,144,128]{2,1,0:T(8,128)(2,1)S(1)}, u32[]{:S(2)}, u32[]{:S(2)}) async-start(bf16[32,144,128]{2,1,0:T(8,128)(2,1)} %broadcast_dynamic-update-slice_fusion), calls=%async_computation.2 | async-start | bytes 2359296 | tf_op jit(solution)/shard_map/all_to_all | solution.py:253
  193.0 0.7 fusion.6
  193.7 0.8 fusion.7
  194.5 54.5 %all-to-all-done.2 = bf16[32,144,128]{2,1,0:T(8,128)(2,1)S(1)} async-done(((bf16[32,144,128]{2,1,0:T(8,128)(2,1)}), bf16[32,144,128]{2,1,0:T(8,128)(2,1)S(1)}, u32[]{:S(2)}, u32[]{:S(2)}) %all-to-all-start.2) | async-done | bytes 1179680 | tf_op jit(solution)/shard_map/all_to_all | solution.py:253
  249.1 0.6 reduce_sum.18
  249.7 0.1 slice.30
  249.7 1.1 pad_maximum_fusion
  250.9 0.8 pad_maximum_fusion.1
  (8 shorter events, 0.1 us)
Async XLA Ops:
  4.4 15.5 %copy-start.1 = (s32[2]{0:T(128)S(1)}, s32[2]{0:T(128)}, u32[]{:S(2)}) copy-start(s32[2]{0:T(128)} %param.10) | copy-start | bytes 28
  4.4 111.3 %copy-start = (f32[4,128]{1,0:T(4,128)S(1)}, f32[4,128]{1,0:T(4,128)}, u32[]{:S(2)}) copy-start(f32[4,128]{1,0:T(4,128)} %gains_ref.3) | copy-start | bytes 6148
  4.4 111.3 %all-to-all-start = ((bf16[32,256,128]{2,1,0:T(8,128)(2,1)}), bf16[32,256,128]{2,1,0:T(8,128)(2,1)S(1)}, u32[]{:S(2)}, u32[]{:S(2)}) async-start(bf16[32,256,128]{2,1,0:T(8,128)(2,1)} %pack_rows.1), calls=%async_computation | async-start | bytes 4194304 | tf_op jit(solution)/shard_map/all_to_all | solution.py:238
  125.6 59.2 %all-to-all-start.1 = ((bf16[32,128,128]{2,1,0:T(8,128)(2,1)}), bf16[32,128,128]{2,1,0:T(8,128)(2,1)S(1)}, u32[]{:S(2)}, u32[]{:S(2)}) async-start(bf16[32,128,128]{2,1,0:T(8,128)(2,1)} %attend_values.1), calls=%async_computation.1 | async-start | bytes 2097152 | tf_op jit(solution)/shard_map/all_to_all | solution.py:243
  147.3 5.5 %collective-permute-start = (f32[4,128]{1,0:T(4,128)S(1)}, f32[4,128]{1,0:T(4,128)S(1)}, u32[]{:S(2)}, u32[]{:S(2)}) collective-permute-start(f32[4,128]{1,0:T(4,128)S(1)} %get-tuple-element.12), channel_id=1, source_target_pairs={{0,128},{128,0},{256,384},{384,256},{1,129},{129,1},{257,385},{385... | collective-permute-start | bytes 6152 | tf_op jit(solution)/shard_map/ppermute | solution.py:218
  152.8 7.0 %collective-permute-start.1 = (f32[4,128]{1,0:T(4,128)S(1)}, f32[4,128]{1,0:T(4,128)S(1)}, u32[]{:S(2)}, u32[]{:S(2)}) collective-permute-start(f32[4,128]{1,0:T(4,128)S(1)} %add.19), channel_id=1, source_target_pairs={{0,256},{128,384},{256,0},{384,128},{1,257},{129,385},{257,1},{385... | collective-permute-start | bytes 6152 | tf_op jit(solution)/shard_map/ppermute | solution.py:218
  159.7 3.0 %collective-permute-start.2 = (f32[4,128]{1,0:T(4,128)S(1)}, f32[4,128]{1,0:T(4,128)S(1)}, u32[]{:S(2)}, u32[]{:S(2)}) collective-permute-start(f32[4,128]{1,0:T(4,128)S(1)} %add.20), channel_id=1, source_target_pairs={{0,1},{1,0},{2,3},{3,2},{4,5},{5,4},{6,7},{7,6},{8,9},{9,8},{10,11... | collective-permute-start | bytes 6152 | tf_op jit(solution)/shard_map/ppermute | solution.py:218
  162.8 14.3 %collective-permute-start.3 = (f32[4,128]{1,0:T(4,128)S(1)}, f32[4,128]{1,0:T(4,128)S(1)}, u32[]{:S(2)}, u32[]{:S(2)}) collective-permute-start(f32[4,128]{1,0:T(4,128)S(1)} %add.21), channel_id=1, source_target_pairs={{0,2},{1,3},{2,0},{3,1},{4,6},{5,7},{6,4},{7,5},{8,10},{9,11},{10,... | collective-permute-start | bytes 6152 | tf_op jit(solution)/shard_map/ppermute | solution.py:218
  184.8 64.2 %all-to-all-start.2 = ((bf16[32,144,128]{2,1,0:T(8,128)(2,1)}), bf16[32,144,128]{2,1,0:T(8,128)(2,1)S(1)}, u32[]{:S(2)}, u32[]{:S(2)}) async-start(bf16[32,144,128]{2,1,0:T(8,128)(2,1)} %broadcast_dynamic-update-slice_fusion), calls=%async_computation.2 | async-start | bytes 2359296 | tf_op jit(solution)/shard_map/all_to_all | solution.py:253

commit v7 on v6

--- a/solution.py
+++ b/solution.py
@@ -13,7 +13,7 @@
 EPS = 1e-06
 GROUP = 8
 KEY_TILE = 512
-SPARE_ROWS = 16
+SPARE_ROWS = 8
 
 
 def inverse_rms(values):
@@ -130,26 +130,36 @@
         store(b, 0, out_txt, grad.astype(BF16))
         add_terms(0, terms)
 
-    backward = values_backward if values_part else scores_backward
+    if values_part:
+        held = [eb_ref.at[b] for b in range(blocks)]
+        results = [forward(0, held[0])]
+        for b in range(blocks):
+            if b + 1 < blocks:
+                results.append(forward(b + 1, held[b + 1]))
+            values_backward(b, held[b], *results[b])
+        for b in range(blocks):
+            at = slice(b * block, (b + 1) * block)
+            col = lax.broadcasted_iota(jnp.int32, (head, block), 1)
+            live = jnp.logical_or(col < img_block, col - img_block + b * txt_block < length)
+            dv_t = jnp.where(live, acc_ref[:, at], 0.0).astype(BF16)
+            store(b, out_dv, out_dv + img, jnp.transpose(dv_t))
+        return
 
     @pl.loop(0, blocks, step=2)
     def _queries(b):
         first = forward(b, eb_ref.at[0])
         second = forward(b + 1, eb_ref.at[1])
-        backward(b, eb_ref.at[0], *first)
-        backward(b + 1, eb_ref.at[1], *second)
+        scores_backward(b, eb_ref.at[0], *first)
+        scores_backward(b + 1, eb_ref.at[1], *second)
 
     @pl.loop(0, blocks)
     def _key_grads(b):
         at = pl.ds(pl.multiple_of(b * block, block), block)
         upstream = jnp.where(live_rows(b), jnp.transpose(acc_ref[:, at]), 0.0)
-        if values_part:
-            store(b, out_dv, out_dv + img, upstream.astype(BF16))
-        else:
-            raw = load(b, img, in_txt + txt).astype(F32)
-            grad, terms = norm_backward(raw, gain_rows(1), upstream)
-            store(b, img, out_txt + txt, grad.astype(BF16))
-            add_terms(1, terms)
+        raw = load(b, img, in_txt + txt).astype(F32)
+        grad, terms = norm_backward(raw, gain_rows(1), upstream)
+        store(b, img, out_txt + txt, grad.astype(BF16))
+        add_terms(1, terms)
 
 
 def attend_pair(arrived, length, gains, img, txt, values_part, spare_rows):
@@ -169,7 +179,7 @@
         scratch_shapes=[
             pltpu.VMEM((full, head), BF16),
             pltpu.VMEM((full, 2 * head), BF16),
-            pltpu.VMEM((2, block, full), BF16),
+            pltpu.VMEM((full // block if values_part else 2, block, full), BF16),
             pltpu.VMEM((head, full), F32),
         ],
         compiler_params=pltpu.CompilerParams(vmem_limit_bytes=40 * 1024 * 1024),
@@ -182,34 +192,9 @@
     )(length, gains, arrived)
 
 
-def pack_kernel(*refs):
-    *parts, out_ref = refs
-    at = 0
-    for part in parts:
-        rows = part.shape[1]
-        out_ref[:, at : at + rows] = part[...]
-        at += rows
-
-
-def pack_rows(*parts):
-    pairs, _, head = parts[0].shape
-    rows = sum(part.shape[1] for part in parts)
-    step = pairs // 4
-    return pl.pallas_call(
-        pack_kernel,
-        out_shape=jax.ShapeDtypeStruct((pairs, rows, head), BF16),
-        grid=(pairs // step,),
-        in_specs=[pl.BlockSpec((step, part.shape[1], head), lambda i: (i, 0, 0)) for part in parts],
-        out_specs=pl.BlockSpec((step, rows, head), lambda i: (i, 0, 0)),
-        name="pack_rows",
-    )(*parts)
-
-
-def split_exact(term):
+def split_rows(term):
     high = lax.reduce_precision(term, 8, 7)
-    middle = lax.reduce_precision(term - high, 8, 7)
-    low = term - high - middle
-    return jnp.concatenate([high, middle, low], axis=0).astype(BF16)
+    return jnp.concatenate([high, term - high], axis=0).astype(BF16)
 
 
 def sum_pairwise(term, axis, steps):
@@ -229,11 +214,14 @@
     pairs = samples * heads
     devices = lax.axis_size("seq")
     assert pairs == devices
-    outgoing = pack_rows(
-        img_qkv.reshape(pairs, 3 * img, head),
-        txt_qkv.reshape(pairs, 3 * txt, head),
-        img_cot.reshape(pairs, img, head),
-        txt_cot.reshape(pairs, txt, head),
+    outgoing = jnp.concatenate(
+        [
+            img_qkv.reshape(pairs, 3 * img, head),
+            txt_qkv.reshape(pairs, 3 * txt, head),
+            img_cot.reshape(pairs, img, head),
+            txt_cot.reshape(pairs, txt, head),
+        ],
+        axis=1,
     )
     arrived = lax.all_to_all(outgoing, "seq", split_axis=0, concat_axis=0, tiled=True)
     sample = lax.axis_index("seq") // heads
@@ -245,14 +233,13 @@
     for axis in ("grp", "dp"):
         terms = sum_pairwise(terms, axis, powers_of_two(lax.axis_size(axis)))
     own = img + txt
-    split = split_exact(terms)
-    split = jnp.pad(split, ((0, SPARE_ROWS - split.shape[0]), (0, 0)))
+    split = split_rows(terms)
     scores_out = lax.dynamic_update_slice(
         scores_out, jnp.broadcast_to(split[None], (devices,) + split.shape), (0, 2 * own, 0)
     )
     scores_back = lax.all_to_all(scores_out, "seq", split_axis=0, concat_axis=0, tiled=True)
-    group_terms = scores_back[:, 2 * own : 2 * own + 12].astype(F32)
-    gain_grad = jnp.sum(group_terms.reshape(devices, 3, 4, head), axis=(0, 1))
+    group_terms = jnp.sum(scores_back[:, 2 * own :].astype(F32), axis=0)
+    gain_grad = group_terms[:4] + group_terms[4:]
 
     def in_samples(rows):
         return rows.reshape(samples, heads, -1, rows.shape[1], head)

time: 252 us -> 247 us (0.980)
  Pallas kernels: 27.9 us -> 22.6 us
  other arithmetic: 2.52 us -> 5.67 us
  waiting for transfers between devices: 171 us -> 168 us
    pallas_call x1 -> x0, Pallas kernels: 3.76 us -> none  [pack_rows(): pl.pallas_call(pack_kernel, out_shape=jax.ShapeDtypeStruct((pairs, rows,...]
    concatenate x1 -> x2, other arithmetic: 0.01 us -> 3.17 us  [the longest x1 3.16 us: per_device(): jnp.concatenate([img_qkv.reshape(pairs, 3 * img, head), txt_qkv.reshape(p...]
    all_to_all x1, waiting for transfers between devices: 54.5 us -> 51.8 us  [per_device(): lax.all_to_all(scores_out, 'seq', split_axis=0, concat_axis=0, tiled=True)]
where the time goes in v7:
time: 247 us
  waiting for transfers between devices  168 us (68%)
  starting transfers between devices  47.1 us (19%)
  Pallas kernels  22.6 us (9%)
  other arithmetic  5.67 us (2%)
  local copies, waits for them, and re-layouts  2.81 us (1%)
    all_to_all x1, waiting for transfers between devices, per_device(): lax.all_to_all(outgoing, 'seq', split_axis=0, concat_axis=0, tiled=True)  95.2 us
    all_to_all x1, waiting for transfers between devices, per_device(): lax.all_to_all(scores_out, 'seq', split_axis=0, concat_axis=0, tiled=True)  51.8 us
    pallas_call x2, Pallas kernels, attend_pair(): pl.pallas_call(functools.partial(pair_kernel, img, txt, values_part), out...  22.6 us
    ppermute x4, starting transfers between devices, sum_pairwise(): lax.ppermute(term, axis, [(i, i ^ step) for i in range(count)])  15.9 us
    all_to_all x1, starting transfers between devices, per_device(): lax.all_to_all(outgoing, 'seq', split_axis=0, concat_axis=0, tiled=True)  15.5 us
    ppermute x4, waiting for transfers between devices, sum_pairwise(): lax.ppermute(term, axis, [(i, i ^ step) for i in range(count)])  13.8 us
    all_to_all x1, starting transfers between devices, per_device(): lax.all_to_all(scores_out, 'seq', split_axis=0, concat_axis=0, tiled=True)  8.15 us
    all_to_all x1, starting transfers between devices, per_device(): lax.all_to_all(values_out, 'seq', split_axis=0, concat_axis=0, tiled=True)  7.58 us
  transfers between devices with their start and end apart: 7, of which 7 were waited for; matrix products, arithmetic and copies ran while one was open for 1% of the time, Pallas kernels for 6%

profile of v7, /device:TPU:24, one launch (start us, length us, event | category | flops | bytes accessed | tf_op | source)
XLA Modules:
  0.0 246.6 jit_solution(5957751737947980908)
XLA Ops:
  0.6 3.2 %pad_maximum_fusion = bf16[32,256,128]{2,1,0:T(8,128)(2,1)} fusion(bf16[32,16,128]{2,1,0:T(8,128)(2,1)} %bitcast.14, bf16[32,48,128]{2,1,0:T(8,128)(2,1)} %bitcast.10, bf16[32,48,128]{2,1,0:T(8,128)(2,1)} %bitcast.11, bf16[32,144,128]{2,1,0:T(8,128)(2,1)} %bitcast.9), kind=kLoop, calls=%fused_computation | loop fusion | flops 8388608 | bytes 4194304 | tf_op jit(solution)/shard_map/concatenate | solution.py:217
  3.8 0.0 copy-start.1
  3.8 0.0 copy-start
  3.8 15.5 %all-to-all-start = ((bf16[32,256,128]{2,1,0:T(8,128)(2,1)}), bf16[32,256,128]{2,1,0:T(8,128)(2,1)S(1)}, u32[]{:S(2)}, u32[]{:S(2)}) async-start(bf16[32,256,128]{2,1,0:T(8,128)(2,1)} %pad_maximum_fusion), calls=%async_computation | async-start | bytes 4194304 | tf_op jit(solution)/shard_map/all_to_all | solution.py:226
  19.3 0.0 copy-done.1
  19.3 0.6 dynamic_slice.3.length_ref
  19.9 95.2 %all-to-all-done.in_ref = bf16[32,256,128]{2,1,0:T(8,128)(2,1)S(1)} async-done(((bf16[32,256,128]{2,1,0:T(8,128)(2,1)}), bf16[32,256,128]{2,1,0:T(8,128)(2,1)S(1)}, u32[]{:S(2)}, u32[]{:S(2)}) %all-to-all-start) | async-done | bytes 2097184 | tf_op jit(solution)/shard_map/all_to_all | solution.py:226
  115.1 0.0 copy-done
  115.1 8.3 %attend_values.1 = bf16[32,128,128]{2,1,0:T(8,128)(2,1)} custom-call(s32[1]{0:T(128)} %dynamic_slice.3.length_ref, f32[4,128]{1,0:T(4,128)S(1)} %copy-done, bf16[32,256,128]{2,1,0:T(8,128)(2,1)S(1)} %all-to-all-done.in_ref), custom_call_target="tpu_custom_call" | custom-call | flops 3221225472 | bytes 2097152 | tf_op jit(solution)/shard_map/attend_values/pallas_call | solution.py:174
  123.4 7.6 %all-to-all-start.1 = ((bf16[32,128,128]{2,1,0:T(8,128)(2,1)}), bf16[32,128,128]{2,1,0:T(8,128)(2,1)S(1)}, u32[]{:S(2)}, u32[]{:S(2)}) async-start(bf16[32,128,128]{2,1,0:T(8,128)(2,1)} %attend_values.1), calls=%async_computation.1 | async-start | bytes 2097152 | tf_op jit(solution)/shard_map/all_to_all | solution.py:231
  131.0 14.2 %attend_scores.1 = (bf16[32,136,128]{2,1,0:T(8,128)(2,1)}, f32[4,128]{1,0:T(4,128)S(1)}) custom-call(s32[1]{0:T(128)} %dynamic_slice.3.length_ref, f32[4,128]{1,0:T(4,128)S(1)} %copy-done, bf16[32,256,128]{2,1,0:T(8,128)(2,1)S(1)} %all-to-all-done.in_ref), custom_call_target="tpu_custom_call" | custom-call | flops 5368709120 | bytes 2228224 | tf_op jit(solution)/shard_map/attend_scores/pallas_call | solution.py:174
  145.3 2.6 %collective-permute-start = (f32[4,128]{1,0:T(4,128)S(1)}, f32[4,128]{1,0:T(4,128)S(1)}, u32[]{:S(2)}, u32[]{:S(2)}) collective-permute-start(f32[4,128]{1,0:T(4,128)S(1)} %get-tuple-element.12), channel_id=1, source_target_pairs={{0,128},{128,0},{256,384},{384,256},{1,129},{129,1},{257,385},{385... | collective-permute-start | bytes 6152 | tf_op jit(solution)/shard_map/ppermute | solution.py:203
  147.9 2.8 %collective-permute-done = f32[4,128]{1,0:T(4,128)S(1)} collective-permute-done((f32[4,128]{1,0:T(4,128)S(1)}, f32[4,128]{1,0:T(4,128)S(1)}, u32[]{:S(2)}, u32[]{:S(2)}) %collective-permute-start) | collective-permute-done | bytes 2080 | tf_op jit(solution)/shard_map/ppermute | solution.py:203
  150.7 3.1 %collective-permute-start.1 = (f32[4,128]{1,0:T(4,128)S(1)}, f32[4,128]{1,0:T(4,128)S(1)}, u32[]{:S(2)}, u32[]{:S(2)}) collective-permute-start(f32[4,128]{1,0:T(4,128)S(1)} %add.20), channel_id=1, source_target_pairs={{0,256},{128,384},{256,0},{384,128},{1,257},{129,385},{257,1},{385... | collective-permute-start | bytes 6152 | tf_op jit(solution)/shard_map/ppermute | solution.py:203
  153.9 3.8 %collective-permute-done.1 = f32[4,128]{1,0:T(4,128)S(1)} collective-permute-done((f32[4,128]{1,0:T(4,128)S(1)}, f32[4,128]{1,0:T(4,128)S(1)}, u32[]{:S(2)}, u32[]{:S(2)}) %collective-permute-start.1) | collective-permute-done | bytes 2080 | tf_op jit(solution)/shard_map/ppermute | solution.py:203
  157.7 1.9 collective-permute-start.2
  159.6 1.1 collective-permute-done.2
  160.8 8.2 %collective-permute-start.3 = (f32[4,128]{1,0:T(4,128)S(1)}, f32[4,128]{1,0:T(4,128)S(1)}, u32[]{:S(2)}, u32[]{:S(2)}) collective-permute-start(f32[4,128]{1,0:T(4,128)S(1)} %add.22), channel_id=1, source_target_pairs={{0,2},{1,3},{2,0},{3,1},{4,6},{5,7},{6,4},{7,5},{8,10},{9,11},{10,... | collective-permute-start | bytes 6152 | tf_op jit(solution)/shard_map/ppermute | solution.py:203
  169.0 6.1 %collective-permute-done.3 = f32[4,128]{1,0:T(4,128)S(1)} collective-permute-done((f32[4,128]{1,0:T(4,128)S(1)}, f32[4,128]{1,0:T(4,128)S(1)}, u32[]{:S(2)}, u32[]{:S(2)}) %collective-permute-start.3) | collective-permute-done | bytes 2080 | tf_op jit(solution)/shard_map/ppermute | solution.py:203
  175.1 0.6 broadcast_dynamic-update-slice_fusion
  175.7 6.9 %all-to-all-done.1 = bf16[32,128,128]{2,1,0:T(8,128)(2,1)S(1)} async-done(((bf16[32,128,128]{2,1,0:T(8,128)(2,1)}), bf16[32,128,128]{2,1,0:T(8,128)(2,1)S(1)}, u32[]{:S(2)}, u32[]{:S(2)}) %all-to-all-start.1) | async-done | bytes 1048608 | tf_op jit(solution)/shard_map/all_to_all | solution.py:231
  182.6 8.1 %all-to-all-start.2 = ((bf16[32,136,128]{2,1,0:T(8,128)(2,1)}), bf16[32,136,128]{2,1,0:T(8,128)(2,1)S(1)}, u32[]{:S(2)}, u32[]{:S(2)}) async-start(bf16[32,136,128]{2,1,0:T(8,128)(2,1)} %broadcast_dynamic-update-slice_fusion), calls=%async_computation.2 | async-start | bytes 2228224 | tf_op jit(solution)/shard_map/all_to_all | solution.py:240
  190.8 0.7 fusion.1
  191.5 0.8 fusion.2
  192.3 51.8 %all-to-all-done.2 = bf16[32,136,128]{2,1,0:T(8,128)(2,1)S(1)} async-done(((bf16[32,136,128]{2,1,0:T(8,128)(2,1)}), bf16[32,136,128]{2,1,0:T(8,128)(2,1)S(1)}, u32[]{:S(2)}, u32[]{:S(2)}) %all-to-all-start.2) | async-done | bytes 1114144 | tf_op jit(solution)/shard_map/all_to_all | solution.py:240
  244.1 0.6 slice_add_fusion
  244.7 0.1 slice.38
  244.8 1.1 pad_maximum_fusion.1
  245.9 0.8 pad_maximum_fusion.2
  (7 shorter events, 0.1 us)
Async XLA Ops:
  3.8 15.5 %copy-start.1 = (s32[2]{0:T(128)S(1)}, s32[2]{0:T(128)}, u32[]{:S(2)}) copy-start(s32[2]{0:T(128)} %param.10) | copy-start | bytes 28
  3.8 111.3 %copy-start = (f32[4,128]{1,0:T(4,128)S(1)}, f32[4,128]{1,0:T(4,128)}, u32[]{:S(2)}) copy-start(f32[4,128]{1,0:T(4,128)} %gains_ref.3) | copy-start | bytes 6148
  3.8 111.3 %all-to-all-start = ((bf16[32,256,128]{2,1,0:T(8,128)(2,1)}), bf16[32,256,128]{2,1,0:T(8,128)(2,1)S(1)}, u32[]{:S(2)}, u32[]{:S(2)}) async-start(bf16[32,256,128]{2,1,0:T(8,128)(2,1)} %pad_maximum_fusion), calls=%async_computation | async-start | bytes 4194304 | tf_op jit(solution)/shard_map/all_to_all | solution.py:226
  123.4 59.2 %all-to-all-start.1 = ((bf16[32,128,128]{2,1,0:T(8,128)(2,1)}), bf16[32,128,128]{2,1,0:T(8,128)(2,1)S(1)}, u32[]{:S(2)}, u32[]{:S(2)}) async-start(bf16[32,128,128]{2,1,0:T(8,128)(2,1)} %attend_values.1), calls=%async_computation.1 | async-start | bytes 2097152 | tf_op jit(solution)/shard_map/all_to_all | solution.py:231
  145.3 5.5 %collective-permute-start = (f32[4,128]{1,0:T(4,128)S(1)}, f32[4,128]{1,0:T(4,128)S(1)}, u32[]{:S(2)}, u32[]{:S(2)}) collective-permute-start(f32[4,128]{1,0:T(4,128)S(1)} %get-tuple-element.12), channel_id=1, source_target_pairs={{0,128},{128,0},{256,384},{384,256},{1,129},{129,1},{257,385},{385... | collective-permute-start | bytes 6152 | tf_op jit(solution)/shard_map/ppermute | solution.py:203
  150.7 7.0 %collective-permute-start.1 = (f32[4,128]{1,0:T(4,128)S(1)}, f32[4,128]{1,0:T(4,128)S(1)}, u32[]{:S(2)}, u32[]{:S(2)}) collective-permute-start(f32[4,128]{1,0:T(4,128)S(1)} %add.20), channel_id=1, source_target_pairs={{0,256},{128,384},{256,0},{384,128},{1,257},{129,385},{257,1},{385... | collective-permute-start | bytes 6152 | tf_op jit(solution)/shard_map/ppermute | solution.py:203
  157.7 3.0 %collective-permute-start.2 = (f32[4,128]{1,0:T(4,128)S(1)}, f32[4,128]{1,0:T(4,128)S(1)}, u32[]{:S(2)}, u32[]{:S(2)}) collective-permute-start(f32[4,128]{1,0:T(4,128)S(1)} %add.21), channel_id=1, source_target_pairs={{0,1},{1,0},{2,3},{3,2},{4,5},{5,4},{6,7},{7,6},{8,9},{9,8},{10,11... | collective-permute-start | bytes 6152 | tf_op jit(solution)/shard_map/ppermute | solution.py:203
  160.8 14.3 %collective-permute-start.3 = (f32[4,128]{1,0:T(4,128)S(1)}, f32[4,128]{1,0:T(4,128)S(1)}, u32[]{:S(2)}, u32[]{:S(2)}) collective-permute-start(f32[4,128]{1,0:T(4,128)S(1)} %add.22), channel_id=1, source_target_pairs={{0,2},{1,3},{2,0},{3,1},{4,6},{5,7},{6,4},{7,5},{8,10},{9,11},{10,... | collective-permute-start | bytes 6152 | tf_op jit(solution)/shard_map/ppermute | solution.py:203
  182.6 61.4 %all-to-all-start.2 = ((bf16[32,136,128]{2,1,0:T(8,128)(2,1)}), bf16[32,136,128]{2,1,0:T(8,128)(2,1)S(1)}, u32[]{:S(2)}, u32[]{:S(2)}) async-start(bf16[32,136,128]{2,1,0:T(8,128)(2,1)} %broadcast_dynamic-update-slice_fusion), calls=%async_computation.2 | async-start | bytes 2228224 | tf_op jit(solution)/shard_map/all_to_all | solution.py:240

commit v8 on v7

--- a/solution.py
+++ b/solution.py
@@ -12,7 +12,7 @@
 BF16 = jnp.bfloat16
 EPS = 1e-06
 GROUP = 8
-KEY_TILE = 512
+PACK_CHUNKS = 4
 SPARE_ROWS = 8
 
 
@@ -39,7 +39,7 @@
     img_block, txt_block = GROUP * img, GROUP * txt
     block = img_block + txt_block
     full = blocks * block
-    tile = math.gcd(KEY_TILE, full)
+    tile = math.gcd(1024 if values_part else 512, full)
     scale = 1.0 / math.sqrt(head)
     to_exp2 = scale * math.log2(math.e)
     in_txt = 3 * img
@@ -192,6 +192,50 @@
     )(length, gains, arrived)
 
 
+def pack_kernel(*refs):
+    *parts, out_ref, held, in_sems, out_sems = refs
+    step = held.shape[0] // PACK_CHUNKS
+    arriving = []
+    for c in range(PACK_CHUNKS):
+        pairs = slice(c * step, (c + 1) * step)
+        chunk = []
+        at = 0
+        for i, part in enumerate(parts):
+            rows = slice(at, at + part.shape[1])
+            copy = pltpu.make_async_copy(part.at[pairs], held.at[pairs, rows], in_sems.at[c, i])
+            copy.start()
+            chunk.append(copy)
+            at += part.shape[1]
+        arriving.append(chunk)
+    leaving = []
+    for c in range(PACK_CHUNKS):
+        pairs = slice(c * step, (c + 1) * step)
+        for copy in arriving[c]:
+            copy.wait()
+        copy = pltpu.make_async_copy(held.at[pairs], out_ref.at[pairs], out_sems.at[c])
+        copy.start()
+        leaving.append(copy)
+    for copy in leaving:
+        copy.wait()
+
+
+def pack_rows(*parts):
+    pairs, _, head = parts[0].shape
+    rows = sum(part.shape[1] for part in parts)
+    return pl.pallas_call(
+        pack_kernel,
+        out_shape=jax.ShapeDtypeStruct((pairs, rows, head), BF16),
+        in_specs=[pl.BlockSpec(memory_space=pl.ANY)] * len(parts),
+        out_specs=pl.BlockSpec(memory_space=pl.ANY),
+        scratch_shapes=[
+            pltpu.VMEM((pairs, rows, head), BF16),
+            pltpu.SemaphoreType.DMA((PACK_CHUNKS, len(parts))),
+            pltpu.SemaphoreType.DMA((PACK_CHUNKS,)),
+        ],
+        name="pack_rows",
+    )(*parts)
+
+
 def split_rows(term):
     high = lax.reduce_precision(term, 8, 7)
     return jnp.concatenate([high, term - high], axis=0).astype(BF16)
@@ -214,14 +258,11 @@
     pairs = samples * heads
     devices = lax.axis_size("seq")
     assert pairs == devices
-    outgoing = jnp.concatenate(
-        [
-            img_qkv.reshape(pairs, 3 * img, head),
-            txt_qkv.reshape(pairs, 3 * txt, head),
-            img_cot.reshape(pairs, img, head),
-            txt_cot.reshape(pairs, txt, head),
-        ],
-        axis=1,
+    outgoing = pack_rows(
+        img_qkv.reshape(pairs, 3 * img, head),
+        txt_qkv.reshape(pairs, 3 * txt, head),
+        img_cot.reshape(pairs, img, head),
+        txt_cot.reshape(pairs, txt, head),
     )
     arrived = lax.all_to_all(outgoing, "seq", split_axis=0, concat_axis=0, tiled=True)
     sample = lax.axis_index("seq") // heads

time: 247 us -> 247 us (level)
  other arithmetic: 5.67 us -> 2.51 us
  Pallas kernels: 22.6 us -> 25.2 us
    concatenate x1 -> x0, other arithmetic: 3.16 us -> none  [per_device(): jnp.concatenate([img_qkv.reshape(pairs, 3 * img, head), txt_qkv.reshape(p...]
    pallas_call x0 -> x1, Pallas kernels: none -> 2.56 us  [pack_rows(): pl.pallas_call(pack_kernel, out_shape=jax.ShapeDtypeStruct((pairs, rows,...]
where the time goes in v8:
time: 247 us; the launch traced here: 246 us
  waiting for transfers between devices  168 us (68%)
  starting transfers between devices  47 us (19%)
  Pallas kernels  25.2 us (10%)
  local copies, waits for them, and re-layouts  2.81 us (1%)
  other arithmetic  2.51 us (1%)
    all_to_all x1, waiting for transfers between devices, per_device(): lax.all_to_all(outgoing, 'seq', split_axis=0, concat_axis=0, tiled=True)  95.2 us
    all_to_all x1, waiting for transfers between devices, per_device(): lax.all_to_all(scores_out, 'seq', split_axis=0, concat_axis=0, tiled=True)  51.8 us
    pallas_call x2, Pallas kernels, attend_pair(): pl.pallas_call(functools.partial(pair_kernel, img, txt, values_part), out...  22.6 us
    ppermute x4, starting transfers between devices, sum_pairwise(): lax.ppermute(term, axis, [(i, i ^ step) for i in range(count)])  15.9 us
    all_to_all x1, starting transfers between devices, per_device(): lax.all_to_all(outgoing, 'seq', split_axis=0, concat_axis=0, tiled=True)  15.4 us
    ppermute x4, waiting for transfers between devices, sum_pairwise(): lax.ppermute(term, axis, [(i, i ^ step) for i in range(count)])  13.8 us
    all_to_all x1, starting transfers between devices, per_device(): lax.all_to_all(scores_out, 'seq', split_axis=0, concat_axis=0, tiled=True)  8.14 us
    all_to_all x1, starting transfers between devices, per_device(): lax.all_to_all(values_out, 'seq', split_axis=0, concat_axis=0, tiled=True)  7.58 us
  transfers between devices with their start and end apart: 7, of which 7 were waited for; matrix products, arithmetic and copies ran while one was open for 1% of the time, Pallas kernels for 6%

profile of v8, /device:TPU:24, one launch (start us, length us, event | category | flops | bytes accessed | tf_op | source)
XLA Modules:
  0.0 246.0 jit_solution(3117848420762128239)
XLA Ops:
  0.6 2.6 %pack_rows.1 = bf16[32,256,128]{2,1,0:T(8,128)(2,1)} custom-call(bf16[32,144,128]{2,1,0:T(8,128)(2,1)} %bitcast.9, bf16[32,48,128]{2,1,0:T(8,128)(2,1)} %bitcast.10, bf16[32,48,128]{2,1,0:T(8,128)(2,1)} %bitcast.11, bf16[32,16,128]{2,1,0:T(8,128)(2,1)} %bitcast.14), custom_call_target="tpu_custom_call" | custom-call | tf_op jit(solution)/shard_map/pack_rows/pallas_call | solution.py:225
  3.2 0.0 copy-start.1
  3.2 0.0 copy-start
  3.2 15.4 %all-to-all-start = ((bf16[32,256,128]{2,1,0:T(8,128)(2,1)}), bf16[32,256,128]{2,1,0:T(8,128)(2,1)S(1)}, u32[]{:S(2)}, u32[]{:S(2)}) async-start(bf16[32,256,128]{2,1,0:T(8,128)(2,1)} %pack_rows.1), calls=%async_computation | async-start | bytes 4194304 | tf_op jit(solution)/shard_map/all_to_all | solution.py:267
  18.6 0.0 copy-done.1
  18.6 0.6 dynamic_slice.3.length_ref
  19.2 95.2 %all-to-all-done.in_ref = bf16[32,256,128]{2,1,0:T(8,128)(2,1)S(1)} async-done(((bf16[32,256,128]{2,1,0:T(8,128)(2,1)}), bf16[32,256,128]{2,1,0:T(8,128)(2,1)S(1)}, u32[]{:S(2)}, u32[]{:S(2)}) %all-to-all-start) | async-done | bytes 2097184 | tf_op jit(solution)/shard_map/all_to_all | solution.py:267
  114.4 0.0 copy-done
  114.4 8.4 %attend_values.1 = bf16[32,128,128]{2,1,0:T(8,128)(2,1)} custom-call(s32[1]{0:T(128)} %dynamic_slice.3.length_ref, f32[4,128]{1,0:T(4,128)S(1)} %copy-done, bf16[32,256,128]{2,1,0:T(8,128)(2,1)S(1)} %all-to-all-done.in_ref), custom_call_target="tpu_custom_call" | custom-call | flops 3221225472 | bytes 2097152 | tf_op jit(solution)/shard_map/attend_values/pallas_call | solution.py:174
  122.8 7.6 %all-to-all-start.1 = ((bf16[32,128,128]{2,1,0:T(8,128)(2,1)}), bf16[32,128,128]{2,1,0:T(8,128)(2,1)S(1)}, u32[]{:S(2)}, u32[]{:S(2)}) async-start(bf16[32,128,128]{2,1,0:T(8,128)(2,1)} %attend_values.1), calls=%async_computation.1 | async-start | bytes 2097152 | tf_op jit(solution)/shard_map/all_to_all | solution.py:272
  130.4 14.2 %attend_scores.1 = (bf16[32,136,128]{2,1,0:T(8,128)(2,1)}, f32[4,128]{1,0:T(4,128)S(1)}) custom-call(s32[1]{0:T(128)} %dynamic_slice.3.length_ref, f32[4,128]{1,0:T(4,128)S(1)} %copy-done, bf16[32,256,128]{2,1,0:T(8,128)(2,1)S(1)} %all-to-all-done.in_ref), custom_call_target="tpu_custom_call" | custom-call | flops 5368709120 | bytes 2228224 | tf_op jit(solution)/shard_map/attend_scores/pallas_call | solution.py:174
  144.7 2.6 %collective-permute-start = (f32[4,128]{1,0:T(4,128)S(1)}, f32[4,128]{1,0:T(4,128)S(1)}, u32[]{:S(2)}, u32[]{:S(2)}) collective-permute-start(f32[4,128]{1,0:T(4,128)S(1)} %get-tuple-element.12), channel_id=1, source_target_pairs={{0,128},{128,0},{256,384},{384,256},{1,129},{129,1},{257,385},{385... | collective-permute-start | bytes 6152 | tf_op jit(solution)/shard_map/ppermute | solution.py:247
  147.3 2.8 %collective-permute-done = f32[4,128]{1,0:T(4,128)S(1)} collective-permute-done((f32[4,128]{1,0:T(4,128)S(1)}, f32[4,128]{1,0:T(4,128)S(1)}, u32[]{:S(2)}, u32[]{:S(2)}) %collective-permute-start) | collective-permute-done | bytes 2080 | tf_op jit(solution)/shard_map/ppermute | solution.py:247
  150.1 3.1 %collective-permute-start.1 = (f32[4,128]{1,0:T(4,128)S(1)}, f32[4,128]{1,0:T(4,128)S(1)}, u32[]{:S(2)}, u32[]{:S(2)}) collective-permute-start(f32[4,128]{1,0:T(4,128)S(1)} %add.20), channel_id=1, source_target_pairs={{0,256},{128,384},{256,0},{384,128},{1,257},{129,385},{257,1},{385... | collective-permute-start | bytes 6152 | tf_op jit(solution)/shard_map/ppermute | solution.py:247
  153.3 3.8 %collective-permute-done.1 = f32[4,128]{1,0:T(4,128)S(1)} collective-permute-done((f32[4,128]{1,0:T(4,128)S(1)}, f32[4,128]{1,0:T(4,128)S(1)}, u32[]{:S(2)}, u32[]{:S(2)}) %collective-permute-start.1) | collective-permute-done | bytes 2080 | tf_op jit(solution)/shard_map/ppermute | solution.py:247
  157.1 1.9 collective-permute-start.2
  159.0 1.1 collective-permute-done.2
  160.2 8.2 %collective-permute-start.3 = (f32[4,128]{1,0:T(4,128)S(1)}, f32[4,128]{1,0:T(4,128)S(1)}, u32[]{:S(2)}, u32[]{:S(2)}) collective-permute-start(f32[4,128]{1,0:T(4,128)S(1)} %add.22), channel_id=1, source_target_pairs={{0,2},{1,3},{2,0},{3,1},{4,6},{5,7},{6,4},{7,5},{8,10},{9,11},{10,... | collective-permute-start | bytes 6152 | tf_op jit(solution)/shard_map/ppermute | solution.py:247
  168.4 6.1 %collective-permute-done.3 = f32[4,128]{1,0:T(4,128)S(1)} collective-permute-done((f32[4,128]{1,0:T(4,128)S(1)}, f32[4,128]{1,0:T(4,128)S(1)}, u32[]{:S(2)}, u32[]{:S(2)}) %collective-permute-start.3) | collective-permute-done | bytes 2080 | tf_op jit(solution)/shard_map/ppermute | solution.py:247
  174.5 0.6 broadcast_dynamic-update-slice_fusion
  175.1 6.9 %all-to-all-done.1 = bf16[32,128,128]{2,1,0:T(8,128)(2,1)S(1)} async-done(((bf16[32,128,128]{2,1,0:T(8,128)(2,1)}), bf16[32,128,128]{2,1,0:T(8,128)(2,1)S(1)}, u32[]{:S(2)}, u32[]{:S(2)}) %all-to-all-start.1) | async-done | bytes 1048608 | tf_op jit(solution)/shard_map/all_to_all | solution.py:272
  182.0 8.1 %all-to-all-start.2 = ((bf16[32,136,128]{2,1,0:T(8,128)(2,1)}), bf16[32,136,128]{2,1,0:T(8,128)(2,1)S(1)}, u32[]{:S(2)}, u32[]{:S(2)}) async-start(bf16[32,136,128]{2,1,0:T(8,128)(2,1)} %broadcast_dynamic-update-slice_fusion), calls=%async_computation.2 | async-start | bytes 2228224 | tf_op jit(solution)/shard_map/all_to_all | solution.py:281
  190.2 0.7 fusion.1
  190.9 0.8 fusion.2
  191.7 51.8 %all-to-all-done.2 = bf16[32,136,128]{2,1,0:T(8,128)(2,1)S(1)} async-done(((bf16[32,136,128]{2,1,0:T(8,128)(2,1)}), bf16[32,136,128]{2,1,0:T(8,128)(2,1)S(1)}, u32[]{:S(2)}, u32[]{:S(2)}) %all-to-all-start.2) | async-done | bytes 1114144 | tf_op jit(solution)/shard_map/all_to_all | solution.py:281
  243.5 0.6 slice_add_fusion
  244.1 0.1 slice.38
  244.1 1.1 pad_maximum_fusion
  245.3 0.8 pad_maximum_fusion.1
  (7 shorter events, 0.1 us)
Async XLA Ops:
  3.2 15.4 %copy-start.1 = (s32[2]{0:T(128)S(1)}, s32[2]{0:T(128)}, u32[]{:S(2)}) copy-start(s32[2]{0:T(128)} %param.10) | copy-start | bytes 28
  3.2 111.2 %copy-start = (f32[4,128]{1,0:T(4,128)S(1)}, f32[4,128]{1,0:T(4,128)}, u32[]{:S(2)}) copy-start(f32[4,128]{1,0:T(4,128)} %gains_ref.3) | copy-start | bytes 6148
  3.2 111.2 %all-to-all-start = ((bf16[32,256,128]{2,1,0:T(8,128)(2,1)}), bf16[32,256,128]{2,1,0:T(8,128)(2,1)S(1)}, u32[]{:S(2)}, u32[]{:S(2)}) async-start(bf16[32,256,128]{2,1,0:T(8,128)(2,1)} %pack_rows.1), calls=%async_computation | async-start | bytes 4194304 | tf_op jit(solution)/shard_map/all_to_all | solution.py:267
  122.8 59.2 %all-to-all-start.1 = ((bf16[32,128,128]{2,1,0:T(8,128)(2,1)}), bf16[32,128,128]{2,1,0:T(8,128)(2,1)S(1)}, u32[]{:S(2)}, u32[]{:S(2)}) async-start(bf16[32,128,128]{2,1,0:T(8,128)(2,1)} %attend_values.1), calls=%async_computation.1 | async-start | bytes 2097152 | tf_op jit(solution)/shard_map/all_to_all | solution.py:272
  144.7 5.5 %collective-permute-start = (f32[4,128]{1,0:T(4,128)S(1)}, f32[4,128]{1,0:T(4,128)S(1)}, u32[]{:S(2)}, u32[]{:S(2)}) collective-permute-start(f32[4,128]{1,0:T(4,128)S(1)} %get-tuple-element.12), channel_id=1, source_target_pairs={{0,128},{128,0},{256,384},{384,256},{1,129},{129,1},{257,385},{385... | collective-permute-start | bytes 6152 | tf_op jit(solution)/shard_map/ppermute | solution.py:247
  150.1 7.0 %collective-permute-start.1 = (f32[4,128]{1,0:T(4,128)S(1)}, f32[4,128]{1,0:T(4,128)S(1)}, u32[]{:S(2)}, u32[]{:S(2)}) collective-permute-start(f32[4,128]{1,0:T(4,128)S(1)} %add.20), channel_id=1, source_target_pairs={{0,256},{128,384},{256,0},{384,128},{1,257},{129,385},{257,1},{385... | collective-permute-start | bytes 6152 | tf_op jit(solution)/shard_map/ppermute | solution.py:247
  157.1 3.0 %collective-permute-start.2 = (f32[4,128]{1,0:T(4,128)S(1)}, f32[4,128]{1,0:T(4,128)S(1)}, u32[]{:S(2)}, u32[]{:S(2)}) collective-permute-start(f32[4,128]{1,0:T(4,128)S(1)} %add.21), channel_id=1, source_target_pairs={{0,1},{1,0},{2,3},{3,2},{4,5},{5,4},{6,7},{7,6},{8,9},{9,8},{10,11... | collective-permute-start | bytes 6152 | tf_op jit(solution)/shard_map/ppermute | solution.py:247
  160.2 14.3 %collective-permute-start.3 = (f32[4,128]{1,0:T(4,128)S(1)}, f32[4,128]{1,0:T(4,128)S(1)}, u32[]{:S(2)}, u32[]{:S(2)}) collective-permute-start(f32[4,128]{1,0:T(4,128)S(1)} %add.22), channel_id=1, source_target_pairs={{0,2},{1,3},{2,0},{3,1},{4,6},{5,7},{6,4},{7,5},{8,10},{9,11},{10,... | collective-permute-start | bytes 6152 | tf_op jit(solution)/shard_map/ppermute | solution.py:247
  182.0 61.4 %all-to-all-start.2 = ((bf16[32,136,128]{2,1,0:T(8,128)(2,1)}), bf16[32,136,128]{2,1,0:T(8,128)(2,1)S(1)}, u32[]{:S(2)}, u32[]{:S(2)}) async-start(bf16[32,136,128]{2,1,0:T(8,128)(2,1)} %broadcast_dynamic-update-slice_fusion), calls=%async_computation.2 | async-start | bytes 2228224 | tf_op jit(solution)/shard_map/all_to_all | solution.py:281

commit v9 on v8

--- a/solution.py
+++ b/solution.py
@@ -39,7 +39,7 @@
     img_block, txt_block = GROUP * img, GROUP * txt
     block = img_block + txt_block
     full = blocks * block
-    tile = math.gcd(1024 if values_part else 512, full)
+    tile = math.gcd(256 if values_part else 512, full)
     scale = 1.0 / math.sqrt(head)
     to_exp2 = scale * math.log2(math.e)
     in_txt = 3 * img
@@ -75,8 +75,8 @@
         terms_ref[which : which + 1] += jnp.sum(terms[:img_block], axis=0, keepdims=True)
         terms_ref[which + 2 : which + 3] += jnp.sum(terms[img_block:], axis=0, keepdims=True)
 
-    acc_ref[...] = jnp.zeros_like(acc_ref)
     if not values_part:
+        acc_ref[...] = jnp.zeros_like(acc_ref)
         terms_ref[...] = jnp.zeros_like(terms_ref)
 
     for b in range(blocks):
@@ -111,7 +111,8 @@
         cot_t = jnp.transpose((cot32 * per_total).astype(BF16))
         for start in range(0, full, tile):
             keys = slice(start, start + tile)
-            acc_ref[:, keys] += jnp.dot(cot_t, held[:, keys], preferred_element_type=F32)
+            sums = jnp.dot(cot_t, held[:, keys], preferred_element_type=F32)
+            acc_ref[:, keys] = sums if b == 0 else acc_ref[:, keys] + sums
 
     def scores_backward(b, held, raw, gain, qn, out, per_total):
         cot = load(b, in_cot, in_cot + img)
@@ -234,6 +235,41 @@
         ],
         name="pack_rows",
     )(*parts)
+
+
+def join_kernel(img, txt, values_ref, scores_ref, img_ref, txt_ref, sems):
+    own = img + txt
+    copies = [
+        pltpu.make_async_copy(source, target, sems.at[i])
+        for i, (source, target) in enumerate(
+            [
+                (scores_ref.at[:, : 2 * img], img_ref.at[:, : 2 * img]),
+                (values_ref.at[:, own : own + img], img_ref.at[:, 2 * img :]),
+                (scores_ref.at[:, 2 * img : 2 * own], txt_ref.at[:, : 2 * txt]),
+                (values_ref.at[:, own + img :], txt_ref.at[:, 2 * txt :]),
+            ]
+        )
+    ]
+    for copy in copies:
+        copy.start()
+    for copy in copies:
+        copy.wait()
+
+
+def join_grads(values, scores, img, txt):
+    pairs, _, head = values.shape
+    return pl.pallas_call(
+        functools.partial(join_kernel, img, txt),
+        out_shape=[
+            jax.ShapeDtypeStruct((pairs, 3 * img, head), BF16),
+            jax.ShapeDtypeStruct((pairs, 3 * txt, head), BF16),
+        ],
+        in_specs=[pl.BlockSpec(memory_space=pltpu.VMEM)] * 2,
+        out_specs=[pl.BlockSpec(memory_space=pl.ANY)] * 2,
+        scratch_shapes=[pltpu.SemaphoreType.DMA((4,))],
+        compiler_params=pltpu.CompilerParams(vmem_limit_bytes=16 * 1024 * 1024),
+        name="join_grads",
+    )(values, scores)
 
 
 def split_rows(term):
@@ -287,12 +323,9 @@
 
     img_out = in_samples(values_back[:, :img])[:, :, 0]
     txt_out = in_samples(values_back[:, img:own])[:, :, 0]
-    img_grad = jnp.concatenate(
-        [scores_back[:, : 2 * img], values_back[:, own : own + img]], axis=1
-    ).reshape(samples, heads, 3, img, head)
-    txt_grad = jnp.concatenate(
-        [scores_back[:, 2 * img : 2 * own], values_back[:, own + img :]], axis=1
-    ).reshape(samples, heads, 3, txt, head)
+    img_grad, txt_grad = join_grads(values_back, scores_back, img, txt)
+    img_grad = img_grad.reshape(samples, heads, 3, img, head)
+    txt_grad = txt_grad.reshape(samples, heads, 3, txt, head)
     return (img_out, txt_out, img_grad, txt_grad, gain_grad)
 
 

time: 247 us -> 245 us (level)
  no operation moved by 1% of the time
where the time goes in v9:
time: 245 us
  waiting for transfers between devices  168 us (69%)
  starting transfers between devices  47 us (19%)
  Pallas kernels  24.9 us (10%)
  local copies, waits for them, and re-layouts  3.66 us (1%)
    all_to_all x1, waiting for transfers between devices, per_device(): lax.all_to_all(outgoing, 'seq', split_axis=0, concat_axis=0, tiled=True)  95.2 us
    all_to_all x1, waiting for transfers between devices, per_device(): lax.all_to_all(scores_out, 'seq', split_axis=0, concat_axis=0, tiled=True)  51.8 us
    pallas_call x2, Pallas kernels, attend_pair(): pl.pallas_call(functools.partial(pair_kernel, img, txt, values_part), out...  21.2 us
    ppermute x4, starting transfers between devices, sum_pairwise(): lax.ppermute(term, axis, [(i, i ^ step) for i in range(count)])  15.9 us
    all_to_all x1, starting transfers between devices, per_device(): lax.all_to_all(outgoing, 'seq', split_axis=0, concat_axis=0, tiled=True)  15.4 us
    ppermute x4, waiting for transfers between devices, sum_pairwise(): lax.ppermute(term, axis, [(i, i ^ step) for i in range(count)])  13.8 us
    all_to_all x1, starting transfers between devices, per_device(): lax.all_to_all(scores_out, 'seq', split_axis=0, concat_axis=0, tiled=True)  8.14 us
    all_to_all x1, starting transfers between devices, per_device(): lax.all_to_all(values_out, 'seq', split_axis=0, concat_axis=0, tiled=True)  7.59 us
  transfers between devices with their start and end apart: 7, of which 7 were waited for; matrix products, arithmetic and copies ran while one was open for 1% of the time, Pallas kernels for 6%

profile of v9, /device:TPU:24, one launch (start us, length us, event | category | flops | bytes accessed | tf_op | source)
XLA Modules:
  0.0 244.9 jit_solution(6231647568548444482)
XLA Ops:
  0.6 2.6 %pack_rows.1 = bf16[32,256,128]{2,1,0:T(8,128)(2,1)} custom-call(bf16[32,144,128]{2,1,0:T(8,128)(2,1)} %bitcast.8, bf16[32,48,128]{2,1,0:T(8,128)(2,1)} %bitcast.9, bf16[32,48,128]{2,1,0:T(8,128)(2,1)} %bitcast.10, bf16[32,16,128]{2,1,0:T(8,128)(2,1)} %bitcast.12), custom_call_target="tpu_custom_call" | custom-call | tf_op jit(solution)/shard_map/pack_rows/pallas_call | solution.py:226
  3.2 0.0 copy-start.2
  3.2 0.0 copy-start.1
  3.2 15.4 %all-to-all-start = ((bf16[32,256,128]{2,1,0:T(8,128)(2,1)}), bf16[32,256,128]{2,1,0:T(8,128)(2,1)S(1)}, u32[]{:S(2)}, u32[]{:S(2)}) async-start(bf16[32,256,128]{2,1,0:T(8,128)(2,1)} %pack_rows.1), calls=%async_computation | async-start | bytes 4194304 | tf_op jit(solution)/shard_map/all_to_all | solution.py:303
  18.6 0.0 copy-done.2
  18.6 0.6 dynamic_slice.3.length_ref
  19.2 95.2 %all-to-all-done.in_ref = bf16[32,256,128]{2,1,0:T(8,128)(2,1)S(1)} async-done(((bf16[32,256,128]{2,1,0:T(8,128)(2,1)}), bf16[32,256,128]{2,1,0:T(8,128)(2,1)S(1)}, u32[]{:S(2)}, u32[]{:S(2)}) %all-to-all-start) | async-done | bytes 2097184 | tf_op jit(solution)/shard_map/all_to_all | solution.py:303
  114.4 0.0 copy-done.1
  114.4 6.9 %attend_values.1 = bf16[32,128,128]{2,1,0:T(8,128)(2,1)S(1)} custom-call(s32[1]{0:T(128)} %dynamic_slice.3.length_ref, f32[4,128]{1,0:T(4,128)S(1)} %copy-done.1, bf16[32,256,128]{2,1,0:T(8,128)(2,1)S(1)} %all-to-all-done.in_ref), custom_call_target="tpu_custom_call" | custom-call | flops 3221225472 | bytes 2097152 | tf_op jit(solution)/shard_map/attend_values/pallas_call | solution.py:175
  121.4 0.0 copy-start
  121.4 1.0 copy-done
  122.3 7.6 %all-to-all-start.1 = ((bf16[32,128,128]{2,1,0:T(8,128)(2,1)}), bf16[32,128,128]{2,1,0:T(8,128)(2,1)S(1)}, u32[]{:S(2)}, u32[]{:S(2)}) async-start(bf16[32,128,128]{2,1,0:T(8,128)(2,1)} %copy-done), calls=%async_computation.1 | async-start | bytes 2097152 | tf_op jit(solution)/shard_map/all_to_all | solution.py:308
  129.9 14.2 %attend_scores.1 = (bf16[32,136,128]{2,1,0:T(8,128)(2,1)}, f32[4,128]{1,0:T(4,128)S(1)}) custom-call(s32[1]{0:T(128)} %dynamic_slice.3.length_ref, f32[4,128]{1,0:T(4,128)S(1)} %copy-done.1, bf16[32,256,128]{2,1,0:T(8,128)(2,1)S(1)} %all-to-all-done.in_ref), custom_call_target="tpu_custom_call" | custom-call | flops 5368709120 | bytes 2228224 | tf_op jit(solution)/shard_map/attend_scores/pallas_call | solution.py:175
  144.2 2.6 %collective-permute-start = (f32[4,128]{1,0:T(4,128)S(1)}, f32[4,128]{1,0:T(4,128)S(1)}, u32[]{:S(2)}, u32[]{:S(2)}) collective-permute-start(f32[4,128]{1,0:T(4,128)S(1)} %get-tuple-element.14), channel_id=1, source_target_pairs={{0,128},{128,0},{256,384},{384,256},{1,129},{129,1},{257,385},{385... | collective-permute-start | bytes 6152 | tf_op jit(solution)/shard_map/ppermute | solution.py:283
  146.8 2.8 %collective-permute-done = f32[4,128]{1,0:T(4,128)S(1)} collective-permute-done((f32[4,128]{1,0:T(4,128)S(1)}, f32[4,128]{1,0:T(4,128)S(1)}, u32[]{:S(2)}, u32[]{:S(2)}) %collective-permute-start) | collective-permute-done | bytes 2080 | tf_op jit(solution)/shard_map/ppermute | solution.py:283
  149.7 3.1 %collective-permute-start.1 = (f32[4,128]{1,0:T(4,128)S(1)}, f32[4,128]{1,0:T(4,128)S(1)}, u32[]{:S(2)}, u32[]{:S(2)}) collective-permute-start(f32[4,128]{1,0:T(4,128)S(1)} %add.20), channel_id=1, source_target_pairs={{0,256},{128,384},{256,0},{384,128},{1,257},{129,385},{257,1},{385... | collective-permute-start | bytes 6152 | tf_op jit(solution)/shard_map/ppermute | solution.py:283
  152.8 3.8 %collective-permute-done.1 = f32[4,128]{1,0:T(4,128)S(1)} collective-permute-done((f32[4,128]{1,0:T(4,128)S(1)}, f32[4,128]{1,0:T(4,128)S(1)}, u32[]{:S(2)}, u32[]{:S(2)}) %collective-permute-start.1) | collective-permute-done | bytes 2080 | tf_op jit(solution)/shard_map/ppermute | solution.py:283
  156.6 1.9 collective-permute-start.2
  158.5 1.1 collective-permute-done.2
  159.7 8.2 %collective-permute-start.3 = (f32[4,128]{1,0:T(4,128)S(1)}, f32[4,128]{1,0:T(4,128)S(1)}, u32[]{:S(2)}, u32[]{:S(2)}) collective-permute-start(f32[4,128]{1,0:T(4,128)S(1)} %add.22), channel_id=1, source_target_pairs={{0,2},{1,3},{2,0},{3,1},{4,6},{5,7},{6,4},{7,5},{8,10},{9,11},{10,... | collective-permute-start | bytes 6152 | tf_op jit(solution)/shard_map/ppermute | solution.py:283
  167.9 6.1 %collective-permute-done.3 = f32[4,128]{1,0:T(4,128)S(1)} collective-permute-done((f32[4,128]{1,0:T(4,128)S(1)}, f32[4,128]{1,0:T(4,128)S(1)}, u32[]{:S(2)}, u32[]{:S(2)}) %collective-permute-start.3) | collective-permute-done | bytes 2080 | tf_op jit(solution)/shard_map/ppermute | solution.py:283
  174.0 0.6 broadcast_dynamic-update-slice_fusion
  174.6 6.9 %all-to-all-done.1.values_ref = bf16[32,128,128]{2,1,0:T(8,128)(2,1)S(1)} async-done(((bf16[32,128,128]{2,1,0:T(8,128)(2,1)}), bf16[32,128,128]{2,1,0:T(8,128)(2,1)S(1)}, u32[]{:S(2)}, u32[]{:S(2)}) %all-to-all-start.1) | async-done | bytes 1048608 | tf_op jit(solution)/shard_map/all_to_all | solution.py:308
  181.6 8.1 %all-to-all-start.2 = ((bf16[32,136,128]{2,1,0:T(8,128)(2,1)}), bf16[32,136,128]{2,1,0:T(8,128)(2,1)S(1)}, u32[]{:S(2)}, u32[]{:S(2)}) async-start(bf16[32,136,128]{2,1,0:T(8,128)(2,1)} %broadcast_dynamic-update-slice_fusion), calls=%async_computation.2 | async-start | bytes 2228224 | tf_op jit(solution)/shard_map/all_to_all | solution.py:317
  189.7 0.8 slice.20
  190.5 0.7 slice.21
  191.2 51.8 %all-to-all-done.2.scores_ref = bf16[32,136,128]{2,1,0:T(8,128)(2,1)S(1)} async-done(((bf16[32,136,128]{2,1,0:T(8,128)(2,1)}), bf16[32,136,128]{2,1,0:T(8,128)(2,1)S(1)}, u32[]{:S(2)}, u32[]{:S(2)}) %all-to-all-start.2) | async-done | bytes 1114144 | tf_op jit(solution)/shard_map/all_to_all | solution.py:317
  243.0 0.6 slice_add_fusion
  243.6 1.2 join_grads.1
  (6 shorter events, 0.1 us)
Async XLA Ops:
  3.2 15.4 %copy-start.2 = (s32[2]{0:T(128)S(1)}, s32[2]{0:T(128)}, u32[]{:S(2)}) copy-start(s32[2]{0:T(128)} %param.10) | copy-start | bytes 28
  3.2 111.2 %copy-start.1 = (f32[4,128]{1,0:T(4,128)S(1)}, f32[4,128]{1,0:T(4,128)}, u32[]{:S(2)}) copy-start(f32[4,128]{1,0:T(4,128)} %gains_ref.3) | copy-start | bytes 6148
  3.2 111.2 %all-to-all-start = ((bf16[32,256,128]{2,1,0:T(8,128)(2,1)}), bf16[32,256,128]{2,1,0:T(8,128)(2,1)S(1)}, u32[]{:S(2)}, u32[]{:S(2)}) async-start(bf16[32,256,128]{2,1,0:T(8,128)(2,1)} %pack_rows.1), calls=%async_computation | async-start | bytes 4194304 | tf_op jit(solution)/shard_map/all_to_all | solution.py:303
  121.4 1.0 copy-start
  122.3 59.2 %all-to-all-start.1 = ((bf16[32,128,128]{2,1,0:T(8,128)(2,1)}), bf16[32,128,128]{2,1,0:T(8,128)(2,1)S(1)}, u32[]{:S(2)}, u32[]{:S(2)}) async-start(bf16[32,128,128]{2,1,0:T(8,128)(2,1)} %copy-done), calls=%async_computation.1 | async-start | bytes 2097152 | tf_op jit(solution)/shard_map/all_to_all | solution.py:308
  144.2 5.5 %collective-permute-start = (f32[4,128]{1,0:T(4,128)S(1)}, f32[4,128]{1,0:T(4,128)S(1)}, u32[]{:S(2)}, u32[]{:S(2)}) collective-permute-start(f32[4,128]{1,0:T(4,128)S(1)} %get-tuple-element.14), channel_id=1, source_target_pairs={{0,128},{128,0},{256,384},{384,256},{1,129},{129,1},{257,385},{385... | collective-permute-start | bytes 6152 | tf_op jit(solution)/shard_map/ppermute | solution.py:283
  149.7 7.0 %collective-permute-start.1 = (f32[4,128]{1,0:T(4,128)S(1)}, f32[4,128]{1,0:T(4,128)S(1)}, u32[]{:S(2)}, u32[]{:S(2)}) collective-permute-start(f32[4,128]{1,0:T(4,128)S(1)} %add.20), channel_id=1, source_target_pairs={{0,256},{128,384},{256,0},{384,128},{1,257},{129,385},{257,1},{385... | collective-permute-start | bytes 6152 | tf_op jit(solution)/shard_map/ppermute | solution.py:283
  156.6 3.0 %collective-permute-start.2 = (f32[4,128]{1,0:T(4,128)S(1)}, f32[4,128]{1,0:T(4,128)S(1)}, u32[]{:S(2)}, u32[]{:S(2)}) collective-permute-start(f32[4,128]{1,0:T(4,128)S(1)} %add.21), channel_id=1, source_target_pairs={{0,1},{1,0},{2,3},{3,2},{4,5},{5,4},{6,7},{7,6},{8,9},{9,8},{10,11... | collective-permute-start | bytes 6152 | tf_op jit(solution)/shard_map/ppermute | solution.py:283
  159.7 14.3 %collective-permute-start.3 = (f32[4,128]{1,0:T(4,128)S(1)}, f32[4,128]{1,0:T(4,128)S(1)}, u32[]{:S(2)}, u32[]{:S(2)}) collective-permute-start(f32[4,128]{1,0:T(4,128)S(1)} %add.22), channel_id=1, source_target_pairs={{0,2},{1,3},{2,0},{3,1},{4,6},{5,7},{6,4},{7,5},{8,10},{9,11},{10,... | collective-permute-start | bytes 6152 | tf_op jit(solution)/shard_map/ppermute | solution.py:283
  181.6 61.4 %all-to-all-start.2 = ((bf16[32,136,128]{2,1,0:T(8,128)(2,1)}), bf16[32,136,128]{2,1,0:T(8,128)(2,1)S(1)}, u32[]{:S(2)}, u32[]{:S(2)}) async-start(bf16[32,136,128]{2,1,0:T(8,128)(2,1)} %broadcast_dynamic-update-slice_fusion), calls=%async_computation.2 | async-start | bytes 2228224 | tf_op jit(solution)/shard_map/all_to_all | solution.py:317

commit v10 on v9

--- a/solution.py
+++ b/solution.py
@@ -183,7 +183,7 @@
             pltpu.VMEM((full // block if values_part else 2, block, full), BF16),
             pltpu.VMEM((head, full), F32),
         ],
-        compiler_params=pltpu.CompilerParams(vmem_limit_bytes=40 * 1024 * 1024),
+        compiler_params=pltpu.CompilerParams(vmem_limit_bytes=(57 if values_part else 40) * 1024 * 1024),
         cost_estimate=pl.CostEstimate(
             flops=(6 if values_part else 10) * full * full * head,
             bytes_accessed=4 * devices * rows * head,

time: 245 us -> 249 us (1.016)
  Pallas kernels: 24.9 us -> 27.4 us
    pallas_call x2, Pallas kernels: 21.2 us -> 23.7 us  [attend_pair(): pl.pallas_call(functools.partial(pair_kernel, img, txt, values_part), out...]
where the time goes in v10:
time: 249 us; the launch traced here: 248 us
  waiting for transfers between devices  168 us (67%)
  starting transfers between devices  47.1 us (19%)
  Pallas kernels  27.4 us (11%)
  local copies, waits for them, and re-layouts  4.04 us (2%)
    all_to_all x1, waiting for transfers between devices, per_device(): lax.all_to_all(outgoing, 'seq', split_axis=0, concat_axis=0, tiled=True)  95.2 us
    all_to_all x1, waiting for transfers between devices, per_device(): lax.all_to_all(scores_out, 'seq', split_axis=0, concat_axis=0, tiled=True)  51.8 us
    pallas_call x2, Pallas kernels, attend_pair(): pl.pallas_call(functools.partial(pair_kernel, img, txt, values_part), out...  23.7 us
    ppermute x4, starting transfers between devices, sum_pairwise(): lax.ppermute(term, axis, [(i, i ^ step) for i in range(count)])  15.9 us
    all_to_all x1, starting transfers between devices, per_device(): lax.all_to_all(outgoing, 'seq', split_axis=0, concat_axis=0, tiled=True)  15.4 us
    ppermute x4, waiting for transfers between devices, sum_pairwise(): lax.ppermute(term, axis, [(i, i ^ step) for i in range(count)])  13.8 us
    all_to_all x1, starting transfers between devices, per_device(): lax.all_to_all(scores_out, 'seq', split_axis=0, concat_axis=0, tiled=True)  8.14 us
    all_to_all x1, starting transfers between devices, per_device(): lax.all_to_all(values_out, 'seq', split_axis=0, concat_axis=0, tiled=True)  7.72 us
  transfers between devices with their start and end apart: 7, of which 7 were waited for; matrix products, arithmetic and copies ran while one was open for 1% of the time, Pallas kernels for 6%

profile of v10, /device:TPU:24, one launch (start us, length us, event | category | flops | bytes accessed | tf_op | source)
XLA Modules:
  0.0 248.0 jit_solution(4848767383048216285)
XLA Ops:
  0.6 2.6 %pack_rows.1 = bf16[32,256,128]{2,1,0:T(8,128)(2,1)} custom-call(bf16[32,144,128]{2,1,0:T(8,128)(2,1)} %bitcast.8, bf16[32,48,128]{2,1,0:T(8,128)(2,1)} %bitcast.9, bf16[32,48,128]{2,1,0:T(8,128)(2,1)} %bitcast.10, bf16[32,16,128]{2,1,0:T(8,128)(2,1)} %bitcast.12), custom_call_target="tpu_custom_call" | custom-call | tf_op jit(solution)/shard_map/pack_rows/pallas_call | solution.py:226
  3.2 0.0 copy-start.3
  3.2 15.4 %all-to-all-start = ((bf16[32,256,128]{2,1,0:T(8,128)(2,1)}), bf16[32,256,128]{2,1,0:T(8,128)(2,1)S(1)}, u32[]{:S(2)}, u32[]{:S(2)}) async-start(bf16[32,256,128]{2,1,0:T(8,128)(2,1)} %pack_rows.1), calls=%async_computation | async-start | bytes 4194304 | tf_op jit(solution)/shard_map/all_to_all | solution.py:303
  18.6 0.0 copy-done.3
  18.6 0.6 dynamic_slice.3.length_ref
  19.2 95.2 %all-to-all-done.in_ref = bf16[32,256,128]{2,1,0:T(8,128)(2,1)S(1)} async-done(((bf16[32,256,128]{2,1,0:T(8,128)(2,1)}), bf16[32,256,128]{2,1,0:T(8,128)(2,1)S(1)}, u32[]{:S(2)}, u32[]{:S(2)}) %all-to-all-start) | async-done | bytes 2097184 | tf_op jit(solution)/shard_map/all_to_all | solution.py:303
  114.4 0.0 copy-start
  114.4 1.3 copy-done
  115.8 0.0 copy-start.2
  115.8 9.5 %attend_values.1 = bf16[32,128,128]{2,1,0:T(8,128)(2,1)} custom-call(s32[1]{0:T(128)} %dynamic_slice.3.length_ref, f32[4,128]{1,0:T(4,128)} %gains_ref.3, bf16[32,256,128]{2,1,0:T(8,128)(2,1)} %copy-done), custom_call_target="tpu_custom_call" | custom-call | flops 3221225472 | bytes 2097152 | tf_op jit(solution)/shard_map/attend_values/pallas_call | solution.py:175
  125.3 0.0 copy-start.1
  125.3 7.7 %all-to-all-start.1 = ((bf16[32,128,128]{2,1,0:T(8,128)(2,1)}), bf16[32,128,128]{2,1,0:T(8,128)(2,1)S(1)}, u32[]{:S(2)}, u32[]{:S(2)}) async-start(bf16[32,128,128]{2,1,0:T(8,128)(2,1)} %attend_values.1), calls=%async_computation.1 | async-start | bytes 2097152 | tf_op jit(solution)/shard_map/all_to_all | solution.py:308
  133.0 0.0 copy-done.2
  133.0 0.0 copy-done.1
  133.0 14.2 %attend_scores.1 = (bf16[32,136,128]{2,1,0:T(8,128)(2,1)}, f32[4,128]{1,0:T(4,128)S(1)}) custom-call(s32[1]{0:T(128)} %dynamic_slice.3.length_ref, f32[4,128]{1,0:T(4,128)S(1)} %copy-done.2, bf16[32,256,128]{2,1,0:T(8,128)(2,1)S(1)} %copy-done.1), custom_call_target="tpu_custom_call" | custom-call | flops 5368709120 | bytes 2228224 | tf_op jit(solution)/shard_map/attend_scores/pallas_call | solution.py:175
  147.2 2.6 %collective-permute-start = (f32[4,128]{1,0:T(4,128)S(1)}, f32[4,128]{1,0:T(4,128)S(1)}, u32[]{:S(2)}, u32[]{:S(2)}) collective-permute-start(f32[4,128]{1,0:T(4,128)S(1)} %get-tuple-element.14), channel_id=1, source_target_pairs={{0,128},{128,0},{256,384},{384,256},{1,129},{129,1},{257,385},{385... | collective-permute-start | bytes 6152 | tf_op jit(solution)/shard_map/ppermute | solution.py:283
  149.9 2.8 %collective-permute-done = f32[4,128]{1,0:T(4,128)S(1)} collective-permute-done((f32[4,128]{1,0:T(4,128)S(1)}, f32[4,128]{1,0:T(4,128)S(1)}, u32[]{:S(2)}, u32[]{:S(2)}) %collective-permute-start) | collective-permute-done | bytes 2080 | tf_op jit(solution)/shard_map/ppermute | solution.py:283
  152.7 3.1 %collective-permute-start.1 = (f32[4,128]{1,0:T(4,128)S(1)}, f32[4,128]{1,0:T(4,128)S(1)}, u32[]{:S(2)}, u32[]{:S(2)}) collective-permute-start(f32[4,128]{1,0:T(4,128)S(1)} %add.20), channel_id=1, source_target_pairs={{0,256},{128,384},{256,0},{384,128},{1,257},{129,385},{257,1},{385... | collective-permute-start | bytes 6152 | tf_op jit(solution)/shard_map/ppermute | solution.py:283
  155.8 3.8 %collective-permute-done.1 = f32[4,128]{1,0:T(4,128)S(1)} collective-permute-done((f32[4,128]{1,0:T(4,128)S(1)}, f32[4,128]{1,0:T(4,128)S(1)}, u32[]{:S(2)}, u32[]{:S(2)}) %collective-permute-start.1) | collective-permute-done | bytes 2080 | tf_op jit(solution)/shard_map/ppermute | solution.py:283
  159.7 1.9 collective-permute-start.2
  161.6 1.1 collective-permute-done.2
  162.7 8.2 %collective-permute-start.3 = (f32[4,128]{1,0:T(4,128)S(1)}, f32[4,128]{1,0:T(4,128)S(1)}, u32[]{:S(2)}, u32[]{:S(2)}) collective-permute-start(f32[4,128]{1,0:T(4,128)S(1)} %add.22), channel_id=1, source_target_pairs={{0,2},{1,3},{2,0},{3,1},{4,6},{5,7},{6,4},{7,5},{8,10},{9,11},{10,... | collective-permute-start | bytes 6152 | tf_op jit(solution)/shard_map/ppermute | solution.py:283
  170.9 6.1 %collective-permute-done.3 = f32[4,128]{1,0:T(4,128)S(1)} collective-permute-done((f32[4,128]{1,0:T(4,128)S(1)}, f32[4,128]{1,0:T(4,128)S(1)}, u32[]{:S(2)}, u32[]{:S(2)}) %collective-permute-start.3) | collective-permute-done | bytes 2080 | tf_op jit(solution)/shard_map/ppermute | solution.py:283
  177.0 0.6 broadcast_dynamic-update-slice_fusion
  177.6 7.0 %all-to-all-done.1.values_ref = bf16[32,128,128]{2,1,0:T(8,128)(2,1)S(1)} async-done(((bf16[32,128,128]{2,1,0:T(8,128)(2,1)}), bf16[32,128,128]{2,1,0:T(8,128)(2,1)S(1)}, u32[]{:S(2)}, u32[]{:S(2)}) %all-to-all-start.1) | async-done | bytes 1048608 | tf_op jit(solution)/shard_map/all_to_all | solution.py:308
  184.6 8.1 %all-to-all-start.2 = ((bf16[32,136,128]{2,1,0:T(8,128)(2,1)}), bf16[32,136,128]{2,1,0:T(8,128)(2,1)S(1)}, u32[]{:S(2)}, u32[]{:S(2)}) async-start(bf16[32,136,128]{2,1,0:T(8,128)(2,1)} %broadcast_dynamic-update-slice_fusion), calls=%async_computation.2 | async-start | bytes 2228224 | tf_op jit(solution)/shard_map/all_to_all | solution.py:317
  192.8 0.8 slice.20
  193.6 0.7 slice.21
  194.3 51.8 %all-to-all-done.2.scores_ref = bf16[32,136,128]{2,1,0:T(8,128)(2,1)S(1)} async-done(((bf16[32,136,128]{2,1,0:T(8,128)(2,1)}), bf16[32,136,128]{2,1,0:T(8,128)(2,1)S(1)}, u32[]{:S(2)}, u32[]{:S(2)}) %all-to-all-start.2) | async-done | bytes 1114144 | tf_op jit(solution)/shard_map/all_to_all | solution.py:317
  246.1 0.6 slice_add_fusion
  246.7 1.2 join_grads.1
  (6 shorter events, 0.1 us)
Async XLA Ops:
  3.2 15.4 %copy-start.3 = (s32[2]{0:T(128)S(1)}, s32[2]{0:T(128)}, u32[]{:S(2)}) copy-start(s32[2]{0:T(128)} %param.10) | copy-start | bytes 28
  3.2 111.2 %all-to-all-start = ((bf16[32,256,128]{2,1,0:T(8,128)(2,1)}), bf16[32,256,128]{2,1,0:T(8,128)(2,1)S(1)}, u32[]{:S(2)}, u32[]{:S(2)}) async-start(bf16[32,256,128]{2,1,0:T(8,128)(2,1)} %pack_rows.1), calls=%async_computation | async-start | bytes 4194304 | tf_op jit(solution)/shard_map/all_to_all | solution.py:303
  114.4 1.3 copy-start
  115.8 17.3 %copy-start.2 = (f32[4,128]{1,0:T(4,128)S(1)}, f32[4,128]{1,0:T(4,128)}, u32[]{:S(2)}) copy-start(f32[4,128]{1,0:T(4,128)} %gains_ref.3) | copy-start | bytes 6148
  125.3 7.7 %copy-start.1 = (bf16[32,256,128]{2,1,0:T(8,128)(2,1)S(1)}, bf16[32,256,128]{2,1,0:T(8,128)(2,1)}, u32[]{:S(2)}) copy-start(bf16[32,256,128]{2,1,0:T(8,128)(2,1)} %copy-done) | copy-start | bytes 6291460
  125.3 59.3 %all-to-all-start.1 = ((bf16[32,128,128]{2,1,0:T(8,128)(2,1)}), bf16[32,128,128]{2,1,0:T(8,128)(2,1)S(1)}, u32[]{:S(2)}, u32[]{:S(2)}) async-start(bf16[32,128,128]{2,1,0:T(8,128)(2,1)} %attend_values.1), calls=%async_computation.1 | async-start | bytes 2097152 | tf_op jit(solution)/shard_map/all_to_all | solution.py:308
  147.2 5.5 %collective-permute-start = (f32[4,128]{1,0:T(4,128)S(1)}, f32[4,128]{1,0:T(4,128)S(1)}, u32[]{:S(2)}, u32[]{:S(2)}) collective-permute-start(f32[4,128]{1,0:T(4,128)S(1)} %get-tuple-element.14), channel_id=1, source_target_pairs={{0,128},{128,0},{256,384},{384,256},{1,129},{129,1},{257,385},{385... | collective-permute-start | bytes 6152 | tf_op jit(solution)/shard_map/ppermute | solution.py:283
  152.7 7.0 %collective-permute-start.1 = (f32[4,128]{1,0:T(4,128)S(1)}, f32[4,128]{1,0:T(4,128)S(1)}, u32[]{:S(2)}, u32[]{:S(2)}) collective-permute-start(f32[4,128]{1,0:T(4,128)S(1)} %add.20), channel_id=1, source_target_pairs={{0,256},{128,384},{256,0},{384,128},{1,257},{129,385},{257,1},{385... | collective-permute-start | bytes 6152 | tf_op jit(solution)/shard_map/ppermute | solution.py:283
  159.7 3.0 %collective-permute-start.2 = (f32[4,128]{1,0:T(4,128)S(1)}, f32[4,128]{1,0:T(4,128)S(1)}, u32[]{:S(2)}, u32[]{:S(2)}) collective-permute-start(f32[4,128]{1,0:T(4,128)S(1)} %add.21), channel_id=1, source_target_pairs={{0,1},{1,0},{2,3},{3,2},{4,5},{5,4},{6,7},{7,6},{8,9},{9,8},{10,11... | collective-permute-start | bytes 6152 | tf_op jit(solution)/shard_map/ppermute | solution.py:283
  162.7 14.3 %collective-permute-start.3 = (f32[4,128]{1,0:T(4,128)S(1)}, f32[4,128]{1,0:T(4,128)S(1)}, u32[]{:S(2)}, u32[]{:S(2)}) collective-permute-start(f32[4,128]{1,0:T(4,128)S(1)} %add.22), channel_id=1, source_target_pairs={{0,2},{1,3},{2,0},{3,1},{4,6},{5,7},{6,4},{7,5},{8,10},{9,11},{10,... | collective-permute-start | bytes 6152 | tf_op jit(solution)/shard_map/ppermute | solution.py:283
  184.6 61.4 %all-to-all-start.2 = ((bf16[32,136,128]{2,1,0:T(8,128)(2,1)}), bf16[32,136,128]{2,1,0:T(8,128)(2,1)S(1)}, u32[]{:S(2)}, u32[]{:S(2)}) async-start(bf16[32,136,128]{2,1,0:T(8,128)(2,1)} %broadcast_dynamic-update-slice_fusion), calls=%async_computation.2 | async-start | bytes 2228224 | tf_op jit(solution)/shard_map/all_to_all | solution.py:317
